TPU v7x, 128 devices: a whole 4x4x4 slice. The times are simulated.
128 devices in a mesh: batch: 4 (over y_lo, core), dap: 32 (over z, x, y_hi).
Axes of the slice: x: 4, y: 4 (y_hi: 2, y_lo: 2; y = y_hi * 2 + y_lo), z: 4, core: 2. Of those that a mesh axis runs over, the one named last changes fastest.
Arguments:
- alignment: bfloat16 [1024, 512, 256], P(('batch', 'dap')), parts along dimension 0, may hold values from -6 to 6
- pair_state: bfloat16 [2048, 512, 128], P(('batch', 'dap')), parts along dimension 0, may hold values from -6 to 6
- row_norm_gain: float32 [256], replicated, may hold values from 0.5 to 1.5
- row_norm_bias: float32 [256], replicated, may hold values from -3 to 3
- pair_norm_gain: float32 [128], replicated, may hold values from 0.25 to 1.75
- pair_weight: bfloat16 [128, 8], replicated, may hold values from -0.5 to 0.5
- row_query: bfloat16 [256, 256], replicated, may hold values from -23 to 23, as said below
- row_key: bfloat16 [256, 256], replicated, may hold values from -0.375 to 0.375, as said below
- row_value: bfloat16 [256, 256], replicated, may hold values from -0.375 to 0.375
- row_gate: bfloat16 [256, 256], replicated, may hold values from -0.375 to 0.375
- row_gate_bias: float32 [256], replicated, may hold values from -4 to 4
- row_output: bfloat16 [256, 256], replicated, may hold values from -0.375 to 0.375
- row_output_bias: float32 [256], replicated, may hold values from -3 to 3
- column_norm_gain: float32 [256], replicated, may hold values from 0.5 to 1.5
- column_norm_bias: float32 [256], replicated, may hold values from -3 to 3
- column_query: bfloat16 [256, 256], replicated, may hold values from -23 to 23, as said below
- column_key: bfloat16 [256, 256], replicated, may hold values from -0.375 to 0.375, as said below
- column_value: bfloat16 [256, 256], replicated, may hold values from -0.375 to 0.375
- column_gate: bfloat16 [256, 256], replicated, may hold values from -0.375 to 0.375
- column_gate_bias: float32 [256], replicated, may hold values from -4 to 4
- column_output: bfloat16 [256, 256], replicated, may hold values from -0.375 to 0.375
- column_output_bias: float32 [256], replicated, may hold values from -3 to 3
Outputs:
- updated: bfloat16 [1024, 512, 256], P(('batch', 'dap')), parts along dimension 0
There are 4 independent parts, one for each index of `batch`. A program takes and returns all parts, laid end to end along the dimension named above; an argument that names none is the same for every part. Nothing has to cross between parts.
Inputs may be any that keep to these rules, and one draw needn't show every extreme that they name: `row_query`: a projection's entries. `row_key`: a projection's entries. `column_query`: a projection's entries. `column_key`: a projection's entries.
All inputs are finite; a program needn't handle non-finite values.
Results may differ from a plain program's by a relative error of at most 0.005.
The roundings to bfloat16 on the way count: a program that leaves them out, or rounds other values in their place, can miss the bound.
Values may be sent and summed in bfloat16 or wider, within the bound.
No kernel may reach another device: no remote copies, remote signals or barrier semaphores. Data moves between devices by JAX's collectives and lax.ppermute only.
A program may use at most 192 MiB of HBM per device.

v0:
```python
import jax
import jax.numpy as jnp
from jax import lax
from jax.sharding import PartitionSpec as P

H = 8
HEAD = 32


epsilon = 1e-05


def layer_norm(values, norm_gain, norm_bias):
    values = values.astype(jnp.float32)
    center = jnp.mean(values, axis=-1, keepdims=True)
    spread = jnp.mean(jnp.square(values - center), axis=-1, keepdims=True)
    return ((values - center) * lax.rsqrt(spread + epsilon) * norm_gain + norm_bias).astype(
        jnp.bfloat16
    )


def project_all(normed, query_weight, key_weight, value_weight, gate_weight, gate_bias):
    feature_width = query_weight.shape[1]
    stacked = jnp.concatenate([query_weight, key_weight, value_weight, gate_weight], axis=1)
    flattened = normed.reshape(-1, normed.shape[-1])
    projected = jnp.dot(flattened, stacked, preferred_element_type=jnp.float32)
    lead_shape = normed.shape[:-1] + (feature_width,)
    queries = (
        (projected[:, :feature_width] * HEAD ** (-0.5)).astype(jnp.bfloat16).reshape(lead_shape)
    )
    key_proj = (
        projected[:, feature_width : 2 * feature_width].astype(jnp.bfloat16).reshape(lead_shape)
    )
    value_proj = (
        projected[:, 2 * feature_width : 3 * feature_width].astype(jnp.bfloat16).reshape(lead_shape)
    )
    gate_proj = jax.nn.sigmoid(projected[:, 3 * feature_width :] + gate_bias).reshape(lead_shape)
    return (queries, key_proj, value_proj, gate_proj)


def output_layer(gated, residual, out_weight, out_bias):
    flattened = gated.reshape(-1, gated.shape[-1])
    update = jnp.dot(flattened, out_weight, preferred_element_type=jnp.float32) + out_bias
    return (residual.astype(jnp.float32) + update.reshape(residual.shape)).astype(jnp.bfloat16)


def group_width(seq_count, row_count):
    target = max(1, 512 // max(row_count, 1))
    best = 1
    for width in range(1, seq_count + 1):
        if seq_count % width == 0 and width <= target:
            best = width
    return best


def per_device(
    alignment,
    pair_state,
    row_norm_gain,
    row_norm_bias,
    pair_norm_gain,
    pair_weight,
    row_query,
    row_key,
    row_value,
    row_gate,
    row_gate_bias,
    row_output,
    row_output_bias,
    column_norm_gain,
    column_norm_bias,
    column_query,
    column_key,
    column_value,
    column_gate,
    column_gate_bias,
    column_output,
    column_output_bias,
):
    seq_count = alignment.shape[0]
    residue_count = alignment.shape[1]
    feature_width = alignment.shape[2]
    pair_normed = layer_norm(pair_state, pair_norm_gain, jnp.zeros_like(pair_norm_gain))
    bias_local = jnp.einsum(
        "irc,ch->hir", pair_normed, pair_weight, preferred_element_type=jnp.float32
    ).astype(jnp.bfloat16)
    normed = layer_norm(alignment, row_norm_gain, row_norm_bias)
    queries, key_proj, value_proj, gate_proj = project_all(
        normed, row_query, row_key, row_value, row_gate, row_gate_bias
    )
    whole_bias = lax.all_gather(bias_local, "dap", axis=1, tiled=True)
    row_count = whole_bias.shape[1]
    width = group_width(seq_count, row_count)
    groups = seq_count // width
    bias_wide = whole_bias.astype(jnp.float32)

    def one_group(parts):
        grp_query, grp_key, grp_value, grp_gate, grp_residual = parts
        query_heads = grp_query.reshape(width, row_count, H, HEAD)
        key_heads = grp_key.reshape(width, residue_count, H, HEAD)
        value_heads = grp_value.reshape(width, residue_count, H, HEAD)
        scores = (
            jnp.einsum(
                "sqhd,skhd->shqk", query_heads, key_heads, preferred_element_type=jnp.float32
            )
            + bias_wide[None]
        )
        weights = jax.nn.softmax(scores, axis=-1).astype(jnp.bfloat16)
        averaged = jnp.einsum(
            "shqk,skhd->sqhd", weights, value_heads, preferred_element_type=jnp.float32
        )
        gated = (grp_gate * averaged.reshape(width, row_count, feature_width)).astype(jnp.bfloat16)
        return output_layer(gated, grp_residual, row_output, row_output_bias)

    grouped_parts = (
        queries.reshape(groups, width, row_count, feature_width),
        key_proj.reshape(groups, width, residue_count, feature_width),
        value_proj.reshape(groups, width, residue_count, feature_width),
        gate_proj.reshape(groups, width, row_count, feature_width),
        alignment.reshape(groups, width, row_count, feature_width),
    )
    result = lax.map(one_group, grouped_parts)
    after_rows = result.reshape(seq_count, row_count, feature_width)
    received = lax.all_to_all(after_rows, "dap", split_axis=1, concat_axis=0, tiled=True)
    seq_total = received.shape[0]
    item_count = received.shape[1]
    column_normed = layer_norm(received, column_norm_gain, column_norm_bias)
    col_query, col_key, col_value, col_gate = project_all(
        column_normed, column_query, column_key, column_value, column_gate, column_gate_bias
    )
    query_heads = col_query.reshape(seq_total, item_count, H, HEAD)
    key_heads = col_key.reshape(seq_total, item_count, H, HEAD)
    value_heads = col_value.reshape(seq_total, item_count, H, HEAD)
    scores = jnp.einsum(
        "srhd,trhd->rhst", query_heads, key_heads, preferred_element_type=jnp.float32
    )
    weights = jax.nn.softmax(scores, axis=-1).astype(jnp.bfloat16)
    averaged = jnp.einsum(
        "rhst,trhd->srhd", weights, value_heads, preferred_element_type=jnp.float32
    )
    gated = (col_gate * averaged.reshape(seq_total, item_count, feature_width)).astype(jnp.bfloat16)
    return lax.all_to_all(
        output_layer(gated, received, column_output, column_output_bias),
        "dap",
        split_axis=0,
        concat_axis=1,
        tiled=True,
    )


def solution(mesh):
    return jax.shard_map(
        per_device,
        mesh=mesh,
        in_specs=(
            P(("batch", "dap"), None, None),
            P(("batch", "dap"), None, None),
            P(),
            P(),
            P(),
            P(),
            P(),
            P(),
            P(),
            P(),
            P(),
            P(),
            P(),
            P(),
            P(),
            P(),
            P(),
            P(),
            P(),
            P(),
            P(),
            P(),
        ),
        out_specs=P(("batch", "dap"), None, None),
        check_vma=False,
    )
```

profile of v0, /device:TPU:0, one launch (start us, length us, event | category | flops | bytes accessed | tf_op | source)
XLA Modules:
  0.0 445.9 jit_solution(5600451749645304226)
XLA Ops:
  6.6 2.4 convert_reduce_fusion
  9.0 3.6 fusion.25
  12.7 3.5 fusion.59
  18.3 2.7 fusion.31
  21.0 3.9 fusion.90
  25.0 2.3 fusion.88
  27.2 3.8 fusion.38
  31.0 68.1 %all-gather.2.cloned.1.call-done = bf16[8,512,512]{2,0,1:T(8,128)(2,1)} async-done(((bf16[8,16,512]{2,0,1:T(8,128)(2,1)}), bf16[8,512,512]{2,0,1:T(8,128)(2,1)}) %all-gather.2.cloned.1.call-update) | async-done | bytes 4194320 | tf_op jit(solution)/shard_map/all_gather | solution.py:91
  99.2 8.7 %copy.100 = f32[8,512,512]{1,2,0:T(8,128)} copy(bf16[8,512,512]{2,0,1:T(8,128)(2,1)} %all-gather.2.cloned.1.call-done) | data formatting | bytes 12582912 | tf_op jit(solution)/shard_map/while | solution.py:122
  107.9 139.9 %while.10 = (s32[]{:T(128)}, bf16[8,1,512,256]{3,2,1,0:T(8,128)(2,1)}, bf16[8,1,512,256]{3,2,1,0:T(8,128)(2,1)}, f32[8,1,512,256]{3,2,0,1:T(8,128)}, bf16[8,1,51...) while((s32[]{:T(128)}, ...), condition=%wide.region_7.8_spmd, body=%wide.region_4.7_spmd.sunk | while | flops 485233664 | bytes 26117752 | solution.py:122
  109.2 4.9 %fusion.127 = f32[8,512]{1,0:T(8,128)S(1)} fusion(f32[8,512,512]{1,2,0:T(8,128)} %get-tuple-element.248, bf16[512,8,32]{0,2,1:T(8,128)(2,1)S(1)} %bitcast.111, bf16[512,8,32]{0,2,1:T(8,128)(2,1)S(1)} %bitcast.113), kind=kOutput, calls=%fused_computation.100.clone.1 | convolution fusion | flops 140509696 | bytes 8929280 | tf_op jit(solution)/shard_map/while/body/eval_jaxpr/sub | solution.py:108
  115.2 6.8 %fusion.128 = f32[8,32,512]{2,1,0:T(8,128)S(1)} fusion(bf16[512,8,32]{0,2,1:T(8,128)(2,1)S(1)} %bitcast.115, f32[8,512]{1,0:T(8,128)S(1)} %fusion.127, f32[8,512,512]{1,2,0:T(8,128)} %get-tuple-element.248, bf16[512,8,32]{0,2,1:T(8,128)(2,1)S(1)} %bitcast.112, bf16[512,8,32]{0,2,1:T(8,128)(2,1)S(1)} %bitcast.114), kind=kOutput, calls=%fused_computation.3.clone.1 | convolution fusion | flops 276828672 | bytes 9715712 | tf_op jit(solution)/shard_map/while/body/eval_jaxpr/shqk,skhd->sqhd/dot_general | solution.py:109
  123.4 1.9 fusion.130
  126.7 4.9 %fusion.127 = f32[8,512]{1,0:T(8,128)S(1)} fusion(f32[8,512,512]{1,2,0:T(8,128)} %get-tuple-element.248, bf16[512,8,32]{0,2,1:T(8,128)(2,1)S(1)} %bitcast.111, bf16[512,8,32]{0,2,1:T(8,128)(2,1)S(1)} %bitcast.113), kind=kOutput, calls=%fused_computation.100.clone.1 | convolution fusion | flops 140509696 | bytes 8929280 | tf_op jit(solution)/shard_map/while/body/eval_jaxpr/sub | solution.py:108
  132.7 6.8 %fusion.128 = f32[8,32,512]{2,1,0:T(8,128)S(1)} fusion(bf16[512,8,32]{0,2,1:T(8,128)(2,1)S(1)} %bitcast.115, f32[8,512]{1,0:T(8,128)S(1)} %fusion.127, f32[8,512,512]{1,2,0:T(8,128)} %get-tuple-element.248, bf16[512,8,32]{0,2,1:T(8,128)(2,1)S(1)} %bitcast.112, bf16[512,8,32]{0,2,1:T(8,128)(2,1)S(1)} %bitcast.114), kind=kOutput, calls=%fused_computation.3.clone.1 | convolution fusion | flops 276828672 | bytes 9715712 | tf_op jit(solution)/shard_map/while/body/eval_jaxpr/shqk,skhd->sqhd/dot_general | solution.py:109
  140.9 1.9 fusion.130
  144.2 4.9 %fusion.127 = f32[8,512]{1,0:T(8,128)S(1)} fusion(f32[8,512,512]{1,2,0:T(8,128)} %get-tuple-element.248, bf16[512,8,32]{0,2,1:T(8,128)(2,1)S(1)} %bitcast.111, bf16[512,8,32]{0,2,1:T(8,128)(2,1)S(1)} %bitcast.113), kind=kOutput, calls=%fused_computation.100.clone.1 | convolution fusion | flops 140509696 | bytes 8929280 | tf_op jit(solution)/shard_map/while/body/eval_jaxpr/sub | solution.py:108
  150.2 6.8 %fusion.128 = f32[8,32,512]{2,1,0:T(8,128)S(1)} fusion(bf16[512,8,32]{0,2,1:T(8,128)(2,1)S(1)} %bitcast.115, f32[8,512]{1,0:T(8,128)S(1)} %fusion.127, f32[8,512,512]{1,2,0:T(8,128)} %get-tuple-element.248, bf16[512,8,32]{0,2,1:T(8,128)(2,1)S(1)} %bitcast.112, bf16[512,8,32]{0,2,1:T(8,128)(2,1)S(1)} %bitcast.114), kind=kOutput, calls=%fused_computation.3.clone.1 | convolution fusion | flops 276828672 | bytes 9715712 | tf_op jit(solution)/shard_map/while/body/eval_jaxpr/shqk,skhd->sqhd/dot_general | solution.py:109
  158.4 1.9 fusion.130
  161.7 4.9 %fusion.127 = f32[8,512]{1,0:T(8,128)S(1)} fusion(f32[8,512,512]{1,2,0:T(8,128)} %get-tuple-element.248, bf16[512,8,32]{0,2,1:T(8,128)(2,1)S(1)} %bitcast.111, bf16[512,8,32]{0,2,1:T(8,128)(2,1)S(1)} %bitcast.113), kind=kOutput, calls=%fused_computation.100.clone.1 | convolution fusion | flops 140509696 | bytes 8929280 | tf_op jit(solution)/shard_map/while/body/eval_jaxpr/sub | solution.py:108
  167.7 6.8 %fusion.128 = f32[8,32,512]{2,1,0:T(8,128)S(1)} fusion(bf16[512,8,32]{0,2,1:T(8,128)(2,1)S(1)} %bitcast.115, f32[8,512]{1,0:T(8,128)S(1)} %fusion.127, f32[8,512,512]{1,2,0:T(8,128)} %get-tuple-element.248, bf16[512,8,32]{0,2,1:T(8,128)(2,1)S(1)} %bitcast.112, bf16[512,8,32]{0,2,1:T(8,128)(2,1)S(1)} %bitcast.114), kind=kOutput, calls=%fused_computation.3.clone.1 | convolution fusion | flops 276828672 | bytes 9715712 | tf_op jit(solution)/shard_map/while/body/eval_jaxpr/shqk,skhd->sqhd/dot_general | solution.py:109
  175.9 1.9 fusion.130
  179.2 4.9 %fusion.127 = f32[8,512]{1,0:T(8,128)S(1)} fusion(f32[8,512,512]{1,2,0:T(8,128)} %get-tuple-element.248, bf16[512,8,32]{0,2,1:T(8,128)(2,1)S(1)} %bitcast.111, bf16[512,8,32]{0,2,1:T(8,128)(2,1)S(1)} %bitcast.113), kind=kOutput, calls=%fused_computation.100.clone.1 | convolution fusion | flops 140509696 | bytes 8929280 | tf_op jit(solution)/shard_map/while/body/eval_jaxpr/sub | solution.py:108
  185.2 6.8 %fusion.128 = f32[8,32,512]{2,1,0:T(8,128)S(1)} fusion(bf16[512,8,32]{0,2,1:T(8,128)(2,1)S(1)} %bitcast.115, f32[8,512]{1,0:T(8,128)S(1)} %fusion.127, f32[8,512,512]{1,2,0:T(8,128)} %get-tuple-element.248, bf16[512,8,32]{0,2,1:T(8,128)(2,1)S(1)} %bitcast.112, bf16[512,8,32]{0,2,1:T(8,128)(2,1)S(1)} %bitcast.114), kind=kOutput, calls=%fused_computation.3.clone.1 | convolution fusion | flops 276828672 | bytes 9715712 | tf_op jit(solution)/shard_map/while/body/eval_jaxpr/shqk,skhd->sqhd/dot_general | solution.py:109
  193.4 1.9 fusion.130
  196.7 4.9 %fusion.127 = f32[8,512]{1,0:T(8,128)S(1)} fusion(f32[8,512,512]{1,2,0:T(8,128)} %get-tuple-element.248, bf16[512,8,32]{0,2,1:T(8,128)(2,1)S(1)} %bitcast.111, bf16[512,8,32]{0,2,1:T(8,128)(2,1)S(1)} %bitcast.113), kind=kOutput, calls=%fused_computation.100.clone.1 | convolution fusion | flops 140509696 | bytes 8929280 | tf_op jit(solution)/shard_map/while/body/eval_jaxpr/sub | solution.py:108
  202.7 6.8 %fusion.128 = f32[8,32,512]{2,1,0:T(8,128)S(1)} fusion(bf16[512,8,32]{0,2,1:T(8,128)(2,1)S(1)} %bitcast.115, f32[8,512]{1,0:T(8,128)S(1)} %fusion.127, f32[8,512,512]{1,2,0:T(8,128)} %get-tuple-element.248, bf16[512,8,32]{0,2,1:T(8,128)(2,1)S(1)} %bitcast.112, bf16[512,8,32]{0,2,1:T(8,128)(2,1)S(1)} %bitcast.114), kind=kOutput, calls=%fused_computation.3.clone.1 | convolution fusion | flops 276828672 | bytes 9715712 | tf_op jit(solution)/shard_map/while/body/eval_jaxpr/shqk,skhd->sqhd/dot_general | solution.py:109
  214.2 4.9 %fusion.127 = f32[8,512]{1,0:T(8,128)S(1)} fusion(f32[8,512,512]{1,2,0:T(8,128)} %get-tuple-element.248, bf16[512,8,32]{0,2,1:T(8,128)(2,1)S(1)} %bitcast.111, bf16[512,8,32]{0,2,1:T(8,128)(2,1)S(1)} %bitcast.113), kind=kOutput, calls=%fused_computation.100.clone.1 | convolution fusion | flops 140509696 | bytes 8929280 | tf_op jit(solution)/shard_map/while/body/eval_jaxpr/sub | solution.py:108
  220.2 6.8 %fusion.128 = f32[8,32,512]{2,1,0:T(8,128)S(1)} fusion(bf16[512,8,32]{0,2,1:T(8,128)(2,1)S(1)} %bitcast.115, f32[8,512]{1,0:T(8,128)S(1)} %fusion.127, f32[8,512,512]{1,2,0:T(8,128)} %get-tuple-element.248, bf16[512,8,32]{0,2,1:T(8,128)(2,1)S(1)} %bitcast.112, bf16[512,8,32]{0,2,1:T(8,128)(2,1)S(1)} %bitcast.114), kind=kOutput, calls=%fused_computation.3.clone.1 | convolution fusion | flops 276828672 | bytes 9715712 | tf_op jit(solution)/shard_map/while/body/eval_jaxpr/shqk,skhd->sqhd/dot_general | solution.py:109
  231.6 4.9 %fusion.127 = f32[8,512]{1,0:T(8,128)S(1)} fusion(f32[8,512,512]{1,2,0:T(8,128)} %get-tuple-element.248, bf16[512,8,32]{0,2,1:T(8,128)(2,1)S(1)} %bitcast.111, bf16[512,8,32]{0,2,1:T(8,128)(2,1)S(1)} %bitcast.113), kind=kOutput, calls=%fused_computation.100.clone.1 | convolution fusion | flops 140509696 | bytes 8929280 | tf_op jit(solution)/shard_map/while/body/eval_jaxpr/sub | solution.py:108
  237.7 6.8 %fusion.128 = f32[8,32,512]{2,1,0:T(8,128)S(1)} fusion(bf16[512,8,32]{0,2,1:T(8,128)(2,1)S(1)} %bitcast.115, f32[8,512]{1,0:T(8,128)S(1)} %fusion.127, f32[8,512,512]{1,2,0:T(8,128)} %get-tuple-element.248, bf16[512,8,32]{0,2,1:T(8,128)(2,1)S(1)} %bitcast.112, bf16[512,8,32]{0,2,1:T(8,128)(2,1)S(1)} %bitcast.114), kind=kOutput, calls=%fused_computation.3.clone.1 | convolution fusion | flops 276828672 | bytes 9715712 | tf_op jit(solution)/shard_map/while/body/eval_jaxpr/shqk,skhd->sqhd/dot_general | solution.py:109
  247.8 2.8 copy.141
  250.5 35.5 %all_to_all.27 = bf16[8,512,256]{2,0,1:T(8,128)(2,1)S(1)} all-to-all(bf16[8,512,256]{2,0,1:T(8,128)(2,1)S(1)} %bitcast.109), channel_id=1, replica_groups=mesh['batch'=4,'dap'=32] {'dap'}, dimensions={1} | all-to-all | bytes 4194304 | tf_op jit(solution)/shard_map/all_to_all | solution.py:124
  286.1 2.5 fusion.89
  291.3 2.8 copy.103
  294.1 2.0 copy-done.1
  296.1 2.3 fusion.46
  298.5 8.0 %fusion.91 = (bf16[4096,1024]{1,0:T(8,128)(2,1)S(1)}, f32[4096,1024]{1,0:T(8,128)}) fusion(bf16[4096,256]{1,0:T(8,128)(2,1)S(1)} %fusion.46, bf16[256,256]{1,0:T(8,128)(2,1)S(1)} %copy-done.9, bf16[256,256]{1,0:T(8,128)(2,1)S(1)} %copy-done.10, bf16[256,256]{1,0:T(8,128)(2,1)S(1)} %copy-done.11, bf16[256,256]{1,0:T(8,128)(2,1)S(1)} %copy-done.12), kind=kOutput, calls=%fused_computation.105 | convolution fusion | flops 2153775104 | bytes 27787264 | tf_op jit(solution)/shard_map/dot_general | solution.py:26
  308.1 6.2 %reshape_reshape.27 = bf16[256,16,8,32]{3,2,1,0:T(8,128)(2,1)} reshape(bf16[4096,256]{1,0:T(8,128)(2,1)S(1)} %get-tuple-element.143) | data formatting | bytes 4194304 | tf_op jit(solution)/shard_map/reshape;reshape | solution.py:132
  314.3 2.6 fusion.32
  316.9 6.2 %reshape_reshape.26 = bf16[256,16,8,32]{3,2,1,0:T(8,128)(2,1)} reshape(bf16[4096,256]{1,0:T(8,128)(2,1)S(1)} %fusion.32) | data formatting | bytes 4194304 | tf_op jit(solution)/shard_map/reshape;reshape | solution.py:131
  323.1 10.0 %reshape_reshape.25 = bf16[256,16,8,32]{3,2,1,0:T(8,128)(2,1)} reshape(bf16[4096,256]{1,0:T(8,128)(2,1)} %get-tuple-element.142) | data formatting | bytes 4194304 | tf_op jit(solution)/shard_map/reshape;reshape | solution.py:133
  333.1 21.3 %fusion.92 = (f32[16,8,256]{2,1,0:T(8,128)S(1)}, f32[16,8,256,256]{2,3,1,0:T(8,128)}) fusion(bf16[256,16,8,32]{3,2,1,0:T(8,128)(2,1)} %reshape_reshape.27, bf16[256,16,8,32]{3,2,1,0:T(8,128)(2,1)} %reshape_reshape.26), kind=kOutput, calls=%fused_computation.106 | convolution fusion | flops 553648384 | bytes 37879808 | tf_op jit(solution)/shard_map/sub | solution.py:137
  354.4 18.0 %fusion.49 = f32[256,16,8,32]{0,3,2,1:T(8,128)} fusion(f32[16,8,256,256]{2,3,1,0:T(8,128)} %get-tuple-element.153, f32[16,8,256]{2,1,0:T(8,128)S(1)} %get-tuple-element.152, bf16[256,16,8,32]{3,2,1,0:T(8,128)(2,1)} %reshape_reshape.25), kind=kOutput, calls=%fused_computation.68 | convolution fusion | flops 553648128 | bytes 39976960 | tf_op jit(solution)/shard_map/rhst,trhd->srhd/dot_general | solution.py:138
  372.4 14.4 %copy.114 = f32[256,16,8,32]{3,2,1,0:T(8,128)} copy(f32[256,16,8,32]{0,3,2,1:T(8,128)} %fusion.49) | data formatting | bytes 8388608 | tf_op jit(solution)/shard_map/rhst,trhd->srhd/transpose | solution.py:138
  386.7 12.2 %reshape.158 = f32[4096,256]{1,0:T(8,128)} reshape(f32[256,16,8,32]{3,2,1,0:T(8,128)} %copy.114) | data formatting | bytes 8388608 | tf_op jit(solution)/shard_map/reshape | solution.py:141
  399.0 4.8 %convolution_add_fusion.1 = f32[4096,256]{1,0:T(8,128)S(1)} fusion(bf16[256,256]{1,0:T(8,128)(2,1)S(1)} %copy-done, f32[256]{0:T(256)S(1)} %copy-done.21, f32[4096,256]{1,0:T(8,128)} %reshape.158, f32[4096,1024]{1,0:T(8,128)} %get-tuple-element.151, f32[256]{0:T(256)S(1)} %copy-done.22), kind=kOutput, calls=%fused_computation.27 | convolution fusion | flops 544210944 | bytes 12716032 | tf_op jit(solution)/shard_map/dot_general | solution.py:43
  404.9 32.6 %all_to_all.28 = bf16[256,16,256]{2,1,0:T(8,128)(2,1)S(1)} all-to-all(bf16[256,16,256]{2,1,0:T(8,128)(2,1)S(1)} %fusion.47), channel_id=1, replica_groups=mesh['batch'=4,'dap'=32] {'dap'}, dimensions={0} | all-to-all | bytes 4194304 | tf_op jit(solution)/shard_map/all_to_all | solution.py:142
  (137 shorter events, 45.4 us)
Async XLA Ops:
  6.5 392.4 %copy-start = (bf16[256,256]{1,0:T(8,128)(2,1)S(1)}, bf16[256,256]{1,0:T(8,128)(2,1)}, u32[]{:S(2)}) copy-start(bf16[256,256]{1,0:T(8,128)(2,1)} %param.44) | copy-start | bytes 393220
  6.5 6.1 %copy-start.23 = (f32[128]{0:T(128)S(1)}, f32[128]{0:T(128)}, u32[]{:S(2)}) copy-start(f32[128]{0:T(128)} %param.28) | copy-start | bytes 1540
  6.5 6.1 %copy-start.19 = (bf16[128,8]{0,1:T(8,128)(2,1)S(1)}, bf16[128,8]{0,1:T(8,128)(2,1)}, u32[]{:S(2)}) copy-start(bf16[128,8]{0,1:T(8,128)(2,1)} %param.29) | copy-start | bytes 6148
  6.5 9.7 %copy-start.3 = (bf16[8,512,256]{2,1,0:T(8,128)(2,1)S(1)}, bf16[8,512,256]{2,1,0:T(8,128)(2,1)}, u32[]{:S(2)}) copy-start(bf16[8,512,256]{2,1,0:T(8,128)(2,1)} %param.24) | copy-start | bytes 6291460
  6.5 92.6 %all-gather.2.cloned.1.call-start = ((), (), s32[]{:S(2)}) async-start(), calls=%async_computation.2 | async-start | bytes 4325376 | tf_op jit(solution)/shard_map/all_gather | solution.py:91
  6.6 6.0 %copy-start.4 = (bf16[16,512,128]{2,1,0:T(8,128)(2,1)S(1)}, bf16[16,512,128]{2,1,0:T(8,128)(2,1)}, u32[]{:S(2)}) copy-start(bf16[16,512,128]{2,1,0:T(8,128)(2,1)} %param.25) | copy-start | bytes 6291460
  12.6 5.6 %copy-start.15 = (f32[256]{0:T(256)S(1)}, f32[256]{0:T(256)}, u32[]{:S(2)}) copy-start(f32[256]{0:T(256)} %param.27) | copy-start | bytes 3076
  12.6 5.6 %copy-start.16 = (f32[256]{0:T(256)S(1)}, f32[256]{0:T(256)}, u32[]{:S(2)}) copy-start(f32[256]{0:T(256)} %param.26) | copy-start | bytes 3076
  16.3 4.7 %copy-start.5 = (bf16[256,256]{1,0:T(8,128)(2,1)S(1)}, bf16[256,256]{1,0:T(8,128)(2,1)}, u32[]{:S(2)}) copy-start(bf16[256,256]{1,0:T(8,128)(2,1)} %param.33) | copy-start | bytes 393220
  16.3 4.7 %copy-start.6 = (bf16[256,256]{1,0:T(8,128)(2,1)S(1)}, bf16[256,256]{1,0:T(8,128)(2,1)}, u32[]{:S(2)}) copy-start(bf16[256,256]{1,0:T(8,128)(2,1)} %param.32) | copy-start | bytes 393220
  16.3 4.7 %copy-start.7 = (bf16[256,256]{1,0:T(8,128)(2,1)S(1)}, bf16[256,256]{1,0:T(8,128)(2,1)}, u32[]{:S(2)}) copy-start(bf16[256,256]{1,0:T(8,128)(2,1)} %param.31) | copy-start | bytes 393220
  16.3 4.7 %copy-start.8 = (bf16[256,256]{1,0:T(8,128)(2,1)S(1)}, bf16[256,256]{1,0:T(8,128)(2,1)}, u32[]{:S(2)}) copy-start(bf16[256,256]{1,0:T(8,128)(2,1)} %param.30) | copy-start | bytes 393220
  24.9 2.3 copy-start.17
  31.0 76.8 %copy-start.18 = (bf16[256,256]{1,0:T(8,128)(2,1)S(1)}, bf16[256,256]{1,0:T(8,128)(2,1)}, u32[]{:S(2)}) copy-start(bf16[256,256]{1,0:T(8,128)(2,1)} %param.35) | copy-start | bytes 393220
  31.0 76.8 %copy-start.20 = (f32[256]{0:T(256)S(1)}, f32[256]{0:T(256)}, u32[]{:S(2)}) copy-start(f32[256]{0:T(256)} %param.36) | copy-start | bytes 3076
  291.3 4.8 %copy-start.13 = (f32[256]{0:T(256)S(1)}, f32[256]{0:T(256)}, u32[]{:S(2)}) copy-start(f32[256]{0:T(256)} %param.38) | copy-start | bytes 3076
  291.3 4.8 %copy-start.14 = (f32[256]{0:T(256)S(1)}, f32[256]{0:T(256)}, u32[]{:S(2)}) copy-start(f32[256]{0:T(256)} %param.37) | copy-start | bytes 3076
  294.1 2.0 copy-start.1
  296.1 2.3 copy-start.9
  296.1 2.3 copy-start.10
  296.1 2.3 copy-start.11
  296.1 2.3 copy-start.12
  386.7 12.2 %copy-start.21 = (f32[256]{0:T(256)S(1)}, f32[256]{0:T(256)}, u32[]{:S(2)}) copy-start(f32[256]{0:T(256)} %param.45) | copy-start | bytes 3076
  386.7 12.2 %copy-start.22 = (f32[256]{0:T(256)S(1)}, f32[256]{0:T(256)}, u32[]{:S(2)}) copy-start(f32[256]{0:T(256)} %param.43) | copy-start | bytes 3076
  399.0 4.9 %copy-start.2 = (f32[32,8,16,256]{3,2,1,0:T(8,128)S(1)}, f32[32,8,16,256]{3,2,1,0:T(8,128)}, u32[]{:S(2)}) copy-start(f32[32,8,16,256]{3,2,1,0:T(8,128)} %copy-done.1) | copy-start | bytes 12582916
Sparse Core Ops, SparseCore 0:
  16.4 82.7 all-gather.1
where the time goes:
time: 448 us; the launch traced here: 446 us
  matrix products  168 us (38%)
  local copies, waits for them, and re-layouts  101 us (23%)
  blocking collectives  68.2 us (15%)
  waiting for transfers between devices  68.1 us (15%)
  other arithmetic  25.6 us (6%)
  between operations  13.8 us (3%)
    all_gather x1, waiting for transfers between devices, per_device(): whole_bias = lax.all_gather(bias_local, 'dap', axis=1, tiled=True)  68.1 us
    dot_general x8, matrix products, one_group(): jnp.einsum('shqk,skhd->sqhd', weights, value_heads, preferred_element_typ...  54.2 us
    sub x8, matrix products, one_group(): weights = jax.nn.softmax(scores, axis=-1).astype(jnp.bfloat16)  39.2 us
    all_to_all x1, blocking collectives, per_device(): lax.all_to_all(after_rows, 'dap', split_axis=1, concat_axis=0, tiled=True)  35.5 us
    all_to_all x1, blocking collectives, per_device(): lax.all_to_all(output_layer(gated, received, column_output, column_output...  32.6 us
    dynamic_slice x56, local copies, waits for them, and re-layouts, per_device(): result = lax.map(one_group, grouped_parts)  30 us
    sub x1, matrix products, per_device(): weights = jax.nn.softmax(scores, axis=-1).astype(jnp.bfloat16)  21.3 us
    dot_general x9, matrix products, output_layer(): jnp.dot(flattened, out_weight, preferred_element_type=jnp.float32)  20.3 us
  transfers between devices with their start and end apart: 1, of which 1 were waited for; matrix products, arithmetic and copies ran while one was open for 3% of the time, Pallas kernels for 0%

commit v1 on v0

v1 whole, which is shorter than its diff:
```python
import functools

import jax
import jax.numpy as jnp
from jax import lax
from jax.experimental import pallas as pl
from jax.experimental.pallas import tpu as pltpu
from jax.sharding import PartitionSpec as P

H = 8
HEAD = 32
C = 256
LANES = 128
GROUP = LANES // HEAD
EPS = 1e-05
BLOCK = 32
VMEM = 56 * 1024 * 1024
NZ, NX, NY = 4, 4, 2
DAP = NZ * NX * NY
NT = (((1,), (1,)), ((), ()))


def norm(x, gain, bias):
    center = jnp.mean(x, axis=-1, keepdims=True)
    moved = x - center
    spread = jnp.mean(moved * moved, axis=-1, keepdims=True)
    return (moved * lax.rsqrt(spread + EPS) * gain + bias).astype(jnp.bfloat16)


def lanes_of(part):
    return slice(part * LANES, (part + 1) * LANES)


def dot(a, b):
    return jnp.dot(a, b, preferred_element_type=jnp.float32)


def softmax_rounded(scores):
    top = jnp.max(scores, axis=-1, keepdims=True)
    e = jnp.exp(scores - top)
    total = jnp.sum(e, axis=-1, keepdims=True)
    return (e * (1.0 / total)).astype(jnp.bfloat16)


def head_of_lane():
    return lax.broadcasted_iota(jnp.int32, (1, LANES), 1) // HEAD


def stacked(q):
    head = head_of_lane()
    masks = [(head == i).astype(jnp.float32).astype(jnp.bfloat16) for i in range(GROUP)]
    return jnp.concatenate([q * mask for mask in masks], axis=0)


def own_lanes(mixed):
    head = head_of_lane()
    rows = mixed.shape[0] // GROUP
    total = mixed[:rows]
    for i in range(1, GROUP):
        total = jnp.where(head == i, mixed[i * rows : (i + 1) * rows], total)
    return total


def pipelined(count, score, soften, average):
    scores, weights = {0: score(0)}, {}
    for n in range(count + 1):
        if n + 1 < count:
            scores[n + 1] = score(n + 1)
        if n < count:
            weights[n] = soften(n, scores.pop(n))
        if n >= 1:
            average(n - 1, weights.pop(n - 1))


def project(normed, q_w, k_w, v_w, g_w, g_b):
    q = (dot(normed, q_w[...]) * HEAD ** (-0.5)).astype(jnp.bfloat16)
    k_t = dot(normed, k_w[...]).T.astype(jnp.bfloat16)
    v = dot(normed, v_w[...]).astype(jnp.bfloat16)
    g = jax.nn.sigmoid(dot(normed, g_w[...]) + g_b[...])
    return q, k_t, v, g


def pair_kernel(x_ref, gain_ref, w_ref, out_ref, held):
    step = pl.program_id(0)
    rows = x_ref.shape[0]
    heads, count, _ = out_ref.shape
    for i in range(rows):
        normed = norm(x_ref[i].astype(jnp.float32), gain_ref[...], 0.0)
        bias = lax.dot_general(w_ref[...], normed, NT, preferred_element_type=jnp.float32)
        for part in range(held.shape[0]):
            held[part, pl.ds(step * rows + i, H, stride=count), :] = bias[:, lanes_of(part)]

    @pl.when(step == pl.num_programs(0) - 1)
    def _():
        for part in range(held.shape[0]):
            out_ref[:, :, lanes_of(part)] = (
                held[part].astype(jnp.bfloat16).reshape(heads, count, LANES)
            )


def pair_bias(pair_state, gain, weight):
    count, res, cz = pair_state.shape
    rows = 4
    return pl.pallas_call(
        pair_kernel,
        grid=(count // rows,),
        out_shape=jax.ShapeDtypeStruct((H, count, res), jnp.bfloat16),
        in_specs=[
            pl.BlockSpec((rows, res, cz), lambda i: (i, 0, 0)),
            pl.BlockSpec((1, cz), lambda i: (0, 0)),
            pl.BlockSpec((H, cz), lambda i: (0, 0)),
        ],
        out_specs=pl.BlockSpec((H, count, res), lambda i: (0, 0, 0)),
        scratch_shapes=[pltpu.VMEM((res // LANES, H * count, LANES), jnp.float32)],
        compiler_params=pltpu.CompilerParams(vmem_limit_bytes=VMEM),
        name="pair_bias",
    )(pair_state, gain.reshape(1, cz), weight.T)


def project_kernel(x_ref, gain, bias, q_w, k_w, v_w, g_w, g_b, *refs):
    q_ref, k_ref, v_ref, g_ref = refs[-4:]
    count, res, width = x_ref.shape
    x = x_ref[...].reshape(count * res, width).astype(jnp.float32)
    normed = norm(x, gain[...], bias[...])
    q, k_t, v, g = project(normed, q_w, k_w, v_w, g_w, g_b)
    for out_ref, value in ((q_ref, q), (v_ref, v), (g_ref, g)):
        out_ref[...] = value.reshape(count, res, width)
    for n in range(count):
        k_ref[n] = k_t[:, n * res : (n + 1) * res]


def row_project(first, count, held, x, gain, bias, q_w, k_w, v_w, g_w, g_b):
    seqs, res, width = x.shape
    once = 2
    block = pl.BlockSpec((once, res, width), lambda s: (first // once + s, 0, 0))
    turned = pl.BlockSpec((once, width, res), lambda s: (first // once + s, 0, 0))
    vector = pl.BlockSpec((1, width), lambda s: (0, 0))
    weight = pl.BlockSpec((width, width), lambda s: (0, 0))
    shape = jax.ShapeDtypeStruct
    return pl.pallas_call(
        project_kernel,
        grid=(count // once,),
        out_shape=[
            shape((seqs, res, width), jnp.bfloat16),
            shape((seqs, width, res), jnp.bfloat16),
            shape((seqs, res, width), jnp.bfloat16),
            shape((seqs, res, width), jnp.float32),
        ],
        in_specs=[block, vector, vector]
        + [weight] * 4
        + [vector]
        + [pl.BlockSpec(memory_space=pl.ANY)] * len(held),
        out_specs=[block, turned, block, block],
        input_output_aliases={8 + n: n for n in range(len(held))},
        compiler_params=pltpu.CompilerParams(vmem_limit_bytes=VMEM),
        cost_estimate=pl.CostEstimate(
            flops=2 * count * res * width * width * 4,
            bytes_accessed=count * res * width * 12,
            transcendentals=count * res * width * 2,
        ),
        name="row_project",
    )(x, gain.reshape(1, -1), bias.reshape(1, -1), q_w, k_w, v_w, g_w, g_b.reshape(1, -1), *held)


def row_kernel(layout, tile, here_ref, q_ref, k_ref, v_ref, g_ref, x_ref, o_w, o_b, *rest):
    pieces, (out_ref, whole, held, weights, sems) = rest[: len(layout)], rest[len(layout) :]
    res = q_ref.shape[1]
    own = res // DAP

    @pl.when(pl.program_id(0) == 0)
    def _():
        copies = []
        z, x, y = here_ref[0], here_ref[1], here_ref[2]
        for n, (piece, (first_head, slots)) in enumerate(zip(pieces, layout)):
            heads = piece.shape[1]
            for m, (zo, xo, yo) in enumerate(slots):
                owner = (
                    lax.rem(z + zo, NZ) * (NX * NY) + lax.rem(x + xo, NX) * NY + lax.rem(y + yo, NY)
                )
                rows = pl.ds(pl.multiple_of(owner * own, own), own)
                copies.append(
                    pltpu.make_async_copy(
                        piece.at[m], whole.at[pl.ds(first_head, heads), rows, :], sems.at[n, m]
                    )
                )
        for copy in copies:
            copy.start()
        for copy in copies:
            copy.wait()

    def place(n):
        t, group = divmod(n, H // GROUP)
        return slice(t * tile, (t + 1) * tile), lanes_of(group), group

    def score(n):
        rows, lanes, _ = place(n)
        held[n % 2] = dot(stacked(q_ref[0, rows, lanes]), k_ref[0, lanes, :])

    def soften(n, _):
        rows, _, group = place(n)
        for i in range(GROUP):
            for low in range(0, tile, BLOCK):
                here = slice(i * tile + low, i * tile + low + BLOCK)
                bias = whole[group * GROUP + i, rows.start + low : rows.start + low + BLOCK, :]
                weights[n % 2, here] = softmax_rounded(held[n % 2, here] + bias.astype(jnp.float32))

    gated = {}

    def average(n, _):
        rows, lanes, group = place(n)
        mixed = own_lanes(dot(weights[n % 2], v_ref[0, :, lanes]))
        gated[group] = (mixed * g_ref[0, rows, lanes]).astype(jnp.bfloat16)
        if len(gated) == H // GROUP:
            both = jnp.concatenate([gated.pop(part) for part in range(H // GROUP)], axis=1)
            after = x_ref[0, rows, :].astype(jnp.float32) + (dot(both, o_w[...]) + o_b[...])
            out_ref[rows.start // own : rows.stop // own, 0] = after.astype(jnp.bfloat16).reshape(
                tile // own, own, C
            )

    pipelined(res // tile * (H // GROUP), score, soften, average)


def row_attention(here, q, k, v, g, x, o_w, o_b, pieces, layout):
    seqs, res, width = x.shape
    own = res // DAP
    block = pl.BlockSpec((1, res, width), lambda s, *_: (s, 0, 0))
    turned = pl.BlockSpec((1, width, res), lambda s, *_: (s, 0, 0))
    most = max(len(slots) for _, slots in layout)
    return pl.pallas_call(
        functools.partial(row_kernel, layout, 256),
        out_shape=jax.ShapeDtypeStruct((DAP, seqs, own, width), jnp.bfloat16),
        grid_spec=pltpu.PrefetchScalarGridSpec(
            num_scalar_prefetch=1,
            grid=(seqs,),
            in_specs=[block, turned, block, block, block]
            + [
                pl.BlockSpec((width, width), lambda s, *_: (0, 0)),
                pl.BlockSpec((1, width), lambda s, *_: (0, 0)),
            ]
            + [pl.BlockSpec(memory_space=pl.ANY)] * len(pieces),
            out_specs=pl.BlockSpec((DAP, 1, own, width), lambda s, *_: (0, s, 0, 0)),
            scratch_shapes=[
                pltpu.VMEM((H, res, res), jnp.bfloat16),
                pltpu.VMEM((2, GROUP * 256, res), jnp.float32),
                pltpu.VMEM((2, GROUP * 256, res), jnp.bfloat16),
                pltpu.SemaphoreType.DMA((len(layout), most)),
            ],
        ),
        compiler_params=pltpu.CompilerParams(vmem_limit_bytes=VMEM),
        name="row_attention",
    )(here, q, k, v, g, x, o_w, o_b.reshape(1, -1), *pieces)


def column_kernel(at_once, x_ref, gain, bias, q_w, k_w, v_w, g_w, g_b, o_w, o_b, out_ref, held):
    step = pl.program_id(0)
    seqs, items, width = x_ref.shape
    parts = width // LANES

    @pl.when(step == 0)
    def _():
        for part in range(parts):
            held[part] = (
                x_ref[:, :, lanes_of(part)].astype(jnp.float32).reshape(seqs * items, LANES)
            )

    mine = [pl.ds(step * at_once + n, seqs, stride=items) for n in range(at_once)]
    x = jnp.concatenate(
        [jnp.concatenate([held[part, rows, :] for rows in mine], axis=0) for part in range(parts)], axis=1
    )
    normed = norm(x, gain[...], bias[...])
    q, k_t, v, g = project(normed, q_w, k_w, v_w, g_w, g_b)
    gated = {}

    def place(n):
        return slice(n // parts * seqs, (n // parts + 1) * seqs), lanes_of(n % parts)

    def score(n):
        rows, lanes = place(n)
        return dot(stacked(q[rows, lanes]), k_t[lanes, rows])

    def average(n, weights):
        rows, lanes = place(n)
        mixed = own_lanes(dot(weights, v[rows, lanes]))
        gated[n] = (mixed * g[rows, lanes]).astype(jnp.bfloat16)

    pipelined(at_once * parts, score, lambda n, scores: softmax_rounded(scores), average)
    gated = [
        jnp.concatenate([gated[n * parts + part] for part in range(parts)], axis=1)
        for n in range(at_once)
    ]
    after = x + (dot(jnp.concatenate(gated, axis=0), o_w[...]) + o_b[...])
    for n, rows in enumerate(mine):
        for part in range(parts):
            held[part, rows, :] = after[n * seqs : (n + 1) * seqs, lanes_of(part)]

    @pl.when(step == pl.num_programs(0) - 1)
    def _():
        for part in range(parts):
            out_ref[:, :, lanes_of(part)] = (
                held[part].astype(jnp.bfloat16).reshape(seqs, items, LANES)
            )


def column_attention(x, gain, bias, q_w, k_w, v_w, g_w, g_b, o_w, o_b):
    seqs, items, width = x.shape
    at_once = 2
    whole = pl.BlockSpec(x.shape, lambda r: (0, 0, 0))
    vector = pl.BlockSpec((1, width), lambda r: (0, 0))
    weight = pl.BlockSpec((width, width), lambda r: (0, 0))
    return pl.pallas_call(
        functools.partial(column_kernel, at_once),
        grid=(items // at_once,),
        out_shape=jax.ShapeDtypeStruct(x.shape, jnp.bfloat16),
        in_specs=[whole, vector, vector] + [weight] * 4 + [vector, weight, vector],
        out_specs=whole,
        scratch_shapes=[pltpu.VMEM((width // LANES, seqs * items, LANES), jnp.float32)],
        compiler_params=pltpu.CompilerParams(vmem_limit_bytes=VMEM),
        name="column_attention",
    )(
        x, gain.reshape(1, -1), bias.reshape(1, -1), q_w, k_w, v_w, g_w, g_b.reshape(1, -1),
        o_w, o_b.reshape(1, -1),
    )


def fetch(value, z=0, x=0, y=0):
    pairs = []
    for dz in range(NZ):
        for dx in range(NX):
            for dy in range(NY):
                src = ((dz + z) % NZ * NX + (dx + x) % NX) * NY + (dy + y) % NY
                pairs.append((src, (dz * NX + dx) * NY + dy))
    return lax.ppermute(value, "dap", pairs)


def shift(values, axis):
    return [(v, fetch(v, **{a: 1}), fetch(v, **{a: 3})) for v, a in zip(values, axis)]


def relay(rings, axis):
    out = []
    for (value, ahead, behind), a in zip(rings, axis):
        half = value.shape[0] // 2
        out.append([value, ahead, fetch(ahead[:half], **{a: 1}), fetch(behind[half:], **{a: 3}), behind])
    return out


def gather_bias(local, work):
    other = fetch(local, y=1)
    order, turned = ("x", "z"), ("z", "x")
    pairs = [
        jnp.stack([local[part * GROUP : (part + 1) * GROUP], other[part * GROUP : (part + 1) * GROUP]])
        for part in range(2)
    ]
    planes = [
        jnp.concatenate([fetch(pair, **{a: step}) if step else pair for step in range(4)])
        for pair, a in zip(pairs, order)
    ]
    rings = shift(planes, turned)
    rings, result = lax.optimization_barrier((rings, work[0]()))
    rings = relay(rings, turned)
    result = work[1](result)
    pieces, layout = [], []
    for part in range(2):
        first, second = order[part], turned[part]
        slots = [{first: a, second: 0, "y": b} for a in range(4) for b in range(NY)]
        half = len(slots) // 2
        for piece, kept, step in zip(
            rings[part], (slots, slots, slots[:half], slots[half:], slots), (0, 1, 2, 2, 3)
        ):
            pieces.append(piece)
            layout.append(
                (part * GROUP, [(s["z"], s["x"], s["y"]) for s in (dict(k, **{second: step}) for k in kept)])
            )
    return pieces, layout, result


def per_device(
    alignment,
    pair_state,
    row_norm_gain,
    row_norm_bias,
    pair_norm_gain,
    pair_weight,
    row_query,
    row_key,
    row_value,
    row_gate,
    row_gate_bias,
    row_output,
    row_output_bias,
    column_norm_gain,
    column_norm_bias,
    column_query,
    column_key,
    column_value,
    column_gate,
    column_gate_bias,
    column_output,
    column_output_bias,
):
    seqs, res, width = alignment.shape
    own = res // DAP
    me = lax.axis_index("dap")
    here = jnp.stack([me // (NX * NY), me // NY % NX, me % NY]).astype(jnp.int32)
    row = (
        alignment, row_norm_gain, row_norm_bias, row_query, row_key, row_value, row_gate, row_gate_bias
    )
    pieces, layout, (q, k, v, g) = gather_bias(
        pair_bias(pair_state, pair_norm_gain, pair_weight),
        (
            lambda: row_project(0, seqs // 2, (), *row),
            lambda held: row_project(seqs // 2, seqs // 2, held, *row),
        ),
    )
    after = row_attention(
        here, q, k, v, g, alignment, row_output, row_output_bias, pieces, layout
    )
    received = lax.all_to_all(after, "dap", split_axis=0, concat_axis=0, tiled=True)
    columns = column_attention(
        received.reshape(DAP * seqs, own, width),
        column_norm_gain,
        column_norm_bias,
        column_query,
        column_key,
        column_value,
        column_gate,
        column_gate_bias,
        column_output,
        column_output_bias,
    )
    back = lax.all_to_all(
        columns.reshape(DAP, seqs, own, width), "dap", split_axis=0, concat_axis=0, tiled=True
    )
    return back.transpose(1, 0, 2, 3).reshape(alignment.shape)


def solution(mesh):
    split = P(("batch", "dap"), None, None)
    return jax.shard_map(
        per_device,
        mesh=mesh,
        in_specs=(split, split) + (P(),) * 20,
        out_specs=split,
        check_vma=False,
    )
```

time: 448 us -> 186 us (0.42)
  matrix products: 168 us -> 0 us
  local copies, waits for them, and re-layouts: 101 us -> 6.34 us
  Pallas kernels: 0 us -> 74.6 us
  waiting for transfers between devices: 68.1 us -> 14.3 us
  other arithmetic: 25.6 us -> 0.65 us
  starting transfers between devices: 0.03 us -> 24.1 us
  between operations: 13.8 us -> 0.2 us
    dot_general x21 -> x0, matrix products: 108 us -> none  [the longest x8 54.2 us: one_group(): jnp.einsum('shqk,skhd->sqhd', weights, value_heads, preferred_element_typ...]
    pallas_call x0 -> x5, Pallas kernels: none -> 74.6 us  [the longest x1 35 us: row_attention(): pl.pallas_call(functools.partial(row_kernel, layout, 256), out_shape=jax....]
    all_gather x1 -> x0, waiting for transfers between devices: 68.1 us -> none  [per_device(): whole_bias = lax.all_gather(bias_local, 'dap', axis=1, tiled=True)]
    sub x9 -> x0, matrix products: 60.4 us -> none  [the longest x8 39.2 us: one_group(): weights = jax.nn.softmax(scores, axis=-1).astype(jnp.bfloat16)]
    dynamic_slice x56 -> x0, local copies, waits for them, and re-layouts: 30 us -> none  [per_device(): result = lax.map(one_group, grouped_parts)]
    ppermute x0 -> x15, starting transfers between devices: none -> 24.1 us  [fetch(): return lax.ppermute(value, 'dap', pairs)]
    another operation x3 -> x2, local copies, waits for them, and re-layouts: 22.4 us -> 0.89 us  [gather_bias(): jnp.stack([local[part * GROUP:(part + 1) * GROUP], other[part * GROUP:(pa...]
    ppermute x0 -> x15, waiting for transfers between devices: none -> 14.3 us  [fetch(): return lax.ppermute(value, 'dap', pairs)]
  transfers between devices with their start and end apart: 1 -> 15, of which waited for: 1 -> 8; matrix products, arithmetic and copies ran while one was open for 3% -> 3% of each run, Pallas kernels for 0% -> 5%
where the time goes in v1:
time: 186 us
  Pallas kernels  74.6 us (40%)
  blocking collectives  65.4 us (35%)
  starting transfers between devices  24.1 us (13%)
  waiting for transfers between devices  14.3 us (8%)
  local copies, waits for them, and re-layouts  6.34 us (3%)
    pallas_call x1, Pallas kernels, row_attention(): pl.pallas_call(functools.partial(row_kernel, layout, 256), out_shape=jax....  35 us
    all_to_all x1, blocking collectives, per_device(): lax.all_to_all(after, 'dap', split_axis=0, concat_axis=0, tiled=True)  34.3 us
    all_to_all x1, blocking collectives, per_device(): lax.all_to_all(columns.reshape(DAP, seqs, own, width), 'dap', split_axis=...  31.1 us
    pallas_call x1, Pallas kernels, column_attention(): pl.pallas_call(functools.partial(column_kernel, at_once), grid=(items //...  25 us
    ppermute x15, starting transfers between devices, fetch(): return lax.ppermute(value, 'dap', pairs)  24.1 us
    ppermute x15, waiting for transfers between devices, fetch(): return lax.ppermute(value, 'dap', pairs)  14.3 us
    pallas_call x2, Pallas kernels, row_project(): pl.pallas_call(project_kernel, grid=(count // once,), out_shape=[shape((s...  9.6 us
    pallas_call x1, Pallas kernels, pair_bias(): pl.pallas_call(pair_kernel, grid=(count // rows,), out_shape=jax.ShapeDty...  5.12 us
  transfers between devices with their start and end apart: 15, of which 8 were waited for; matrix products, arithmetic and copies ran while one was open for 3% of the time, Pallas kernels for 5%

profile of v1, /device:TPU:0, one launch (start us, length us, event | category | flops | bytes accessed | tf_op | source)
XLA Modules:
  0.0 185.7 jit_solution(8287618169252228014)
XLA Ops:
  0.0 5.1 %pair_bias.1 = bf16[8,16,512]{2,1,0:T(8,128)(2,1)} custom-call(bf16[16,512,128]{2,1,0:T(8,128)(2,1)} %x_ref.4, f32[1,128]{1,0:T(1,128)} %bitcast.48, bf16[8,128]{1,0:T(8,128)(2,1)} %bitcast.36), custom_call_target="tpu_custom_call" | custom-call | tf_op jit(solution)/shard_map/pair_bias/pallas_call | solution.py:104
  5.1 3.3 %collective-permute-start = (bf16[8,16,512]{2,1,0:T(8,128)(2,1)}, bf16[8,16,512]{2,1,0:T(8,128)(2,1)S(1)}, u32[]{:S(2)}, u32[]{:S(2)}) collective-permute-start(bf16[8,16,512]{2,1,0:T(8,128)(2,1)} %pair_bias.1), channel_id=1, source_target_pairs={{1,0},{0,1},{3,2},{2,3},{5,4},{4,5},{7,6},{6,7},{9,8},{8,9},{11,10... | collective-permute-start | bytes 393224 | tf_op jit(solution)/shard_map/ppermute | solution.py:332
  8.4 0.9 constant_dynamic-update-slice_fusion.9
  9.3 0.9 slice_bitcast_fusion.1
  10.2 1.9 %collective-permute-done = bf16[8,16,512]{2,1,0:T(8,128)(2,1)S(1)} collective-permute-done((bf16[8,16,512]{2,1,0:T(8,128)(2,1)}, bf16[8,16,512]{2,1,0:T(8,128)(2,1)S(1)}, u32[]{:S(2)}, u32[]{:S(2)}) %collective-permute-start) | collective-permute-done | bytes 131104 | tf_op jit(solution)/shard_map/ppermute | solution.py:332
  12.1 4.2 %collective-permute-start.6 = (bf16[2,4,16,512]{3,2,1,0:T(8,128)(2,1)S(1)}, bf16[2,4,16,512]{3,2,1,0:T(8,128)(2,1)S(1)}, u32[]{:S(2)}, u32[]{:S(2)}) collective-permute-start(bf16[2,4,16,512]{3,2,1,0:T(8,128)(2,1)S(1)} %pad_maximum_fusion.1), channel_id=1, source_target_pairs={{8,0},{9,1},{10,2},{11,3},{12,4},{13,5},{14,6},{15,7},{16,8},{17,9... | collective-permute-start | bytes 393224 | tf_op jit(solution)/shard_map/ppermute | solution.py:332
  16.3 0.0 collective-permute-start.7
  16.3 1.3 collective-permute-start.8
  17.6 2.8 %collective-permute-start.1 = (bf16[2,4,16,512]{3,2,1,0:T(8,128)(2,1)S(1)}, bf16[2,4,16,512]{3,2,1,0:T(8,128)(2,1)S(1)}, u32[]{:S(2)}, u32[]{:S(2)}) collective-permute-start(bf16[2,4,16,512]{3,2,1,0:T(8,128)(2,1)S(1)} %pad_maximum_fusion), channel_id=1, source_target_pairs={{2,0},{3,1},{4,2},{5,3},{6,4},{7,5},{0,6},{1,7},{10,8},{11,9},{12,... | collective-permute-start | bytes 393224 | tf_op jit(solution)/shard_map/ppermute | solution.py:332
  20.4 0.8 collective-permute-start.2
  21.2 0.0 collective-permute-done.6
  21.2 1.3 collective-permute-start.3
  22.5 0.9 collective-permute-done.7
  23.4 1.0 collective-permute-done.8
  24.4 1.6 collective-permute-start.10
  26.0 1.7 collective-permute-start.9
  27.7 0.0 collective-permute-done.1
  27.8 0.0 collective-permute-done.2
  27.8 1.6 collective-permute-done.3
  29.4 3.0 %collective-permute-start.4 = (bf16[8,4,16,512]{3,2,1,0:T(8,128)(2,1)S(1)}, bf16[8,4,16,512]{3,2,1,0:T(8,128)(2,1)S(1)}, u32[]{:S(2)}, u32[]{:S(2)}) collective-permute-start(bf16[8,4,16,512]{3,2,1,0:T(8,128)(2,1)S(1)} %constant_dynamic-update-slice_fusion.rest_0_), channel_id=1, source_target_pairs={{8,0},{9,1},{10,2},{11,3},{12,4},{13,5},{14,6},{15,7},{16,8},{17,9... | collective-permute-start | bytes 1572872 | tf_op jit(solution)/shard_map/ppermute | solution.py:332
  32.4 0.1 collective-permute-start.5
  32.5 4.8 %row_project.2 = (bf16[8,512,256]{2,1,0:T(8,128)(2,1)}, bf16[8,256,512]{2,1,0:T(8,128)(2,1)}, bf16[8,512,256]{2,1,0:T(8,128)(2,1)}, f32[8,512,256]{2,1,0:T(8,128)}) custom-call(bf16[8,512,256]{2,1,0:T(8,128)(2,1)} %x_ref.7, f32[1,256]{1,0:T(1,128)} %bitcast.37, f32[1,256]{1,0:T(1,128)} %bitcast.39, bf16[256,256]{1,0:T(8,128)(2,1)} %q_w.4, ...), custom_call_target="tpu_custom_call" | custom-call | flops 1073741824 | bytes 6291456 | tf_op jit(solution)/shard_map/row_project/pallas_call | solution.py:140
  37.3 2.5 %collective-permute-done.10.rest_9_ = bf16[8,4,16,512]{3,2,1,0:T(8,128)(2,1)S(1)} collective-permute-done((bf16[8,4,16,512]{3,2,1,0:T(8,128)(2,1)S(1)}, bf16[8,4,16,512]{3,2,1,0:T(8,128)(2,1)S(1)}, u32[]{:S(2)}, u32[]{:S(2)}) %collective-permute-start.10) | collective-permute-done | bytes 524320 | tf_op jit(solution)/shard_map/ppermute | solution.py:332
  39.8 0.0 collective-permute-done.9.rest_6_
  39.8 2.8 %collective-permute-done.4.rest_1_ = bf16[8,4,16,512]{3,2,1,0:T(8,128)(2,1)S(1)} collective-permute-done((bf16[8,4,16,512]{3,2,1,0:T(8,128)(2,1)S(1)}, bf16[8,4,16,512]{3,2,1,0:T(8,128)(2,1)S(1)}, u32[]{:S(2)}, u32[]{:S(2)}) %collective-permute-start.4) | collective-permute-done | bytes 524320 | tf_op jit(solution)/shard_map/ppermute | solution.py:332
  42.6 3.4 %collective-permute-done.5.rest_4_ = bf16[8,4,16,512]{3,2,1,0:T(8,128)(2,1)S(1)} collective-permute-done((bf16[8,4,16,512]{3,2,1,0:T(8,128)(2,1)S(1)}, bf16[8,4,16,512]{3,2,1,0:T(8,128)(2,1)S(1)}, u32[]{:S(2)}, u32[]{:S(2)}) %collective-permute-start.5) | collective-permute-done | bytes 524320 | tf_op jit(solution)/shard_map/ppermute | solution.py:332
  46.0 0.4 collective-permute-start.11
  46.4 0.7 slice.29
  47.1 1.7 collective-permute-start.12
  48.8 0.8 slice.30
  49.6 0.0 collective-permute-start.13
  49.6 0.7 slice.31
  50.3 2.0 %collective-permute-start.14 = (bf16[4,4,16,512]{3,2,1,0:T(8,128)(2,1)}, bf16[4,4,16,512]{3,2,1,0:T(8,128)(2,1)S(1)}, u32[]{:S(2)}, u32[]{:S(2)}) collective-permute-start(bf16[4,4,16,512]{3,2,1,0:T(8,128)(2,1)} %slice.31), channel_id=1, source_target_pairs={{6,0},{7,1},{0,2},{1,3},{2,4},{3,5},{4,6},{5,7},{14,8},{15,9},{8,1... | collective-permute-start | bytes 786440 | tf_op jit(solution)/shard_map/ppermute | solution.py:332
  52.3 0.6 pad_add_fusion.here_ref
  53.0 4.8 %row_project.3 = (bf16[8,512,256]{2,1,0:T(8,128)(2,1)}, bf16[8,256,512]{2,1,0:T(8,128)(2,1)}, bf16[8,512,256]{2,1,0:T(8,128)(2,1)}, f32[8,512,256]{2,1,0:T(8,128)}) custom-call(bf16[8,512,256]{2,1,0:T(8,128)(2,1)} %x_ref.7, f32[1,256]{1,0:T(1,128)} %bitcast.38, ...), custom_call_target="tpu_custom_call", output_to_operand_aliasing={{0}: (8, {}), {1}: (9, {}), {2}: (10, {}), {3}: (11, {})} | custom-call | flops 1073741824 | bytes 6291456 | tf_op jit(solution)/shard_map/row_project/pallas_call | solution.py:140
  57.8 0.0 collective-permute-done.11.rest_2_
  57.8 0.0 collective-permute-done.12.rest_3_
  57.8 0.0 collective-permute-done.13.rest_7_
  57.9 0.2 collective-permute-done.14.rest_8_
  58.1 0.4 copy-done.6
  58.5 0.1 copy-done.7
  58.6 0.1 copy-done.8
  58.7 0.1 copy-done.9
  58.8 35.0 %row_attention.1 = bf16[32,8,16,256]{3,2,1,0:T(8,128)(2,1)} custom-call(s32[3]{0:T(128)} %pad_add_fusion.here_ref, bf16[8,512,256]{2,1,0:T(8,128)(2,1)} %get-tuple-element.31.q_ref, bf16[8,256,512]{2,1,0:T(8,128)(2,1)} %get-tuple-element.32.k_ref, bf16[8,512,256]{2,1,0:T(8,128)(2,1)} %get-tuple-element.33.v_ref, f32[8,512,256]{2,1,0:T(8,128)} %get-tuple-element.34.g_ref, ...), custom_call_target="tpu_custom_call" | custom-call | tf_op jit(solution)/shard_map/row_attention/pallas_call | solution.py:229
  93.8 34.3 %all_to_all.10 = bf16[32,8,16,256]{3,2,1,0:T(8,128)(2,1)} all-to-all(bf16[32,8,16,256]{3,2,1,0:T(8,128)(2,1)} %row_attention.1), channel_id=1, replica_groups=mesh['batch'=4,'dap'=32] {'dap'}, dimensions={0} | all-to-all | bytes 4194304 | tf_op jit(solution)/shard_map/all_to_all | solution.py:418
  128.1 25.0 %column_attention.1 = bf16[256,16,256]{2,1,0:T(8,128)(2,1)} custom-call(bf16[256,16,256]{2,1,0:T(8,128)(2,1)} %bitcast.33, f32[1,256]{1,0:T(1,128)} %bitcast.44, f32[1,256]{1,0:T(1,128)} %bitcast.45, bf16[256,256]{1,0:T(8,128)(2,1)} %q_w.5, bf16[256,256]{1,0:T(8,128)(2,1)} %k_w.5, bf16[256,256]{1,0:T(8,128)(2,1)} %v_w.5, bf16[256,256]{1,0:T(8,128)(2,1)} %g_w.5, ...), custom_call_target="tpu_custom_call" | custom-call | tf_op jit(solution)/shard_map/column_attention/pallas_call | solution.py:310
  153.0 31.1 %all_to_all.11 = bf16[32,8,16,256]{3,2,1,0:T(8,128)(2,1)S(1)} all-to-all(bf16[32,8,16,256]{3,2,1,0:T(8,128)(2,1)} %bitcast.34), channel_id=1, replica_groups=mesh['batch'=4,'dap'=32] {'dap'}, dimensions={0} | all-to-all | bytes 4194304 | tf_op jit(solution)/shard_map/all_to_all | solution.py:431
  184.2 1.5 copy.27
  (27 shorter events, 0.2 us)
Async XLA Ops:
  5.1 7.0 %collective-permute-start = (bf16[8,16,512]{2,1,0:T(8,128)(2,1)}, bf16[8,16,512]{2,1,0:T(8,128)(2,1)S(1)}, u32[]{:S(2)}, u32[]{:S(2)}) collective-permute-start(bf16[8,16,512]{2,1,0:T(8,128)(2,1)} %pair_bias.1), channel_id=1, source_target_pairs={{1,0},{0,1},{3,2},{2,3},{5,4},{4,5},{7,6},{6,7},{9,8},{8,9},{11,10... | collective-permute-start | bytes 393224 | tf_op jit(solution)/shard_map/ppermute | solution.py:332
  12.1 9.1 %collective-permute-start.6 = (bf16[2,4,16,512]{3,2,1,0:T(8,128)(2,1)S(1)}, bf16[2,4,16,512]{3,2,1,0:T(8,128)(2,1)S(1)}, u32[]{:S(2)}, u32[]{:S(2)}) collective-permute-start(bf16[2,4,16,512]{3,2,1,0:T(8,128)(2,1)S(1)} %pad_maximum_fusion.1), channel_id=1, source_target_pairs={{8,0},{9,1},{10,2},{11,3},{12,4},{13,5},{14,6},{15,7},{16,8},{17,9... | collective-permute-start | bytes 393224 | tf_op jit(solution)/shard_map/ppermute | solution.py:332
  16.3 7.1 %collective-permute-start.7 = (bf16[2,4,16,512]{3,2,1,0:T(8,128)(2,1)S(1)}, bf16[2,4,16,512]{3,2,1,0:T(8,128)(2,1)S(1)}, u32[]{:S(2)}, u32[]{:S(2)}) collective-permute-start(bf16[2,4,16,512]{3,2,1,0:T(8,128)(2,1)S(1)} %pad_maximum_fusion.1), channel_id=1, source_target_pairs={{16,0},{17,1},{18,2},{19,3},{20,4},{21,5},{22,6},{23,7},{24,8},{25... | collective-permute-start | bytes 393224 | tf_op jit(solution)/shard_map/ppermute | solution.py:332
  16.3 8.1 %collective-permute-start.8 = (bf16[2,4,16,512]{3,2,1,0:T(8,128)(2,1)S(1)}, bf16[2,4,16,512]{3,2,1,0:T(8,128)(2,1)S(1)}, u32[]{:S(2)}, u32[]{:S(2)}) collective-permute-start(bf16[2,4,16,512]{3,2,1,0:T(8,128)(2,1)S(1)} %pad_maximum_fusion.1), channel_id=1, source_target_pairs={{24,0},{25,1},{26,2},{27,3},{28,4},{29,5},{30,6},{31,7},{0,8},{1,9... | collective-permute-start | bytes 393224 | tf_op jit(solution)/shard_map/ppermute | solution.py:332
  17.6 10.2 %collective-permute-start.1 = (bf16[2,4,16,512]{3,2,1,0:T(8,128)(2,1)S(1)}, bf16[2,4,16,512]{3,2,1,0:T(8,128)(2,1)S(1)}, u32[]{:S(2)}, u32[]{:S(2)}) collective-permute-start(bf16[2,4,16,512]{3,2,1,0:T(8,128)(2,1)S(1)} %pad_maximum_fusion), channel_id=1, source_target_pairs={{2,0},{3,1},{4,2},{5,3},{6,4},{7,5},{0,6},{1,7},{10,8},{11,9},{12,... | collective-permute-start | bytes 393224 | tf_op jit(solution)/shard_map/ppermute | solution.py:332
  20.4 7.4 %collective-permute-start.2 = (bf16[2,4,16,512]{3,2,1,0:T(8,128)(2,1)S(1)}, bf16[2,4,16,512]{3,2,1,0:T(8,128)(2,1)S(1)}, u32[]{:S(2)}, u32[]{:S(2)}) collective-permute-start(bf16[2,4,16,512]{3,2,1,0:T(8,128)(2,1)S(1)} %pad_maximum_fusion), channel_id=1, source_target_pairs={{4,0},{5,1},{6,2},{7,3},{0,4},{1,5},{2,6},{3,7},{12,8},{13,9},{14,... | collective-permute-start | bytes 393224 | tf_op jit(solution)/shard_map/ppermute | solution.py:332
  21.2 8.1 %collective-permute-start.3 = (bf16[2,4,16,512]{3,2,1,0:T(8,128)(2,1)S(1)}, bf16[2,4,16,512]{3,2,1,0:T(8,128)(2,1)S(1)}, u32[]{:S(2)}, u32[]{:S(2)}) collective-permute-start(bf16[2,4,16,512]{3,2,1,0:T(8,128)(2,1)S(1)} %pad_maximum_fusion), channel_id=1, source_target_pairs={{6,0},{7,1},{0,2},{1,3},{2,4},{3,5},{4,6},{5,7},{14,8},{15,9},{8,1... | collective-permute-start | bytes 393224 | tf_op jit(solution)/shard_map/ppermute | solution.py:332
  24.4 12.9 %copy-start.4 = (bf16[8,4,16,512]{3,2,1,0:T(8,128)(2,1)}, bf16[8,4,16,512]{3,2,1,0:T(8,128)(2,1)S(1)}, u32[]{:S(2)}) copy-start(bf16[8,4,16,512]{3,2,1,0:T(8,128)(2,1)S(1)} %constant_dynamic-update-slice_fusion.5.rest_5_) | copy-start | bytes 1572868
  24.4 15.4 %collective-permute-start.10 = (bf16[8,4,16,512]{3,2,1,0:T(8,128)(2,1)S(1)}, bf16[8,4,16,512]{3,2,1,0:T(8,128)(2,1)S(1)}, u32[]{:S(2)}, u32[]{:S(2)}) collective-permute-start(bf16[8,4,16,512]{3,2,1,0:T(8,128)(2,1)S(1)} %constant_dynamic-update-slice_fusion.5.rest_5_), channel_id=1, source_target_pairs={{6,0},{7,1},{0,2},{1,3},{2,4},{3,5},{4,6},{5,7},{14,8},{15,9},{8,1... | collective-permute-start | bytes 1572872 | tf_op jit(solution)/shard_map/ppermute | solution.py:332
  26.0 13.8 %collective-permute-start.9 = (bf16[8,4,16,512]{3,2,1,0:T(8,128)(2,1)S(1)}, bf16[8,4,16,512]{3,2,1,0:T(8,128)(2,1)S(1)}, u32[]{:S(2)}, u32[]{:S(2)}) collective-permute-start(bf16[8,4,16,512]{3,2,1,0:T(8,128)(2,1)S(1)} %constant_dynamic-update-slice_fusion.5.rest_5_), channel_id=1, source_target_pairs={{2,0},{3,1},{4,2},{5,3},{6,4},{7,5},{0,6},{1,7},{10,8},{11,9},{12,... | collective-permute-start | bytes 1572872 | tf_op jit(solution)/shard_map/ppermute | solution.py:332
  29.4 16.6 %copy-start.5 = (bf16[8,4,16,512]{3,2,1,0:T(8,128)(2,1)}, bf16[8,4,16,512]{3,2,1,0:T(8,128)(2,1)S(1)}, u32[]{:S(2)}) copy-start(bf16[8,4,16,512]{3,2,1,0:T(8,128)(2,1)S(1)} %constant_dynamic-update-slice_fusion.rest_0_) | copy-start | bytes 1572868
  29.4 13.2 %collective-permute-start.4 = (bf16[8,4,16,512]{3,2,1,0:T(8,128)(2,1)S(1)}, bf16[8,4,16,512]{3,2,1,0:T(8,128)(2,1)S(1)}, u32[]{:S(2)}, u32[]{:S(2)}) collective-permute-start(bf16[8,4,16,512]{3,2,1,0:T(8,128)(2,1)S(1)} %constant_dynamic-update-slice_fusion.rest_0_), channel_id=1, source_target_pairs={{8,0},{9,1},{10,2},{11,3},{12,4},{13,5},{14,6},{15,7},{16,8},{17,9... | collective-permute-start | bytes 1572872 | tf_op jit(solution)/shard_map/ppermute | solution.py:332
  32.4 13.5 %collective-permute-start.5 = (bf16[8,4,16,512]{3,2,1,0:T(8,128)(2,1)S(1)}, bf16[8,4,16,512]{3,2,1,0:T(8,128)(2,1)S(1)}, u32[]{:S(2)}, u32[]{:S(2)}) collective-permute-start(bf16[8,4,16,512]{3,2,1,0:T(8,128)(2,1)S(1)} %constant_dynamic-update-slice_fusion.rest_0_), channel_id=1, source_target_pairs={{24,0},{25,1},{26,2},{27,3},{28,4},{29,5},{30,6},{31,7},{0,8},{1,9... | collective-permute-start | bytes 1572872 | tf_op jit(solution)/shard_map/ppermute | solution.py:332
  39.8 18.0 %copy-start = (bf16[8,4,16,512]{3,2,1,0:T(8,128)(2,1)}, bf16[8,4,16,512]{3,2,1,0:T(8,128)(2,1)S(1)}, u32[]{:S(2)}) copy-start(bf16[8,4,16,512]{3,2,1,0:T(8,128)(2,1)S(1)} %collective-permute-done.10.rest_9_) | copy-start | bytes 1572868
  39.8 18.0 %copy-start.1 = (bf16[8,4,16,512]{3,2,1,0:T(8,128)(2,1)}, bf16[8,4,16,512]{3,2,1,0:T(8,128)(2,1)S(1)}, u32[]{:S(2)}) copy-start(bf16[8,4,16,512]{3,2,1,0:T(8,128)(2,1)S(1)} %collective-permute-done.9.rest_6_) | copy-start | bytes 1572868
  42.6 15.2 %copy-start.2 = (bf16[8,4,16,512]{3,2,1,0:T(8,128)(2,1)}, bf16[8,4,16,512]{3,2,1,0:T(8,128)(2,1)S(1)}, u32[]{:S(2)}) copy-start(bf16[8,4,16,512]{3,2,1,0:T(8,128)(2,1)S(1)} %collective-permute-done.4.rest_1_) | copy-start | bytes 1572868
  46.0 11.8 %copy-start.3 = (bf16[8,4,16,512]{3,2,1,0:T(8,128)(2,1)}, bf16[8,4,16,512]{3,2,1,0:T(8,128)(2,1)S(1)}, u32[]{:S(2)}) copy-start(bf16[8,4,16,512]{3,2,1,0:T(8,128)(2,1)S(1)} %collective-permute-done.5.rest_4_) | copy-start | bytes 1572868
  46.0 11.8 %collective-permute-start.11 = (bf16[4,4,16,512]{3,2,1,0:T(8,128)(2,1)S(1)}, bf16[4,4,16,512]{3,2,1,0:T(8,128)(2,1)S(1)}, u32[]{:S(2)}, u32[]{:S(2)}) collective-permute-start(bf16[4,4,16,512]{3,2,1,0:T(8,128)(2,1)S(1)} %slice.28), channel_id=1, source_target_pairs={{8,0},{9,1},{10,2},{11,3},{12,4},{13,5},{14,6},{15,7},{16,8},{17,9... | collective-permute-start | bytes 786440 | tf_op jit(solution)/shard_map/ppermute | solution.py:332
  47.1 10.7 %collective-permute-start.12 = (bf16[4,4,16,512]{3,2,1,0:T(8,128)(2,1)}, bf16[4,4,16,512]{3,2,1,0:T(8,128)(2,1)S(1)}, u32[]{:S(2)}, u32[]{:S(2)}) collective-permute-start(bf16[4,4,16,512]{3,2,1,0:T(8,128)(2,1)} %slice.29), channel_id=1, source_target_pairs={{24,0},{25,1},{26,2},{27,3},{28,4},{29,5},{30,6},{31,7},{0,8},{1,9... | collective-permute-start | bytes 786440 | tf_op jit(solution)/shard_map/ppermute | solution.py:332
  49.6 8.3 %collective-permute-start.13 = (bf16[4,4,16,512]{3,2,1,0:T(8,128)(2,1)}, bf16[4,4,16,512]{3,2,1,0:T(8,128)(2,1)S(1)}, u32[]{:S(2)}, u32[]{:S(2)}) collective-permute-start(bf16[4,4,16,512]{3,2,1,0:T(8,128)(2,1)} %slice.30), channel_id=1, source_target_pairs={{2,0},{3,1},{4,2},{5,3},{6,4},{7,5},{0,6},{1,7},{10,8},{11,9},{12,... | collective-permute-start | bytes 786440 | tf_op jit(solution)/shard_map/ppermute | solution.py:332
  50.3 7.8 %collective-permute-start.14 = (bf16[4,4,16,512]{3,2,1,0:T(8,128)(2,1)}, bf16[4,4,16,512]{3,2,1,0:T(8,128)(2,1)S(1)}, u32[]{:S(2)}, u32[]{:S(2)}) collective-permute-start(bf16[4,4,16,512]{3,2,1,0:T(8,128)(2,1)} %slice.31), channel_id=1, source_target_pairs={{6,0},{7,1},{0,2},{1,3},{2,4},{3,5},{4,6},{5,7},{14,8},{15,9},{8,1... | collective-permute-start | bytes 786440 | tf_op jit(solution)/shard_map/ppermute | solution.py:332
  57.8 0.7 copy-start.6
  57.8 0.8 copy-start.7
  57.9 0.8 copy-start.8
  58.1 0.7 copy-start.9

commit v2 on v1

v2 whole, which is shorter than its diff:
```python
import functools

import jax
import jax.numpy as jnp
from jax import lax
from jax.experimental import pallas as pl
from jax.experimental.pallas import tpu as pltpu
from jax.sharding import PartitionSpec as P

H = 8
HEAD = 32
C = 256
LANES = 128
GROUP = LANES // HEAD
EPS = 1e-05
VMEM = 40 * 1024 * 1024
NZ, NX, NY = 4, 4, 2
DAP = NZ * NX * NY
NT = (((1,), (1,)), ((), ()))


def norm(x, gain, bias):
    center = jnp.mean(x, axis=-1, keepdims=True)
    moved = x - center
    spread = jnp.mean(moved * moved, axis=-1, keepdims=True)
    return (moved * lax.rsqrt(spread + EPS) * gain + bias).astype(jnp.bfloat16)


def lanes_of(part):
    return slice(part * LANES, (part + 1) * LANES)


def dot(a, b):
    return jnp.dot(a, b, preferred_element_type=jnp.float32)


def softmax_rounded(scores):
    top = jnp.max(scores, axis=-1, keepdims=True)
    e = jnp.exp(scores - top)
    total = jnp.sum(e, axis=-1, keepdims=True)
    return (e * (1.0 / total)).astype(jnp.bfloat16)


def head_of_lane():
    return lax.broadcasted_iota(jnp.int32, (1, LANES), 1) // HEAD


def stacked(q):
    head = head_of_lane()
    masks = [(head == i).astype(jnp.float32).astype(jnp.bfloat16) for i in range(GROUP)]
    return jnp.concatenate([q * mask for mask in masks], axis=0)


def own_lanes(mixed):
    head = head_of_lane()
    rows = mixed.shape[0] // GROUP
    total = mixed[:rows]
    for i in range(1, GROUP):
        total = jnp.where(head == i, mixed[i * rows : (i + 1) * rows], total)
    return total


def pipelined(count, score, soften, average):
    scores, weights = {0: score(0)}, {}
    for n in range(count + 1):
        if n + 1 < count:
            scores[n + 1] = score(n + 1)
        if n < count:
            weights[n] = soften(n, scores.pop(n))
        if n >= 1:
            average(n - 1, weights.pop(n - 1))


def project(normed, q_w, k_w, v_w, g_w, g_b):
    q = (dot(normed, q_w[...]) * HEAD ** (-0.5)).astype(jnp.bfloat16)
    k_t = dot(normed, k_w[...]).T.astype(jnp.bfloat16)
    v = dot(normed, v_w[...]).astype(jnp.bfloat16)
    g = jax.nn.sigmoid(dot(normed, g_w[...]) + g_b[...])
    return q, k_t, v, g


def pair_kernel(x_ref, gain_ref, w_ref, out_ref, held):
    step = pl.program_id(0)
    rows = x_ref.shape[0]
    heads, count, _ = out_ref.shape
    for i in range(rows):
        normed = norm(x_ref[i].astype(jnp.float32), gain_ref[...], 0.0)
        bias = lax.dot_general(w_ref[...], normed, NT, preferred_element_type=jnp.float32)
        for part in range(held.shape[0]):
            held[part, pl.ds(step * rows + i, H, stride=count), :] = bias[:, lanes_of(part)]

    @pl.when(step == pl.num_programs(0) - 1)
    def _():
        for part in range(held.shape[0]):
            out_ref[:, :, lanes_of(part)] = (
                held[part].astype(jnp.bfloat16).reshape(heads, count, LANES)
            )


def pair_bias(pair_state, gain, weight):
    count, res, cz = pair_state.shape
    rows = 4
    return pl.pallas_call(
        pair_kernel,
        grid=(count // rows,),
        out_shape=jax.ShapeDtypeStruct((H, count, res), jnp.bfloat16),
        in_specs=[
            pl.BlockSpec((rows, res, cz), lambda i: (i, 0, 0)),
            pl.BlockSpec((1, cz), lambda i: (0, 0)),
            pl.BlockSpec((H, cz), lambda i: (0, 0)),
        ],
        out_specs=pl.BlockSpec((H, count, res), lambda i: (0, 0, 0)),
        scratch_shapes=[pltpu.VMEM((res // LANES, H * count, LANES), jnp.float32)],
        compiler_params=pltpu.CompilerParams(vmem_limit_bytes=VMEM),
        name="pair_bias",
    )(pair_state, gain.reshape(1, cz), weight.T)


def project_kernel(x_ref, gain, bias, q_w, k_w, v_w, g_w, g_b, q_ref, k_ref, v_ref, g_ref):
    count, res, width = x_ref.shape
    x = x_ref[...].reshape(count * res, width).astype(jnp.float32)
    normed = norm(x, gain[...], bias[...])
    q, k_t, v, g = project(normed, q_w, k_w, v_w, g_w, g_b)
    for out_ref, value in ((q_ref, q), (v_ref, v), (g_ref, g)):
        out_ref[...] = value.reshape(count, res, width)
    for n in range(count):
        k_ref[n] = k_t[:, n * res : (n + 1) * res]


def row_project(x, gain, bias, q_w, k_w, v_w, g_w, g_b):
    seqs, res, width = x.shape
    count = 2
    block = pl.BlockSpec((count, res, width), lambda s: (s, 0, 0))
    turned = pl.BlockSpec((count, width, res), lambda s: (s, 0, 0))
    vector = pl.BlockSpec((1, width), lambda s: (0, 0))
    weight = pl.BlockSpec((width, width), lambda s: (0, 0))
    shape = jax.ShapeDtypeStruct
    return pl.pallas_call(
        project_kernel,
        grid=(seqs // count,),
        out_shape=[
            shape((seqs, res, width), jnp.bfloat16),
            shape((seqs, width, res), jnp.bfloat16),
            shape((seqs, res, width), jnp.bfloat16),
            shape((seqs, res, width), jnp.float32),
        ],
        in_specs=[block, vector, vector] + [weight] * 4 + [vector],
        out_specs=[block, turned, block, block],
        compiler_params=pltpu.CompilerParams(vmem_limit_bytes=VMEM),
        cost_estimate=pl.CostEstimate(
            flops=2 * seqs * res * width * width * 4,
            bytes_accessed=x.size * 12,
            transcendentals=x.size * 2,
        ),
        name="row_project",
    )(x, gain.reshape(1, -1), bias.reshape(1, -1), q_w, k_w, v_w, g_w, g_b.reshape(1, -1))


def row_kernel(here_ref, q_ref, k_ref, v_ref, g_ref, x_ref, bias_ref, o_w, o_b, *rest):
    out_ref, held, weights = rest[-3:]
    seqs, tile, width = q_ref.shape
    own = out_ref.shape[2]
    groups = H // GROUP

    def place(n):
        return n // groups, n % groups, lanes_of(n % groups)

    def score(n):
        seq, _, lanes = place(n)
        held[n % 2] = dot(stacked(q_ref[seq, :, lanes]), k_ref[seq, lanes, :])

    def slot(x, y):
        return lax.rem(x - here_ref[1] + NX, NX) * NY + lax.rem(y - here_ref[2] + NY, NY)

    def soften(n, _):
        _, group, _ = place(n)
        for i in range(GROUP):
            for x in range(NX):
                rows = slice(i * tile + x * NY * own, i * tile + (x + 1) * NY * own)
                bias = [bias_ref[slot(x, y), group * GROUP + i] for y in range(NY)]
                bias = jnp.concatenate(bias, axis=0).astype(jnp.float32)
                weights[n % 2, rows] = softmax_rounded(held[n % 2, rows] + bias)

    gated = {}

    def average(n, _):
        seq, group, lanes = place(n)
        mixed = own_lanes(dot(weights[n % 2], v_ref[seq, :, lanes]))
        gated[group] = (mixed * g_ref[seq, :, lanes]).astype(jnp.bfloat16)
        if len(gated) == groups:
            both = jnp.concatenate([gated.pop(part) for part in range(groups)], axis=1)
            after = x_ref[seq].astype(jnp.float32) + (dot(both, o_w[...]) + o_b[...])
            out_ref[:, seq] = after.astype(jnp.bfloat16).reshape(out_ref.shape[0], own, width)

    pipelined(seqs * groups, score, soften, average)


def row_attention(plane, here, q, k, v, g, x, bias, o_w, o_b, held):
    seqs, res, width = x.shape
    own = res // DAP
    tile = res // NZ
    once = 4

    def which(here):
        return lax.rem(here[0] + plane, NZ)

    queries = pl.BlockSpec((once, tile, width), lambda s, here: (s, which(here), 0))
    args = [q, k, v, g, x, bias, o_w, o_b.reshape(1, -1), *held]
    return pl.pallas_call(
        row_kernel,
        out_shape=jax.ShapeDtypeStruct((DAP, seqs, own, width), jnp.bfloat16),
        grid_spec=pltpu.PrefetchScalarGridSpec(
            num_scalar_prefetch=1,
            grid=(seqs // once,),
            in_specs=[
                queries,
                pl.BlockSpec((once, width, res), lambda s, here: (s, 0, 0)),
                pl.BlockSpec((once, res, width), lambda s, here: (s, 0, 0)),
                queries,
                queries,
                pl.BlockSpec(bias.shape, lambda s, here: (0, 0, 0, 0)),
                pl.BlockSpec((width, width), lambda s, here: (0, 0)),
                pl.BlockSpec((1, width), lambda s, here: (0, 0)),
            ]
            + [pl.BlockSpec(memory_space=pl.ANY)] * len(held),
            out_specs=pl.BlockSpec(
                (DAP // NZ, once, own, width), lambda s, here: (which(here), s, 0, 0)
            ),
            scratch_shapes=[
                pltpu.VMEM((2, GROUP * tile, res), jnp.float32),
                pltpu.VMEM((2, GROUP * tile, res), jnp.bfloat16),
            ],
        ),
        input_output_aliases={len(args): 0} if held else {},
        compiler_params=pltpu.CompilerParams(vmem_limit_bytes=VMEM),
        cost_estimate=pl.CostEstimate(
            flops=seqs * H * tile * res * 256 * 16,
            bytes_accessed=8 * 1024 * 1024,
            transcendentals=seqs * H * tile * res,
        ),
        name="row_attention",
    )(here, *args)


def column_kernel(at_once, x_ref, gain, bias, q_w, k_w, v_w, g_w, g_b, o_w, o_b, out_ref, held, scores, weights):
    step = pl.program_id(0)
    seqs, items, width = x_ref.shape
    parts = width // LANES

    @pl.when(step == 0)
    def _():
        for part in range(parts):
            held[part] = (
                x_ref[:, :, lanes_of(part)].astype(jnp.float32).reshape(seqs * items, LANES)
            )

    mine = [pl.ds(step * at_once + n, seqs, stride=items) for n in range(at_once)]
    x = jnp.concatenate(
        [jnp.concatenate([held[part, rows, :] for rows in mine], axis=0) for part in range(parts)], axis=1
    )
    normed = norm(x, gain[...], bias[...])
    q, k_t, v, g = project(normed, q_w, k_w, v_w, g_w, g_b)
    gated = {}

    def place(n):
        return slice(n // parts * seqs, (n // parts + 1) * seqs), lanes_of(n % parts)

    def score(n):
        rows, lanes = place(n)
        scores[n % 2] = dot(stacked(q[rows, lanes]), k_t[lanes, rows])

    def soften(n, _):
        for low in range(0, GROUP * seqs, 64):
            weights[n % 2, low : low + 64] = softmax_rounded(scores[n % 2, low : low + 64])

    def average(n, _):
        rows, lanes = place(n)
        mixed = own_lanes(dot(weights[n % 2], v[rows, lanes]))
        gated[n] = (mixed * g[rows, lanes]).astype(jnp.bfloat16)

    pipelined(at_once * parts, score, soften, average)
    gated = [
        jnp.concatenate([gated[n * parts + part] for part in range(parts)], axis=1)
        for n in range(at_once)
    ]
    after = x + (dot(jnp.concatenate(gated, axis=0), o_w[...]) + o_b[...])
    for n, rows in enumerate(mine):
        for part in range(parts):
            held[part, rows, :] = after[n * seqs : (n + 1) * seqs, lanes_of(part)]

    @pl.when(step == pl.num_programs(0) - 1)
    def _():
        for part in range(parts):
            out_ref[:, :, lanes_of(part)] = (
                held[part].astype(jnp.bfloat16).reshape(seqs, items, LANES)
            )


def column_attention(x, gain, bias, q_w, k_w, v_w, g_w, g_b, o_w, o_b):
    seqs, items, width = x.shape
    at_once = 4
    whole = pl.BlockSpec(x.shape, lambda r: (0, 0, 0))
    vector = pl.BlockSpec((1, width), lambda r: (0, 0))
    weight = pl.BlockSpec((width, width), lambda r: (0, 0))
    return pl.pallas_call(
        functools.partial(column_kernel, at_once),
        grid=(items // at_once,),
        out_shape=jax.ShapeDtypeStruct(x.shape, jnp.bfloat16),
        in_specs=[whole, vector, vector] + [weight] * 4 + [vector, weight, vector],
        out_specs=whole,
        scratch_shapes=[
            pltpu.VMEM((width // LANES, seqs * items, LANES), jnp.float32),
            pltpu.VMEM((2, GROUP * seqs, seqs), jnp.float32),
            pltpu.VMEM((2, GROUP * seqs, seqs), jnp.bfloat16),
        ],
        compiler_params=pltpu.CompilerParams(vmem_limit_bytes=VMEM),
        name="column_attention",
    )(
        x, gain.reshape(1, -1), bias.reshape(1, -1), q_w, k_w, v_w, g_w, g_b.reshape(1, -1),
        o_w, o_b.reshape(1, -1),
    )


def fetch(value, z=0, x=0, y=0):
    pairs = []
    for dz in range(NZ):
        for dx in range(NX):
            for dy in range(NY):
                src = ((dz + z) % NZ * NX + (dx + x) % NX) * NY + (dy + y) % NY
                pairs.append((src, (dz * NX + dx) * NY + dy))
    return lax.ppermute(value, "dap", pairs)


def plane_bias(local):
    near = {(x, y): fetch(local, x=x, y=y) for y in range(NY) for x in (1, 3, 2, 0) if x or y}
    near[0, 0] = local
    return jnp.stack([near[x, y] for x in range(NX) for y in range(NY)])


def per_device(
    alignment,
    pair_state,
    row_norm_gain,
    row_norm_bias,
    pair_norm_gain,
    pair_weight,
    row_query,
    row_key,
    row_value,
    row_gate,
    row_gate_bias,
    row_output,
    row_output_bias,
    column_norm_gain,
    column_norm_bias,
    column_query,
    column_key,
    column_value,
    column_gate,
    column_gate_bias,
    column_output,
    column_output_bias,
):
    seqs, res, width = alignment.shape
    own = res // DAP
    me = lax.axis_index("dap")
    here = jnp.stack([me // (NX * NY), me // NY % NX, me % NY]).astype(jnp.int32)
    bias = plane_bias(pair_bias(pair_state, pair_norm_gain, pair_weight))
    bias, inputs = lax.optimization_barrier((bias, alignment))
    ahead, behind = fetch(bias, z=1), fetch(bias, z=3)
    projected = row_project(
        inputs, row_norm_gain, row_norm_bias, row_query, row_key, row_value, row_gate, row_gate_bias
    )

    def attend(plane, bias, *held):
        return row_attention(
            plane, here, *projected, alignment, bias, row_output, row_output_bias, held
        )

    after = attend(0, bias)
    ahead, behind, after = lax.optimization_barrier((ahead, behind, after))
    far = fetch(ahead, z=1)
    after = attend(3, behind, attend(1, ahead, after))
    after = attend(2, far, after)
    received = lax.all_to_all(after, "dap", split_axis=0, concat_axis=0, tiled=True)
    columns = column_attention(
        received.reshape(DAP * seqs, own, width),
        column_norm_gain,
        column_norm_bias,
        column_query,
        column_key,
        column_value,
        column_gate,
        column_gate_bias,
        column_output,
        column_output_bias,
    )
    back = lax.all_to_all(
        columns.reshape(DAP, seqs, own, width), "dap", split_axis=0, concat_axis=0, tiled=True
    )
    return back.transpose(1, 0, 2, 3).reshape(alignment.shape)


def solution(mesh):
    split = P(("batch", "dap"), None, None)
    return jax.shard_map(
        per_device,
        mesh=mesh,
        in_specs=(split, split) + (P(),) * 20,
        out_specs=split,
        check_vma=False,
    )
```

time: 186 us -> 179 us (0.962)
  Pallas kernels: 74.6 us -> 62.6 us
  local copies, waits for them, and re-layouts: 6.34 us -> 12.9 us
  starting transfers between devices: 24.1 us -> 18.6 us
  blocking collectives: 65.4 us -> 68 us
    unnamed x26 -> x53, local copies, waits for them, and re-layouts: 1.68 us -> 11.4 us
    ppermute x15 -> x10, starting transfers between devices: 24.1 us -> 18.6 us  [fetch(): return lax.ppermute(value, 'dap', pairs)]
    pallas_call x1, Pallas kernels: 25 us -> 19.4 us  [column_attention(): pl.pallas_call(functools.partial(column_kernel, at_once), grid=(items //...]
    pallas_call x3 -> x5, Pallas kernels: 44.6 us -> 40 us  [the longest x4 35.5 us: row_attention(): pl.pallas_call(row_kernel, out_shape=jax.ShapeDtypeStruct((DAP, seqs, own...]
    slice x4 -> x0, local copies, waits for them, and re-layouts: 2.23 us -> none  [the longest x2 1.46 us: relay(): behind[half:]]
    all_to_all x1, blocking collectives: 34.3 us -> 36.3 us  [per_device(): lax.all_to_all(after, 'dap', split_axis=0, concat_axis=0, tiled=True)]
    pallas_call x1, Pallas kernels: 5.12 us -> 3.15 us  [pair_bias(): pl.pallas_call(pair_kernel, grid=(count // rows,), out_shape=jax.ShapeDty...]
    ppermute x15 -> x10, waiting for transfers between devices: 14.3 us -> 16 us  [fetch(): return lax.ppermute(value, 'dap', pairs)]
  transfers between devices with their start and end apart: 15 -> 10, of which waited for: 8 -> 7; matrix products, arithmetic and copies ran while one was open for 3% -> 3% of each run, Pallas kernels for 5% -> 17%
where the time goes in v2:
time: 179 us; the launch traced here: 178 us
  blocking collectives  68 us (38%)
  Pallas kernels  62.6 us (35%)
  starting transfers between devices  18.6 us (10%)
  waiting for transfers between devices  16 us (9%)
  local copies, waits for them, and re-layouts  12.9 us (7%)
    all_to_all x1, blocking collectives, per_device(): lax.all_to_all(after, 'dap', split_axis=0, concat_axis=0, tiled=True)  36.3 us
    pallas_call x4, Pallas kernels, row_attention(): pl.pallas_call(row_kernel, out_shape=jax.ShapeDtypeStruct((DAP, seqs, own...  35.5 us
    all_to_all x1, blocking collectives, per_device(): lax.all_to_all(columns.reshape(DAP, seqs, own, width), 'dap', split_axis=...  31.7 us
    pallas_call x1, Pallas kernels, column_attention(): pl.pallas_call(functools.partial(column_kernel, at_once), grid=(items //...  19.4 us
    ppermute x10, starting transfers between devices, fetch(): return lax.ppermute(value, 'dap', pairs)  18.6 us
    ppermute x10, waiting for transfers between devices, fetch(): return lax.ppermute(value, 'dap', pairs)  16 us
    unnamed x53, local copies, waits for them, and re-layouts  11.4 us
    pallas_call x1, Pallas kernels, row_project(): pl.pallas_call(project_kernel, grid=(seqs // count,), out_shape=[shape((s...  4.56 us
  transfers between devices with their start and end apart: 10, of which 7 were waited for; matrix products, arithmetic and copies ran while one was open for 3% of the time, Pallas kernels for 17%

profile of v2, /device:TPU:0, one launch (start us, length us, event | category | flops | bytes accessed | tf_op | source)
XLA Modules:
  0.0 178.5 jit_solution(16445678537463488503)
XLA Ops:
  0.0 1.6 copy-done
  1.6 0.7 copy-done.6
  2.3 0.7 copy-done.11
  3.0 3.2 %pair_bias.1 = bf16[8,16,512]{2,1,0:T(8,128)(2,1)S(1)} custom-call(bf16[16,512,128]{2,1,0:T(8,128)(2,1)S(1)} %copy-done, f32[1,128]{1,0:T(1,128)S(1)} %bitcast.40, bf16[8,128]{1,0:T(8,128)(2,1)S(1)} %bitcast.35), custom_call_target="tpu_custom_call" | custom-call | tf_op jit(solution)/shard_map/pair_bias/pallas_call | solution.py:103
  6.1 3.4 %collective-permute-start = (bf16[8,16,512]{2,1,0:T(8,128)(2,1)S(1)}, bf16[8,16,512]{2,1,0:T(8,128)(2,1)}, u32[]{:S(2)}, u32[]{:S(2)}) collective-permute-start(bf16[8,16,512]{2,1,0:T(8,128)(2,1)S(1)} %pair_bias.1), channel_id=1, source_target_pairs={{1,0},{0,1},{3,2},{2,3},{5,4},{4,5},{7,6},{6,7},{9,8},{8,9},{11,10... | collective-permute-start | bytes 393224 | tf_op jit(solution)/shard_map/ppermute | solution.py:331
  9.5 2.8 %collective-permute-start.1 = (bf16[8,16,512]{2,1,0:T(8,128)(2,1)S(1)}, bf16[8,16,512]{2,1,0:T(8,128)(2,1)}, u32[]{:S(2)}, u32[]{:S(2)}) collective-permute-start(bf16[8,16,512]{2,1,0:T(8,128)(2,1)S(1)} %pair_bias.1), channel_id=1, source_target_pairs={{2,0},{3,1},{4,2},{5,3},{6,4},{7,5},{0,6},{1,7},{10,8},{11,9},{12,... | collective-permute-start | bytes 393224 | tf_op jit(solution)/shard_map/ppermute | solution.py:331
  12.2 0.6 collective-permute-start.2
  12.8 0.4 collective-permute-start.3
  13.3 5.7 %collective-permute-start.4 = (bf16[8,16,512]{2,1,0:T(8,128)(2,1)S(1)}, bf16[8,16,512]{2,1,0:T(8,128)(2,1)}, u32[]{:S(2)}, u32[]{:S(2)}) collective-permute-start(bf16[8,16,512]{2,1,0:T(8,128)(2,1)S(1)} %pair_bias.1), channel_id=1, source_target_pairs={{5,0},{4,1},{7,2},{6,3},{1,4},{0,5},{3,6},{2,7},{13,8},{12,9},{15,... | collective-permute-start | bytes 393224 | tf_op jit(solution)/shard_map/ppermute | solution.py:331
  19.1 0.1 pad_add_fusion.here_ref
  19.1 1.2 collective-permute-start.5
  20.4 0.9 bitcast_dynamic-update-slice_fusion.6
  21.3 0.1 collective-permute-start.6
  21.4 0.9 bitcast_dynamic-update-slice_fusion.5
  22.3 1.1 collective-permute-done.2
  23.4 0.9 bitcast_dynamic-update-slice_fusion.4
  24.3 0.9 bitcast_dynamic-update-slice_fusion.3
  25.2 0.5 collective-permute-done.4
  25.8 0.9 bitcast_dynamic-update-slice_fusion.2
  26.7 0.1 collective-permute-done.5
  26.8 3.1 %collective-permute-done.6 = bf16[8,16,512]{2,1,0:T(8,128)(2,1)S(1)} collective-permute-done((bf16[8,16,512]{2,1,0:T(8,128)(2,1)S(1)}, bf16[8,16,512]{2,1,0:T(8,128)(2,1)S(1)}, u32[]{:S(2)}, u32[]{:S(2)}) %collective-permute-start.6) | collective-permute-done | bytes 131104 | tf_op jit(solution)/shard_map/ppermute | solution.py:331
  29.9 4.1 %collective-permute-start.7 = (bf16[8,8,16,512]{3,2,1,0:T(8,128)(2,1)S(1)}, bf16[8,8,16,512]{3,2,1,0:T(8,128)(2,1)S(1)}, u32[]{:S(2)}, u32[]{:S(2)}) collective-permute-start(bf16[8,8,16,512]{3,2,1,0:T(8,128)(2,1)S(1)} %bitcast_dynamic-update-slice_fusion.bias_ref), channel_id=1, source_target_pairs={{8,0},{9,1},{10,2},{11,3},{12,4},{13,5},{14,6},{15,7},{16,8},{17,9... | collective-permute-start | bytes 3145736 | tf_op jit(solution)/shard_map/ppermute | solution.py:331
  34.1 0.0 copy-start.15
  34.1 0.9 copy-done.15
  35.0 0.9 copy-done.16
  35.9 4.6 %row_project.1 = (bf16[8,512,256]{2,1,0:T(8,128)(2,1)S(1)}, bf16[8,256,512]{2,1,0:T(8,128)(2,1)S(1)}, bf16[8,512,256]{2,1,0:T(8,128)(2,1)S(1)}, f32[8,512,256]{2,1,0:T(8,128)S(1)}) custom-call(bf16[8,512,256]{2,1,0:T(8,128)(2,1)S(1)} %copy-done.12, f32[1,256]{1,0:T(1,128)S(1)} %bitcast.41, f32[1,256]{1,0:T(1,128)S(1)} %bitcast.42, ...), custom_call_target="tpu_custom_call" | custom-call | flops 2147483648 | bytes 12582912 | tf_op jit(solution)/shard_map/row_project/pallas_call | solution.py:138
  40.5 1.9 %copy-done.22 = f32[8,512,256]{2,1,0:T(8,128)} copy-done((f32[8,512,256]{2,1,0:T(8,128)}, f32[8,512,256]{2,1,0:T(8,128)S(1)}, u32[]{:S(2)}) %copy-start.22) | copy-done | bytes 4194328
  42.4 8.9 %row_attention.4.rest_0_ = bf16[32,8,16,256]{3,2,1,0:T(8,128)(2,1)S(1)} custom-call(s32[3]{0:T(128)S(1)} %pad_add_fusion.here_ref, bf16[8,512,256]{2,1,0:T(8,128)(2,1)S(1)} %get-tuple-element.15.q_ref, bf16[8,256,512]{2,1,0:T(8,128)(2,1)S(1)} %get-tuple-element.16.k_ref, bf16[8,512,256]{2,1,0:T(8,128)(2,1)S(1)} %get-tuple-element.17.v_ref, ...), custom_call_target="tpu_custom_call" | custom-call | flops 17179869184 | bytes 8388608 | tf_op jit(solution)/shard_map/row_attention/pallas_call | solution.py:209
  51.3 3.6 %collective-permute-done.7.bias_ref = bf16[8,8,16,512]{3,2,1,0:T(8,128)(2,1)S(1)} collective-permute-done((bf16[8,8,16,512]{3,2,1,0:T(8,128)(2,1)S(1)}, bf16[8,8,16,512]{3,2,1,0:T(8,128)(2,1)S(1)}, u32[]{:S(2)}, u32[]{:S(2)}) %collective-permute-start.7) | collective-permute-done | bytes 1048608 | tf_op jit(solution)/shard_map/ppermute | solution.py:331
  54.9 3.4 %collective-permute-done.8.bias_ref = bf16[8,8,16,512]{3,2,1,0:T(8,128)(2,1)S(1)} collective-permute-done((bf16[8,8,16,512]{3,2,1,0:T(8,128)(2,1)S(1)}, bf16[8,8,16,512]{3,2,1,0:T(8,128)(2,1)S(1)}, u32[]{:S(2)}, u32[]{:S(2)}) %collective-permute-start.8) | collective-permute-done | bytes 1048608 | tf_op jit(solution)/shard_map/ppermute | solution.py:331
  58.3 0.3 collective-permute-start.9
  58.6 8.9 %row_attention.5.rest_0_ = bf16[32,8,16,256]{3,2,1,0:T(8,128)(2,1)S(1)} custom-call(s32[3]{0:T(128)S(1)} %pad_add_fusion.here_ref, bf16[8,512,256]{2,1,0:T(8,128)(2,1)S(1)} %get-tuple-element.15.q_ref, bf16[8,256,512]{2,1,0:T(8,128)(2,1)S(1)} %get-tuple-element.16.k_ref, ...), custom_call_target="tpu_custom_call", output_to_operand_aliasing={{}: (9, {})} | custom-call | flops 17179869184 | bytes 8388608 | tf_op jit(solution)/shard_map/row_attention/pallas_call | solution.py:209
  67.5 8.9 %row_attention.6.rest_0_ = bf16[32,8,16,256]{3,2,1,0:T(8,128)(2,1)S(1)} custom-call(s32[3]{0:T(128)S(1)} %pad_add_fusion.here_ref, bf16[8,512,256]{2,1,0:T(8,128)(2,1)S(1)} %get-tuple-element.15.q_ref, bf16[8,256,512]{2,1,0:T(8,128)(2,1)S(1)} %get-tuple-element.16.k_ref, ...), custom_call_target="tpu_custom_call", output_to_operand_aliasing={{}: (9, {})} | custom-call | flops 17179869184 | bytes 8388608 | tf_op jit(solution)/shard_map/row_attention/pallas_call | solution.py:209
  76.4 4.1 %collective-permute-done.9.bias_ref = bf16[8,8,16,512]{3,2,1,0:T(8,128)(2,1)S(1)} collective-permute-done((bf16[8,8,16,512]{3,2,1,0:T(8,128)(2,1)S(1)}, bf16[8,8,16,512]{3,2,1,0:T(8,128)(2,1)S(1)}, u32[]{:S(2)}, u32[]{:S(2)}) %collective-permute-start.9) | collective-permute-done | bytes 1048608 | tf_op jit(solution)/shard_map/ppermute | solution.py:331
  80.5 8.9 %row_attention.7 = bf16[32,8,16,256]{3,2,1,0:T(8,128)(2,1)S(1)} custom-call(s32[3]{0:T(128)S(1)} %pad_add_fusion.here_ref, bf16[8,512,256]{2,1,0:T(8,128)(2,1)S(1)} %get-tuple-element.15.q_ref, bf16[8,256,512]{2,1,0:T(8,128)(2,1)S(1)} %get-tuple-element.16.k_ref, bf16[8,512,256]{2,1,0:T(8,128)(2,1)S(1)} %get-tuple-element.17.v_ref, ...), custom_call_target="tpu_custom_call", output_to_operand_aliasing={{}: (9, {})} | custom-call | flops 17179869184 | bytes 8388608 | tf_op jit(solution)/shard_map/row_attention/pallas_call | solution.py:209
  89.4 0.0 copy-start.1
  89.4 0.0 copy-start.2
  89.4 0.0 copy-start.3
  89.4 0.0 copy-start.4
  89.4 0.0 copy-start.5
  89.4 0.0 copy-start.7
  89.4 0.0 copy-start.8
  89.4 0.0 copy-start.9
  89.5 0.0 copy-start.10
  89.5 36.3 %all_to_all.10 = bf16[32,8,16,256]{3,2,1,0:T(8,128)(2,1)S(1)} all-to-all(bf16[32,8,16,256]{3,2,1,0:T(8,128)(2,1)S(1)} %row_attention.7), channel_id=1, replica_groups=mesh['batch'=4,'dap'=32] {'dap'}, dimensions={0} | all-to-all | bytes 4194304 | tf_op jit(solution)/shard_map/all_to_all | solution.py:385
  125.8 19.4 %column_attention.1 = bf16[256,16,256]{2,1,0:T(8,128)(2,1)S(1)} custom-call(bf16[256,16,256]{2,1,0:T(8,128)(2,1)S(1)} %bitcast.33, f32[1,256]{1,0:T(1,128)S(1)} %bitcast.36, f32[1,256]{1,0:T(1,128)S(1)} %bitcast.37, bf16[256,256]{1,0:T(8,128)(2,1)S(1)} %copy-done.1, bf16[256,256]{1,0:T(8,128)(2,1)S(1)} %copy-done.2, bf16[256,256]{1,0:T(8,128)(2,1)S(1)} %copy-done.3, ...), custom_call_target="tpu_custom_call" | custom-call | tf_op jit(solution)/shard_map/column_attention/pallas_call | solution.py:305
  145.2 31.7 %all_to_all.11 = bf16[32,8,16,256]{3,2,1,0:T(8,128)(2,1)S(1)} all-to-all(bf16[32,8,16,256]{3,2,1,0:T(8,128)(2,1)S(1)} %bitcast.34), channel_id=1, replica_groups=mesh['batch'=4,'dap'=32] {'dap'}, dimensions={0} | all-to-all | bytes 4194304 | tf_op jit(solution)/shard_map/all_to_all | solution.py:398
  177.0 1.5 copy.26
  (37 shorter events, 0.1 us)
Async XLA Ops:
  0.0 1.6 copy-start
  1.6 0.7 copy-start.6
  2.3 0.7 copy-start.11
  2.9 31.1 %copy-start.12 = (bf16[8,512,256]{2,1,0:T(8,128)(2,1)S(1)}, bf16[8,512,256]{2,1,0:T(8,128)(2,1)}, u32[]{:S(2)}) copy-start(bf16[8,512,256]{2,1,0:T(8,128)(2,1)} %x_ref.10) | copy-start | bytes 6291460
  2.9 31.1 %copy-start.13 = (bf16[256,256]{1,0:T(8,128)(2,1)S(1)}, bf16[256,256]{1,0:T(8,128)(2,1)}, u32[]{:S(2)}) copy-start(bf16[256,256]{1,0:T(8,128)(2,1)} %q_w.2) | copy-start | bytes 393220
  2.9 31.1 %copy-start.14 = (bf16[256,256]{1,0:T(8,128)(2,1)S(1)}, bf16[256,256]{1,0:T(8,128)(2,1)}, u32[]{:S(2)}) copy-start(bf16[256,256]{1,0:T(8,128)(2,1)} %k_w.2) | copy-start | bytes 393220
  2.9 31.1 %copy-start.18 = (f32[256]{0:T(256)S(1)}, f32[256]{0:T(256)}, u32[]{:S(2)}) copy-start(f32[256]{0:T(256)} %param.24) | copy-start | bytes 3076
  2.9 31.1 %copy-start.19 = (f32[256]{0:T(256)S(1)}, f32[256]{0:T(256)}, u32[]{:S(2)}) copy-start(f32[256]{0:T(256)} %param.25) | copy-start | bytes 3076
  3.0 31.1 %copy-start.20 = (f32[256]{0:T(256)S(1)}, f32[256]{0:T(256)}, u32[]{:S(2)}) copy-start(f32[256]{0:T(256)} %param.32) | copy-start | bytes 3076
  6.1 13.0 %collective-permute-start = (bf16[8,16,512]{2,1,0:T(8,128)(2,1)S(1)}, bf16[8,16,512]{2,1,0:T(8,128)(2,1)}, u32[]{:S(2)}, u32[]{:S(2)}) collective-permute-start(bf16[8,16,512]{2,1,0:T(8,128)(2,1)S(1)} %pair_bias.1), channel_id=1, source_target_pairs={{1,0},{0,1},{3,2},{2,3},{5,4},{4,5},{7,6},{6,7},{9,8},{8,9},{11,10... | collective-permute-start | bytes 393224 | tf_op jit(solution)/shard_map/ppermute | solution.py:331
  9.5 11.8 %collective-permute-start.1 = (bf16[8,16,512]{2,1,0:T(8,128)(2,1)S(1)}, bf16[8,16,512]{2,1,0:T(8,128)(2,1)}, u32[]{:S(2)}, u32[]{:S(2)}) collective-permute-start(bf16[8,16,512]{2,1,0:T(8,128)(2,1)S(1)} %pair_bias.1), channel_id=1, source_target_pairs={{2,0},{3,1},{4,2},{5,3},{6,4},{7,5},{0,6},{1,7},{10,8},{11,9},{12,... | collective-permute-start | bytes 393224 | tf_op jit(solution)/shard_map/ppermute | solution.py:331
  12.2 11.1 %collective-permute-start.2 = (bf16[8,16,512]{2,1,0:T(8,128)(2,1)S(1)}, bf16[8,16,512]{2,1,0:T(8,128)(2,1)}, u32[]{:S(2)}, u32[]{:S(2)}) collective-permute-start(bf16[8,16,512]{2,1,0:T(8,128)(2,1)S(1)} %pair_bias.1), channel_id=1, source_target_pairs={{3,0},{2,1},{5,2},{4,3},{7,4},{6,5},{1,6},{0,7},{11,8},{10,9},{13,... | collective-permute-start | bytes 393224 | tf_op jit(solution)/shard_map/ppermute | solution.py:331
  12.8 11.4 %collective-permute-start.3 = (bf16[8,16,512]{2,1,0:T(8,128)(2,1)S(1)}, bf16[8,16,512]{2,1,0:T(8,128)(2,1)}, u32[]{:S(2)}, u32[]{:S(2)}) collective-permute-start(bf16[8,16,512]{2,1,0:T(8,128)(2,1)S(1)} %pair_bias.1), channel_id=1, source_target_pairs={{4,0},{5,1},{6,2},{7,3},{0,4},{1,5},{2,6},{3,7},{12,8},{13,9},{14,... | collective-permute-start | bytes 393224 | tf_op jit(solution)/shard_map/ppermute | solution.py:331
  13.3 12.5 %collective-permute-start.4 = (bf16[8,16,512]{2,1,0:T(8,128)(2,1)S(1)}, bf16[8,16,512]{2,1,0:T(8,128)(2,1)}, u32[]{:S(2)}, u32[]{:S(2)}) collective-permute-start(bf16[8,16,512]{2,1,0:T(8,128)(2,1)S(1)} %pair_bias.1), channel_id=1, source_target_pairs={{5,0},{4,1},{7,2},{6,3},{1,4},{0,5},{3,6},{2,7},{13,8},{12,9},{15,... | collective-permute-start | bytes 393224 | tf_op jit(solution)/shard_map/ppermute | solution.py:331
  19.1 7.7 %collective-permute-start.5 = (bf16[8,16,512]{2,1,0:T(8,128)(2,1)S(1)}, bf16[8,16,512]{2,1,0:T(8,128)(2,1)S(1)}, u32[]{:S(2)}, u32[]{:S(2)}) collective-permute-start(bf16[8,16,512]{2,1,0:T(8,128)(2,1)S(1)} %pair_bias.1), channel_id=1, source_target_pairs={{6,0},{7,1},{0,2},{1,3},{2,4},{3,5},{4,6},{5,7},{14,8},{15,9},{8,1... | collective-permute-start | bytes 393224 | tf_op jit(solution)/shard_map/ppermute | solution.py:331
  21.3 8.7 %collective-permute-start.6 = (bf16[8,16,512]{2,1,0:T(8,128)(2,1)S(1)}, bf16[8,16,512]{2,1,0:T(8,128)(2,1)S(1)}, u32[]{:S(2)}, u32[]{:S(2)}) collective-permute-start(bf16[8,16,512]{2,1,0:T(8,128)(2,1)S(1)} %pair_bias.1), channel_id=1, source_target_pairs={{7,0},{6,1},{1,2},{0,3},{3,4},{2,5},{5,6},{4,7},{15,8},{14,9},{9,1... | collective-permute-start | bytes 393224 | tf_op jit(solution)/shard_map/ppermute | solution.py:331
  29.9 25.0 %collective-permute-start.7 = (bf16[8,8,16,512]{3,2,1,0:T(8,128)(2,1)S(1)}, bf16[8,8,16,512]{3,2,1,0:T(8,128)(2,1)S(1)}, u32[]{:S(2)}, u32[]{:S(2)}) collective-permute-start(bf16[8,8,16,512]{3,2,1,0:T(8,128)(2,1)S(1)} %bitcast_dynamic-update-slice_fusion.bias_ref), channel_id=1, source_target_pairs={{8,0},{9,1},{10,2},{11,3},{12,4},{13,5},{14,6},{15,7},{16,8},{17,9... | collective-permute-start | bytes 3145736 | tf_op jit(solution)/shard_map/ppermute | solution.py:331
  34.0 24.3 %collective-permute-start.8 = (bf16[8,8,16,512]{3,2,1,0:T(8,128)(2,1)S(1)}, bf16[8,8,16,512]{3,2,1,0:T(8,128)(2,1)S(1)}, u32[]{:S(2)}, u32[]{:S(2)}) collective-permute-start(bf16[8,8,16,512]{3,2,1,0:T(8,128)(2,1)S(1)} %bitcast_dynamic-update-slice_fusion.bias_ref), channel_id=1, source_target_pairs={{24,0},{25,1},{26,2},{27,3},{28,4},{29,5},{30,6},{31,7},{0,8},{1,9... | collective-permute-start | bytes 3145736 | tf_op jit(solution)/shard_map/ppermute | solution.py:331
  34.1 0.9 copy-start.15
  35.0 0.9 copy-start.16
  35.9 6.5 %copy-start.17 = (bf16[256,256]{1,0:T(8,128)(2,1)S(1)}, bf16[256,256]{1,0:T(8,128)(2,1)}, u32[]{:S(2)}) copy-start(bf16[256,256]{1,0:T(8,128)(2,1)} %o_w.8) | copy-start | bytes 393220
  35.9 6.5 %copy-start.21 = (f32[256]{0:T(256)S(1)}, f32[256]{0:T(256)}, u32[]{:S(2)}) copy-start(f32[256]{0:T(256)} %param.34) | copy-start | bytes 3076
  40.5 2.0 %copy-start.22 = (f32[8,512,256]{2,1,0:T(8,128)}, f32[8,512,256]{2,1,0:T(8,128)S(1)}, u32[]{:S(2)}) copy-start(f32[8,512,256]{2,1,0:T(8,128)S(1)} %get-tuple-element.18.g_ref) | copy-start | bytes 12582916
  58.3 22.1 %collective-permute-start.9 = (bf16[8,8,16,512]{3,2,1,0:T(8,128)(2,1)S(1)}, bf16[8,8,16,512]{3,2,1,0:T(8,128)(2,1)S(1)}, u32[]{:S(2)}, u32[]{:S(2)}) collective-permute-start(bf16[8,8,16,512]{3,2,1,0:T(8,128)(2,1)S(1)} %collective-permute-done.7.bias_ref), channel_id=1, source_target_pairs={{8,0},{9,1},{10,2},{11,3},{12,4},{13,5},{14,6},{15,7},{16,8},{17,9... | collective-permute-start | bytes 3145736 | tf_op jit(solution)/shard_map/ppermute | solution.py:331
  89.4 36.4 %copy-start.1 = (bf16[256,256]{1,0:T(8,128)(2,1)S(1)}, bf16[256,256]{1,0:T(8,128)(2,1)}, u32[]{:S(2)}) copy-start(bf16[256,256]{1,0:T(8,128)(2,1)} %q_w.3) | copy-start | bytes 393220
  89.4 36.4 %copy-start.2 = (bf16[256,256]{1,0:T(8,128)(2,1)S(1)}, bf16[256,256]{1,0:T(8,128)(2,1)}, u32[]{:S(2)}) copy-start(bf16[256,256]{1,0:T(8,128)(2,1)} %k_w.3) | copy-start | bytes 393220
  89.4 36.4 %copy-start.3 = (bf16[256,256]{1,0:T(8,128)(2,1)S(1)}, bf16[256,256]{1,0:T(8,128)(2,1)}, u32[]{:S(2)}) copy-start(bf16[256,256]{1,0:T(8,128)(2,1)} %v_w.3) | copy-start | bytes 393220
  89.4 36.4 %copy-start.4 = (bf16[256,256]{1,0:T(8,128)(2,1)S(1)}, bf16[256,256]{1,0:T(8,128)(2,1)}, u32[]{:S(2)}) copy-start(bf16[256,256]{1,0:T(8,128)(2,1)} %g_w.3) | copy-start | bytes 393220
  89.4 36.4 %copy-start.5 = (bf16[256,256]{1,0:T(8,128)(2,1)S(1)}, bf16[256,256]{1,0:T(8,128)(2,1)}, u32[]{:S(2)}) copy-start(bf16[256,256]{1,0:T(8,128)(2,1)} %o_w.9) | copy-start | bytes 393220
  89.4 36.4 %copy-start.7 = (f32[256]{0:T(256)S(1)}, f32[256]{0:T(256)}, u32[]{:S(2)}) copy-start(f32[256]{0:T(256)} %param.35) | copy-start | bytes 3076
  89.4 36.4 %copy-start.8 = (f32[256]{0:T(256)S(1)}, f32[256]{0:T(256)}, u32[]{:S(2)}) copy-start(f32[256]{0:T(256)} %param.36) | copy-start | bytes 3076
  89.4 36.4 %copy-start.9 = (f32[256]{0:T(256)S(1)}, f32[256]{0:T(256)}, u32[]{:S(2)}) copy-start(f32[256]{0:T(256)} %param.41) | copy-start | bytes 3076
  89.5 36.4 %copy-start.10 = (f32[256]{0:T(256)S(1)}, f32[256]{0:T(256)}, u32[]{:S(2)}) copy-start(f32[256]{0:T(256)} %param.43) | copy-start | bytes 3076

commit v3 on v2

v3 whole, which is shorter than its diff:
```python
import functools

import jax
import jax.numpy as jnp
from jax import lax
from jax.experimental import pallas as pl
from jax.experimental.pallas import tpu as pltpu
from jax.sharding import PartitionSpec as P

H = 8
HEAD = 32
C = 256
LANES = 128
GROUP = LANES // HEAD
EPS = 1e-05
MIB = 1024 * 1024
HALVES = 2
HALF_ROWS = 8
NZ, NX, NY = 4, 4, 2
DAP = NZ * NX * NY
NT = (((1,), (1,)), ((), ()))


def norm(x, gain, bias):
    center = jnp.mean(x, axis=-1, keepdims=True)
    moved = x - center
    spread = jnp.mean(moved * moved, axis=-1, keepdims=True)
    return moved * lax.rsqrt(spread + EPS) * gain + bias


def lanes_of(part):
    return slice(part * LANES, (part + 1) * LANES)


def dot(a, b):
    return jnp.dot(a, b, preferred_element_type=jnp.float32)


def softmax_rounded(scores):
    top = jnp.max(scores, axis=-1, keepdims=True)
    e = jnp.exp(scores - top)
    total = jnp.sum(e, axis=-1, keepdims=True)
    return (e * (1.0 / total)).astype(jnp.bfloat16)


def head_of_lane():
    return lax.broadcasted_iota(jnp.int32, (1, LANES), 1) // HEAD


def stacked(q):
    head = head_of_lane()
    masks = [(head == i).astype(jnp.float32).astype(jnp.bfloat16) for i in range(GROUP)]
    return jnp.concatenate([q * mask for mask in masks], axis=0)


def own_lanes(mixed):
    head = head_of_lane()
    rows = mixed.shape[0] // GROUP
    total = mixed[:rows]
    for i in range(1, GROUP):
        total = jnp.where(head == i, mixed[i * rows : (i + 1) * rows], total)
    return total


def pipelined(count, score, soften, average):
    scores, weights = {0: score(0)}, {}
    for n in range(count + 1):
        if n + 1 < count:
            scores[n + 1] = score(n + 1)
        if n < count:
            weights[n] = soften(n, scores.pop(n))
        if n >= 1:
            average(n - 1, weights.pop(n - 1))


def project(normed, at_queries, q_w, k_w, v_w, g_w, g_b):
    q = (dot(at_queries, q_w[...]) * HEAD ** (-0.5)).astype(jnp.bfloat16)
    k_t = dot(normed, k_w[...]).T.astype(jnp.bfloat16)
    v = dot(normed, v_w[...]).astype(jnp.bfloat16)
    g = jax.nn.sigmoid(dot(at_queries, g_w[...]) + g_b[...])
    return q, k_t, v, g


def pair_kernel(x_ref, gain_ref, w_ref, out_ref, held):
    step = pl.program_id(0)
    rows = x_ref.shape[0]
    for i in range(rows):
        normed = norm(x_ref[i].astype(jnp.float32), gain_ref[...], 0.0).astype(jnp.bfloat16)
        bias = lax.dot_general(w_ref[...], normed, NT, preferred_element_type=jnp.float32)
        for part in range(held.shape[0]):
            low = step * rows // HALF_ROWS * (H * HALF_ROWS) + lax.rem(step * rows, HALF_ROWS) + i
            held[part, pl.ds(low, H, stride=HALF_ROWS), :] = bias[:, lanes_of(part)]

    @pl.when(step == pl.num_programs(0) - 1)
    def _():
        for part in range(held.shape[0]):
            out_ref[:, :, lanes_of(part)] = (
                held[part].astype(jnp.bfloat16).reshape(out_ref.shape[:2] + (LANES,))
            )


def pair_bias(pair_state, gain, weight):
    count, res, cz = pair_state.shape
    rows = 4
    return pl.pallas_call(
        pair_kernel,
        grid=(count // rows,),
        out_shape=jax.ShapeDtypeStruct((H, count, res), jnp.bfloat16),
        in_specs=[
            pl.BlockSpec((rows, res, cz), lambda i: (i, 0, 0)),
            pl.BlockSpec((1, cz), lambda i: (0, 0)),
            pl.BlockSpec((H, cz), lambda i: (0, 0)),
        ],
        out_specs=pl.BlockSpec((H, count, res), lambda i: (0, 0, 0)),
        scratch_shapes=[pltpu.VMEM((res // LANES, H * count, LANES), jnp.float32)],
        compiler_params=pltpu.CompilerParams(vmem_limit_bytes=56 * MIB),
        name="pair_bias",
    )(pair_state, gain.reshape(1, cz), weight.T)


def project_kernel(x_ref, gain, bias, q_w, k_w, v_w, g_w, g_b, q_ref, k_ref, v_ref, g_ref):
    count, res, width = x_ref.shape
    x = x_ref[...].reshape(count * res, width).astype(jnp.float32)
    normed = norm(x, gain[...], bias[...])
    split = normed.reshape(count, DAP, HALVES, HALF_ROWS, width)
    halves = [split[:, :, half].reshape(count, res // HALVES, width) for half in range(HALVES)]
    at_queries = jnp.concatenate(halves, axis=1).reshape(count * res, width)
    q, k_t, v, g = project(
        normed.astype(jnp.bfloat16), at_queries.astype(jnp.bfloat16), q_w, k_w, v_w, g_w, g_b
    )
    for out_ref, value in ((q_ref, q), (v_ref, v), (g_ref, g)):
        out_ref[...] = value.reshape(count, res, width)
    for n in range(count):
        k_ref[n] = k_t[:, n * res : (n + 1) * res]


def row_project(x, gain, bias, q_w, k_w, v_w, g_w, g_b):
    seqs, res, width = x.shape
    count = 2
    block = pl.BlockSpec((count, res, width), lambda s: (s, 0, 0))
    turned = pl.BlockSpec((count, width, res), lambda s: (s, 0, 0))
    vector = pl.BlockSpec((1, width), lambda s: (0, 0))
    weight = pl.BlockSpec((width, width), lambda s: (0, 0))
    shape = jax.ShapeDtypeStruct
    return pl.pallas_call(
        project_kernel,
        grid=(seqs // count,),
        out_shape=[
            shape((seqs, res, width), jnp.bfloat16),
            shape((seqs, width, res), jnp.bfloat16),
            shape((seqs, res, width), jnp.bfloat16),
            shape((seqs, res, width), jnp.float32),
        ],
        in_specs=[block, vector, vector] + [weight] * 4 + [vector],
        out_specs=[block, turned, block, block],
        compiler_params=pltpu.CompilerParams(vmem_limit_bytes=24 * MIB),
        cost_estimate=pl.CostEstimate(
            flops=2 * seqs * res * width * width * 4,
            bytes_accessed=x.size * 12,
            transcendentals=x.size * 2,
        ),
        name="row_project",
    )(x, gain.reshape(1, -1), bias.reshape(1, -1), q_w, k_w, v_w, g_w, g_b.reshape(1, -1))


def row_kernel(blocks, here_ref, *refs):
    count = len(blocks)
    planes = 1 + max(which for _, _, which in blocks)
    q_refs, g_refs, x_refs, (k_ref, v_ref) = refs[:2], refs[2:4], refs[4:6], refs[6:8]
    bias_refs, (o_w, o_b) = refs[8 : 8 + planes], refs[8 + planes : 10 + planes]
    held, weights, ready, sems = refs[-4:]
    halves = sorted({half for _, half, _ in blocks})
    outs = dict(zip(halves, refs[-4 - len(halves) : -4]))
    step, last = pl.program_id(0), pl.num_programs(0) - 1
    seqs, part_rows, width = q_refs[0].shape
    tile = count * part_rows
    owners = part_rows // HALF_ROWS
    groups = H // GROUP

    def place(n):
        return n // groups, n % groups, lanes_of(n % groups)

    def both(pick):
        return jnp.concatenate([pick(n) for n in range(count)], axis=0)

    def score(n):
        seq, _, lanes = place(n)
        q = both(lambda b: q_refs[b][seq, :, lanes])
        held[n % 2] = dot(stacked(q), k_ref[seq, lanes, :])

    def slot(x, y):
        return lax.rem(x - here_ref[1] + NX, NX) * NY + lax.rem(y - here_ref[2] + NY, NY)

    slots = [slot(x, y) for x in range(NX) for y in range(NY)]
    taken = 4

    def soften(n, _):
        _, group, _ = place(n)
        for b, (_, half, which) in enumerate(blocks):
            for two in range(0, GROUP, 2):
                for first in range(0, owners, taken):
                    piece = (half * H + group * GROUP + two) // 2
                    bias = [
                        bias_refs[which][slots[o], piece].astype(jnp.float32)
                        for o in range(first, first + taken)
                    ]
                    for i in range(2):
                        low = (two + i) * tile + b * part_rows + first * HALF_ROWS
                        rows = slice(low, low + taken * HALF_ROWS)
                        mine = [value[i * HALF_ROWS : (i + 1) * HALF_ROWS] for value in bias]
                        weights[n % 2, rows] = softmax_rounded(
                            held[n % 2, rows] + jnp.concatenate(mine, axis=0)
                        )

    gated, done = {}, []

    def average(n, _):
        seq, group, lanes = place(n)
        mixed = own_lanes(dot(weights[n % 2], v_ref[seq, :, lanes]))
        gated[group] = (mixed * both(lambda b: g_refs[b][seq, :, lanes])).astype(jnp.bfloat16)
        if len(gated) == groups:
            whole = jnp.concatenate([gated.pop(part) for part in range(groups)], axis=1)
            update = dot(whole, o_w[...]) + o_b[...]
            after = []
            for b, (_, half, _) in enumerate(blocks):
                x = x_refs[b][seq].astype(jnp.float32).reshape(owners, HALVES, HALF_ROWS, width)
                own = update[b * part_rows : (b + 1) * part_rows].reshape(owners, HALF_ROWS, width)
                after.append(x[:, half] + own)
            done.append(after)
            if len(done) == 2:
                low = (seq - 1) * HALF_ROWS
                for b in range(count):
                    rows = jnp.concatenate([value[b] for value in done], axis=1)
                    ready[step, b, :, low : low + 2 * HALF_ROWS] = rows.astype(jnp.bfloat16)
                done.clear()

    pipelined(seqs * groups, score, soften, average)

    def copies(step):
        for b, (plane, half, _) in enumerate(blocks):
            first = pl.multiple_of(lax.rem(here_ref[0] + plane, NZ) * owners, owners)
            rows = pl.ds(pl.multiple_of(step * seqs * HALF_ROWS, seqs * HALF_ROWS), seqs * HALF_ROWS)
            yield pltpu.make_async_copy(
                ready.at[step, b], outs[half].at[pl.ds(first, owners), rows], sems.at[step, b]
            )

    for copy in copies(step):
        copy.start()

    @pl.when(step == last)
    def _():
        for n in range(ready.shape[0]):
            for copy in copies(n):
                copy.wait()


def row_attention(blocks, here, q, k, v, g, x, biases, o_w, o_b, held):
    seqs, res, width = x.shape
    own = res // DAP
    part_rows = DAP // NZ * HALF_ROWS
    once = 4
    halves = sorted({half for _, half, _ in blocks})

    def which(here, plane):
        return lax.rem(here[0] + plane, NZ)

    queries = [
        pl.BlockSpec(
            (once, part_rows, width),
            lambda s, here, plane=plane, half=half: (s, half * NZ + which(here, plane), 0),
        )
        for plane, half, _ in blocks
    ]
    residual = [
        pl.BlockSpec((once, res // NZ, width), lambda s, here, plane=plane: (s, which(here, plane), 0))
        for plane, _, _ in blocks
    ]
    args = [q, q, g, g, x, x, k, v, *biases, o_w, o_b.reshape(1, -1), *held]
    return pl.pallas_call(
        functools.partial(row_kernel, blocks),
        out_shape=[jax.ShapeDtypeStruct((DAP, seqs * HALF_ROWS, width), jnp.bfloat16)] * len(halves),
        grid_spec=pltpu.PrefetchScalarGridSpec(
            num_scalar_prefetch=1,
            grid=(seqs // once,),
            in_specs=queries
            + queries
            + residual
            + [
                pl.BlockSpec((once, width, res), lambda s, here: (s, 0, 0)),
                pl.BlockSpec((once, res, width), lambda s, here: (s, 0, 0)),
            ]
            + [pl.BlockSpec(bias.shape, lambda s, here: (0, 0, 0, 0)) for bias in biases]
            + [
                pl.BlockSpec((width, width), lambda s, here: (0, 0)),
                pl.BlockSpec((1, width), lambda s, here: (0, 0)),
            ]
            + [pl.BlockSpec(memory_space=pl.ANY)] * len(held),
            out_specs=[pl.BlockSpec(memory_space=pl.ANY)] * len(halves),
            scratch_shapes=[
                pltpu.VMEM((2, GROUP * part_rows * len(blocks), res), jnp.float32),
                pltpu.VMEM((2, GROUP * part_rows * len(blocks), res), jnp.bfloat16),
                pltpu.VMEM(
                    (seqs // once, len(blocks), DAP // NZ, once * HALF_ROWS, width), jnp.bfloat16
                ),
                pltpu.SemaphoreType.DMA((seqs // once, len(blocks))),
            ],
        ),
        input_output_aliases={len(args) + 1 - len(held) + n: n for n in range(len(held))},
        compiler_params=pltpu.CompilerParams(vmem_limit_bytes=24 * MIB),
        cost_estimate=pl.CostEstimate(
            flops=seqs * H * part_rows * len(blocks) * res * 256 * 16,
            bytes_accessed=8 * 1024 * 1024,
            transcendentals=seqs * H * part_rows * len(blocks) * res,
        ),
        name="row_attention",
    )(here, *args)


def column_kernel(at_once, x_ref, gain, bias, q_w, k_w, v_w, g_w, g_b, o_w, o_b, *refs):
    out_ref, held, scores, weights = refs[-4:]
    step = pl.program_id(0)
    owners, per, width = x_ref.shape
    items = pl.num_programs(0) * at_once
    seqs = owners * per // items
    parts = width // LANES

    @pl.when(step == 0)
    def _():
        for part in range(parts):
            held[part] = x_ref[:, :, lanes_of(part)].astype(jnp.float32).reshape(-1, LANES)

    mine = [pl.ds(step * at_once + n, seqs, stride=items) for n in range(at_once)]
    x = jnp.concatenate(
        [jnp.concatenate([held[part, rows, :] for rows in mine], axis=0) for part in range(parts)], axis=1
    )
    normed = norm(x, gain[...], bias[...]).astype(jnp.bfloat16)
    q, k_t, v, g = project(normed, normed, q_w, k_w, v_w, g_w, g_b)
    gated = {}

    def place(n):
        return slice(n // parts * seqs, (n // parts + 1) * seqs), lanes_of(n % parts)

    def score(n):
        rows, lanes = place(n)
        scores[n % 2] = dot(stacked(q[rows, lanes]), k_t[lanes, rows])

    def soften(n, _):
        for low in range(0, GROUP * seqs, 64):
            weights[n % 2, low : low + 64] = softmax_rounded(scores[n % 2, low : low + 64])

    def average(n, _):
        rows, lanes = place(n)
        mixed = own_lanes(dot(weights[n % 2], v[rows, lanes]))
        gated[n] = (mixed * g[rows, lanes]).astype(jnp.bfloat16)

    pipelined(at_once * parts, score, soften, average)
    gated = [
        jnp.concatenate([gated[n * parts + part] for part in range(parts)], axis=1)
        for n in range(at_once)
    ]
    after = x + (dot(jnp.concatenate(gated, axis=0), o_w[...]) + o_b[...])
    for n, rows in enumerate(mine):
        for part in range(parts):
            held[part, rows, :] = after[n * seqs : (n + 1) * seqs, lanes_of(part)]

    @pl.when(step == pl.num_programs(0) - 1)
    def _():
        for part in range(parts):
            out_ref[:, :, lanes_of(part)] = (
                held[part].reshape(owners, per, LANES).astype(jnp.bfloat16)
            )


def column_attention(items, half, before, x, gain, bias, q_w, k_w, v_w, g_w, g_b, o_w, o_b):
    width = x.shape[2]
    seqs = x.size // (items * width)
    at_once = 4
    whole = pl.BlockSpec(x.shape, lambda r: (0, 0, 0))
    vector = pl.BlockSpec((1, width), lambda r: (0, 0))
    weight = pl.BlockSpec((width, width), lambda r: (0, 0))
    return pl.pallas_call(
        functools.partial(column_kernel, at_once),
        grid=(items // at_once,),
        out_shape=[jax.ShapeDtypeStruct((DAP, HALVES * x.shape[1], width), jnp.bfloat16)],
        in_specs=[whole, vector, vector]
        + [weight] * 4
        + [vector, weight, vector]
        + [pl.BlockSpec(memory_space=pl.ANY)] * len(before),
        out_specs=[pl.BlockSpec(x.shape, lambda r: (0, half, 0))],
        input_output_aliases={10: 0} if before else {},
        scratch_shapes=[
            pltpu.VMEM((width // LANES, seqs * items, LANES), jnp.float32),
            pltpu.VMEM((2, GROUP * seqs, seqs), jnp.float32),
            pltpu.VMEM((2, GROUP * seqs, seqs), jnp.bfloat16),
        ],
        compiler_params=pltpu.CompilerParams(vmem_limit_bytes=24 * MIB),
        name="column_attention",
    )(
        x, gain.reshape(1, -1), bias.reshape(1, -1), q_w, k_w, v_w, g_w, g_b.reshape(1, -1),
        o_w, o_b.reshape(1, -1), *before,
    )


def fetch(value, z=0, x=0, y=0):
    pairs = []
    for dz in range(NZ):
        for dx in range(NX):
            for dy in range(NY):
                src = ((dz + z) % NZ * NX + (dx + x) % NX) * NY + (dy + y) % NY
                pairs.append((src, (dz * NX + dx) * NY + dy))
    return lax.ppermute(value, "dap", pairs)


def join_kernel(*refs):
    count = len(refs) - 2
    parts, out_ref, sems = refs[:count], refs[count], refs[count + 1]
    place, copies = 0, []
    for n, part in enumerate(parts):
        size = part.shape[0]
        copies.append(pltpu.make_async_copy(part, out_ref.at[pl.ds(place, size)], sems.at[n]))
        place += size
    for copy in copies:
        copy.start()
    for copy in copies:
        copy.wait()


def join(*parts):
    total = sum(part.shape[0] for part in parts)
    return pl.pallas_call(
        join_kernel,
        out_shape=jax.ShapeDtypeStruct((total,) + parts[0].shape[1:], parts[0].dtype),
        in_specs=[pl.BlockSpec(memory_space=pl.ANY)] * len(parts),
        out_specs=pl.BlockSpec(memory_space=pl.ANY),
        scratch_shapes=[pltpu.SemaphoreType.DMA((len(parts),))],
        compiler_params=pltpu.CompilerParams(vmem_limit_bytes=8 * MIB),
        name="join",
    )(*parts)


def exchange(value):
    return lax.all_to_all(value, "dap", split_axis=0, concat_axis=0, tiled=True)


def per_device(
    alignment,
    pair_state,
    row_norm_gain,
    row_norm_bias,
    pair_norm_gain,
    pair_weight,
    row_query,
    row_key,
    row_value,
    row_gate,
    row_gate_bias,
    row_output,
    row_output_bias,
    column_norm_gain,
    column_norm_bias,
    column_query,
    column_key,
    column_value,
    column_gate,
    column_gate_bias,
    column_output,
    column_output_bias,
):
    seqs, res, width = alignment.shape
    own = res // DAP
    me = lax.axis_index("dap")
    here = jnp.stack([me // (NX * NY), me // NY % NX, me % NY]).astype(jnp.int32)
    local = pair_bias(pair_state, pair_norm_gain, pair_weight)[None]
    pair = join(local, fetch(local, y=1))
    own_plane = join(pair, *(fetch(pair, x=step) for step in (1, 2, 3)))
    far_pair = fetch(pair, z=2)
    own_plane, far_pair, inputs = lax.optimization_barrier((own_plane, far_pair, alignment))
    ahead, behind = fetch(own_plane, z=1), fetch(own_plane, z=3)
    far_plane = join(far_pair, *(fetch(far_pair, x=step) for step in (1, 2, 3)))
    projected = row_project(
        inputs, row_norm_gain, row_norm_bias, row_query, row_key, row_value, row_gate, row_gate_bias
    )

    def attend(blocks, biases, *held):
        return row_attention(
            blocks, here, *projected, alignment, biases, row_output, row_output_bias, held
        )

    after = attend(((0, 0, 0), (0, 1, 0)), [own_plane])
    after = attend(((2, 0, 0), (2, 1, 0)), [far_plane], *after)
    first = attend(((1, 0, 0), (3, 0, 1)), [ahead, behind], after[0])[0]
    second = attend(((1, 1, 0), (3, 1, 1)), [ahead, behind], after[1])[0]
    first, second = lax.optimization_barrier((exchange(first), second))
    items = own // HALVES
    columns = ()
    for half, part in enumerate((first, exchange(second))):
        columns = column_attention(
            items,
            half,
            columns,
            part,
            column_norm_gain,
            column_norm_bias,
            column_query,
            column_key,
            column_value,
            column_gate,
            column_gate_bias,
            column_output,
            column_output_bias,
        )
    back = exchange(columns[0]).reshape(DAP, HALVES, seqs, items, width)
    return back.transpose(2, 0, 1, 3, 4).reshape(alignment.shape)


def solution(mesh):
    split = P(("batch", "dap"), None, None)
    return jax.shard_map(
        per_device,
        mesh=mesh,
        in_specs=(split, split) + (P(),) * 20,
        out_specs=split,
        check_vma=False,
    )
```

time: 179 us -> 175 us (0.978)
  blocking collectives: 68 us -> 31.4 us
  starting transfers between devices: 18.6 us -> 36.8 us
  local copies, waits for them, and re-layouts: 12.9 us -> 19.1 us
  waiting for transfers between devices: 16 us -> 21 us
  Pallas kernels: 62.6 us -> 65.6 us
    all_to_all x2 -> x1, blocking collectives: 68 us -> 31.4 us  [exchange(): return lax.all_to_all(value, 'dap', split_axis=0, concat_axis=0, tiled=True)]
    all_to_all x0 -> x2, starting transfers between devices: none -> 18.7 us  [exchange(): return lax.all_to_all(value, 'dap', split_axis=0, concat_axis=0, tiled=True)]
    all_to_all x0 -> x2, waiting for transfers between devices: none -> 6.36 us  [exchange(): return lax.all_to_all(value, 'dap', split_axis=0, concat_axis=0, tiled=True)]
    unnamed x53 -> x70, local copies, waits for them, and re-layouts: 11.4 us -> 17.6 us
    pallas_call x1, Pallas kernels: 3.15 us -> 5.26 us  [pair_bias(): pl.pallas_call(pair_kernel, grid=(count // rows,), out_shape=jax.ShapeDty...]
    pallas_call x4 -> x7, Pallas kernels: 35.5 us -> 36.8 us  [the longest x4 36.2 us: row_attention(): pl.pallas_call(functools.partial(row_kernel, blocks), out_shape=[jax.Shap...]
    pallas_call x1 -> x2, Pallas kernels: 19.4 us -> 19.3 us  [column_attention(): pl.pallas_call(functools.partial(column_kernel, at_once), grid=(items //...]
  transfers between devices with their start and end apart: 10 -> 12, of which waited for: 7 -> 6; matrix products, arithmetic and copies ran while one was open for 3% -> 0% of each run, Pallas kernels for 17% -> 23%
where the time goes in v3:
time: 175 us; the launch traced here: 174 us
  Pallas kernels  65.6 us (37%)
  starting transfers between devices  36.8 us (21%)
  blocking collectives  31.4 us (18%)
  waiting for transfers between devices  21 us (12%)
  local copies, waits for them, and re-layouts  19.1 us (11%)
    pallas_call x4, Pallas kernels, row_attention(): pl.pallas_call(functools.partial(row_kernel, blocks), out_shape=[jax.Shap...  36.2 us
    all_to_all x1, blocking collectives, exchange(): return lax.all_to_all(value, 'dap', split_axis=0, concat_axis=0, tiled=True)  31.4 us
    pallas_call x2, Pallas kernels, column_attention(): pl.pallas_call(functools.partial(column_kernel, at_once), grid=(items //...  19.3 us
    all_to_all x2, starting transfers between devices, exchange(): return lax.all_to_all(value, 'dap', split_axis=0, concat_axis=0, tiled=True)  18.7 us
    ppermute x10, starting transfers between devices, fetch(): return lax.ppermute(value, 'dap', pairs)  18.1 us
    unnamed x70, local copies, waits for them, and re-layouts  17.6 us
    ppermute x10, waiting for transfers between devices, fetch(): return lax.ppermute(value, 'dap', pairs)  14.6 us
    all_to_all x2, waiting for transfers between devices, exchange(): return lax.all_to_all(value, 'dap', split_axis=0, concat_axis=0, tiled=True)  6.36 us
  transfers between devices with their start and end apart: 12, of which 6 were waited for; matrix products, arithmetic and copies ran while one was open for 0% of the time, Pallas kernels for 23%

profile of v3, /device:TPU:0, one launch (start us, length us, event | category | flops | bytes accessed | tf_op | source)
XLA Modules:
  0.0 174.4 jit_solution(11005902042011238956)
XLA Ops:
  0.0 5.3 %pair_bias.1 = bf16[8,16,512]{2,1,0:T(8,128)(2,1)} custom-call(bf16[16,512,128]{2,1,0:T(8,128)(2,1)} %x_ref.1, f32[1,128]{1,0:T(1,128)} %bitcast.37, bf16[8,128]{1,0:T(8,128)(2,1)} %bitcast.36), custom_call_target="tpu_custom_call" | custom-call | tf_op jit(solution)/shard_map/pair_bias/pallas_call | solution.py:105
  5.3 3.3 %collective-permute-start = (bf16[1,8,16,512]{3,2,1,0:T(8,128)(2,1)}, bf16[1,8,16,512]{3,2,1,0:T(8,128)(2,1)S(1)}, u32[]{:S(2)}, u32[]{:S(2)}) collective-permute-start(bf16[1,8,16,512]{3,2,1,0:T(8,128)(2,1)} %bitcast.18), channel_id=1, source_target_pairs={{1,0},{0,1},{3,2},{2,3},{5,4},{4,5},{7,6},{6,7},{9,8},{8,9},{11,10... | collective-permute-start | bytes 393224 | tf_op jit(solution)/shard_map/ppermute | solution.py:411
  8.6 3.7 %collective-permute-done.refs_1_ = bf16[1,8,16,512]{3,2,1,0:T(8,128)(2,1)S(1)} collective-permute-done((bf16[1,8,16,512]{3,2,1,0:T(8,128)(2,1)}, bf16[1,8,16,512]{3,2,1,0:T(8,128)(2,1)S(1)}, u32[]{:S(2)}, u32[]{:S(2)}) %collective-permute-start) | collective-permute-done | bytes 131104 | tf_op jit(solution)/shard_map/ppermute | solution.py:411
  12.3 0.9 copy-done.7
  13.2 0.3 join.3.refs_0_
  13.5 2.9 %collective-permute-start.1 = (bf16[2,8,16,512]{3,2,1,0:T(8,128)(2,1)S(1)}, bf16[2,8,16,512]{3,2,1,0:T(8,128)(2,1)S(1)}, u32[]{:S(2)}, u32[]{:S(2)}) collective-permute-start(bf16[2,8,16,512]{3,2,1,0:T(8,128)(2,1)S(1)} %join.3.refs_0_), channel_id=1, source_target_pairs={{2,0},{3,1},{4,2},{5,3},{6,4},{7,5},{0,6},{1,7},{10,8},{11,9},{12,... | collective-permute-start | bytes 786440 | tf_op jit(solution)/shard_map/ppermute | solution.py:411
  16.4 0.8 collective-permute-start.2
  17.2 0.9 collective-permute-start.3
  18.1 3.9 %collective-permute-start.4 = (bf16[2,8,16,512]{3,2,1,0:T(8,128)(2,1)S(1)}, bf16[2,8,16,512]{3,2,1,0:T(8,128)(2,1)S(1)}, u32[]{:S(2)}, u32[]{:S(2)}) collective-permute-start(bf16[2,8,16,512]{3,2,1,0:T(8,128)(2,1)S(1)} %join.3.refs_0_), channel_id=1, source_target_pairs={{16,0},{17,1},{18,2},{19,3},{20,4},{21,5},{22,6},{23,7},{24,8},{25... | collective-permute-start | bytes 786440 | tf_op jit(solution)/shard_map/ppermute | solution.py:411
  22.0 0.1 pad_add_fusion.here_ref
  22.0 4.7 %collective-permute-done.1.refs_1_ = bf16[2,8,16,512]{3,2,1,0:T(8,128)(2,1)S(1)} collective-permute-done((bf16[2,8,16,512]{3,2,1,0:T(8,128)(2,1)S(1)}, bf16[2,8,16,512]{3,2,1,0:T(8,128)(2,1)S(1)}, u32[]{:S(2)}, u32[]{:S(2)}) %collective-permute-start.1) | collective-permute-done | bytes 262176 | tf_op jit(solution)/shard_map/ppermute | solution.py:411
  26.7 0.4 collective-permute-done.2.refs_2_
  27.1 3.3 %collective-permute-done.3.refs_3_ = bf16[2,8,16,512]{3,2,1,0:T(8,128)(2,1)S(1)} collective-permute-done((bf16[2,8,16,512]{3,2,1,0:T(8,128)(2,1)S(1)}, bf16[2,8,16,512]{3,2,1,0:T(8,128)(2,1)S(1)}, u32[]{:S(2)}, u32[]{:S(2)}) %collective-permute-start.3) | collective-permute-done | bytes 262176 | tf_op jit(solution)/shard_map/ppermute | solution.py:411
  30.4 0.1 join.4.refs_8_
  30.5 0.7 collective-permute-start.7
  31.2 0.8 collective-permute-start.8
  32.0 0.8 collective-permute-start.9
  32.8 4.0 %collective-permute-start.5 = (bf16[8,8,16,512]{3,2,1,0:T(8,128)(2,1)S(1)}, bf16[8,8,16,512]{3,2,1,0:T(8,128)(2,1)S(1)}, u32[]{:S(2)}, u32[]{:S(2)}) collective-permute-start(bf16[8,8,16,512]{3,2,1,0:T(8,128)(2,1)S(1)} %join.4.refs_8_), channel_id=1, source_target_pairs={{8,0},{9,1},{10,2},{11,3},{12,4},{13,5},{14,6},{15,7},{16,8},{17,9... | collective-permute-start | bytes 3145736 | tf_op jit(solution)/shard_map/ppermute | solution.py:411
  37.0 4.3 %row_project.1 = (bf16[8,512,256]{2,1,0:T(8,128)(2,1)S(1)}, bf16[8,256,512]{2,1,0:T(8,128)(2,1)S(1)}, bf16[8,512,256]{2,1,0:T(8,128)(2,1)S(1)}, f32[8,512,256]{2,1,0:T(8,128)S(1)}) custom-call(bf16[8,512,256]{2,1,0:T(8,128)(2,1)S(1)} %copy-done.12, f32[1,256]{1,0:T(1,128)S(1)} %bitcast.28, f32[1,256]{1,0:T(1,128)S(1)} %bitcast.29, ...), custom_call_target="tpu_custom_call" | custom-call | flops 2147483648 | bytes 12582912 | tf_op jit(solution)/shard_map/row_project/pallas_call | solution.py:145
  41.3 0.0 copy-start.29
  41.4 9.2 %row_attention.4 = (bf16[32,64,256]{2,1,0:T(8,128)(2,1)}, bf16[32,64,256]{2,1,0:T(8,128)(2,1)}) custom-call(s32[3]{0:T(128)S(1)} %pad_add_fusion.here_ref, bf16[8,512,256]{2,1,0:T(8,128)(2,1)S(1)} %get-tuple-element.19.refs_0_.refs_1_, bf16[8,512,256]{2,1,0:T(8,128)(2,1)S(1)} %get-tuple-element.19.refs_0_.refs_1_, ...), custom_call_target="tpu_custom_call" | custom-call | flops 17179869184 | bytes 8388608 | tf_op jit(solution)/shard_map/row_attention/pallas_call | solution.py:279
  50.6 0.1 join.5.refs_8_
  50.7 8.9 %row_attention.5 = (bf16[32,64,256]{2,1,0:T(8,128)(2,1)}, bf16[32,64,256]{2,1,0:T(8,128)(2,1)}) custom-call(s32[3]{0:T(128)S(1)} %pad_add_fusion.here_ref, bf16[8,512,256]{2,1,0:T(8,128)(2,1)S(1)} %get-tuple-element.19.refs_0_.refs_1_, bf16[8,512,256]{2,1,0:T(8,128)(2,1)S(1)} %get-tuple-element.19.refs_0_.refs_1_, ...), custom_call_target="tpu_custom_call", output_to_operand_aliasing={{0}: (12, {}), {1}: (13, {})} | custom-call | flops 17179869184 | bytes 8388608 | tf_op jit(solution)/shard_map/row_attention/pallas_call | solution.py:279
  59.6 2.5 %collective-permute-done.6.refs_9_ = bf16[8,8,16,512]{3,2,1,0:T(8,128)(2,1)S(1)} collective-permute-done((bf16[8,8,16,512]{3,2,1,0:T(8,128)(2,1)S(1)}, bf16[8,8,16,512]{3,2,1,0:T(8,128)(2,1)S(1)}, u32[]{:S(2)}, u32[]{:S(2)}) %collective-permute-start.6) | collective-permute-done | bytes 1048608 | tf_op jit(solution)/shard_map/ppermute | solution.py:411
  62.1 9.1 %row_attention.6 = bf16[32,64,256]{2,1,0:T(8,128)(2,1)} custom-call(s32[3]{0:T(128)S(1)} %pad_add_fusion.here_ref, bf16[8,512,256]{2,1,0:T(8,128)(2,1)S(1)} %get-tuple-element.19.refs_0_.refs_1_, bf16[8,512,256]{2,1,0:T(8,128)(2,1)S(1)} %get-tuple-element.19.refs_0_.refs_1_, ...), custom_call_target="tpu_custom_call", output_to_operand_aliasing={{}: (13, {})} | custom-call | flops 17179869184 | bytes 8388608 | tf_op jit(solution)/shard_map/row_attention/pallas_call | solution.py:279
  71.3 0.9 copy-done.14
  72.2 1.0 copy-done.16
  73.3 8.4 %all-to-all-start = ((bf16[32,64,256]{2,1,0:T(8,128)(2,1)}), bf16[32,64,256]{2,1,0:T(8,128)(2,1)S(1)}, u32[]{:S(2)}, u32[]{:S(2)}) async-start(bf16[32,64,256]{2,1,0:T(8,128)(2,1)} %row_attention.6), calls=%async_computation | async-start | bytes 2097152 | tf_op jit(solution)/shard_map/all_to_all | solution.py:442
  81.7 0.0 copy-start.13
  81.7 1.6 copy-done.13
  83.3 1.2 copy-done.15
  84.5 1.2 copy-done.17
  85.7 2.2 %copy-done.28 = f32[8,512,256]{2,1,0:T(8,128)S(1)} copy-done((f32[8,512,256]{2,1,0:T(8,128)S(1)}, f32[8,512,256]{2,1,0:T(8,128)}, u32[]{:S(2)}) %copy-start.28) | copy-done | bytes 4194328
  87.9 1.6 copy-done.30
  89.5 1.6 copy-done.32
  91.1 1.6 copy-done.34
  92.7 9.1 %row_attention.7 = bf16[32,64,256]{2,1,0:T(8,128)(2,1)} custom-call(s32[3]{0:T(128)S(1)} %pad_add_fusion.here_ref, bf16[8,512,256]{2,1,0:T(8,128)(2,1)S(1)} %copy-done.30, bf16[8,512,256]{2,1,0:T(8,128)(2,1)S(1)} %copy-done.30, f32[8,512,256]{2,1,0:T(8,128)S(1)} %copy-done.28, f32[8,512,256]{2,1,0:T(8,128)S(1)} %copy-done.28, ...), custom_call_target="tpu_custom_call", output_to_operand_aliasing={{}: (13, {})} | custom-call | flops 17179869184 | bytes 8388608 | tf_op jit(solution)/shard_map/row_attention/pallas_call | solution.py:279
  101.8 0.0 copy-start
  101.9 10.3 %all-to-all-start.1 = ((bf16[32,64,256]{2,1,0:T(8,128)(2,1)}), bf16[32,64,256]{2,1,0:T(8,128)(2,1)}, u32[]{:S(2)}, u32[]{:S(2)}) async-start(bf16[32,64,256]{2,1,0:T(8,128)(2,1)} %row_attention.7), calls=%async_computation.1 | async-start | bytes 2097152 | tf_op jit(solution)/shard_map/all_to_all | solution.py:442
  112.3 0.9 copy-done.3
  113.2 0.9 copy-done.5
  114.1 9.0 %column_attention.2.refs_0_ = bf16[32,128,256]{2,1,0:T(8,128)(2,1)S(1)} custom-call(bf16[32,64,256]{2,1,0:T(8,128)(2,1)S(1)} %all-to-all-done.x_ref, f32[1,256]{1,0:T(1,128)S(1)} %bitcast.20, f32[1,256]{1,0:T(1,128)S(1)} %bitcast.22, bf16[256,256]{1,0:T(8,128)(2,1)S(1)} %copy-done, bf16[256,256]{1,0:T(8,128)(2,1)S(1)} %copy-done.1, ...), custom_call_target="tpu_custom_call" | custom-call | tf_op jit(solution)/shard_map/column_attention/pallas_call | solution.py:381
  123.1 6.4 %all-to-all-done.1.x_ref = bf16[32,64,256]{2,1,0:T(8,128)(2,1)} async-done(((bf16[32,64,256]{2,1,0:T(8,128)(2,1)}), bf16[32,64,256]{2,1,0:T(8,128)(2,1)}, u32[]{:S(2)}, u32[]{:S(2)}) %all-to-all-start.1) | async-done | bytes 1048608 | tf_op jit(solution)/shard_map/all_to_all | solution.py:442
  129.5 0.9 copy-done.4
  130.4 0.9 copy-done.6
  131.3 10.2 %column_attention.3 = bf16[32,128,256]{2,1,0:T(8,128)(2,1)S(1)} custom-call(bf16[32,64,256]{2,1,0:T(8,128)(2,1)} %all-to-all-done.1.x_ref, f32[1,256]{1,0:T(1,128)S(1)} %bitcast.21, f32[1,256]{1,0:T(1,128)S(1)} %bitcast.23, bf16[256,256]{1,0:T(8,128)(2,1)S(1)} %copy-done, bf16[256,256]{1,0:T(8,128)(2,1)S(1)} %copy-done.1, ...), custom_call_target="tpu_custom_call", output_to_operand_aliasing={{}: (10, {})} | custom-call | tf_op jit(solution)/shard_map/column_attention/pallas_call | solution.py:381
  141.5 31.4 %all_to_all.15 = bf16[32,128,256]{2,1,0:T(8,128)(2,1)S(1)} all-to-all(bf16[32,128,256]{2,1,0:T(8,128)(2,1)S(1)} %column_attention.3), channel_id=1, replica_groups=mesh['batch'=4,'dap'=32] {'dap'}, dimensions={0} | all-to-all | bytes 4194304 | tf_op jit(solution)/shard_map/all_to_all | solution.py:442
  172.9 1.5 copy.28
  (60 shorter events, 0.1 us)
Async XLA Ops:
  0.0 36.9 %copy-start.12 = (bf16[8,512,256]{2,1,0:T(8,128)(2,1)S(1)}, bf16[8,512,256]{2,1,0:T(8,128)(2,1)}, u32[]{:S(2)}) copy-start(bf16[8,512,256]{2,1,0:T(8,128)(2,1)} %refs_5_.7) | copy-start | bytes 6291460
  0.0 36.9 %copy-start.18 = (bf16[256,256]{1,0:T(8,128)(2,1)S(1)}, bf16[256,256]{1,0:T(8,128)(2,1)}, u32[]{:S(2)}) copy-start(bf16[256,256]{1,0:T(8,128)(2,1)} %q_w.3) | copy-start | bytes 393220
  0.0 36.9 %copy-start.23 = (f32[256]{0:T(256)S(1)}, f32[256]{0:T(256)}, u32[]{:S(2)}) copy-start(f32[256]{0:T(256)} %param.24) | copy-start | bytes 3076
  0.0 36.9 %copy-start.24 = (f32[256]{0:T(256)S(1)}, f32[256]{0:T(256)}, u32[]{:S(2)}) copy-start(f32[256]{0:T(256)} %param.25) | copy-start | bytes 3076
  0.0 36.9 %copy-start.25 = (f32[256]{0:T(256)S(1)}, f32[256]{0:T(256)}, u32[]{:S(2)}) copy-start(f32[256]{0:T(256)} %param.32) | copy-start | bytes 3076
  5.3 7.0 %collective-permute-start = (bf16[1,8,16,512]{3,2,1,0:T(8,128)(2,1)}, bf16[1,8,16,512]{3,2,1,0:T(8,128)(2,1)S(1)}, u32[]{:S(2)}, u32[]{:S(2)}) collective-permute-start(bf16[1,8,16,512]{3,2,1,0:T(8,128)(2,1)} %bitcast.18), channel_id=1, source_target_pairs={{1,0},{0,1},{3,2},{2,3},{5,4},{4,5},{7,6},{6,7},{9,8},{8,9},{11,10... | collective-permute-start | bytes 393224 | tf_op jit(solution)/shard_map/ppermute | solution.py:411
  12.3 0.9 copy-start.7
  13.5 13.2 %collective-permute-start.1 = (bf16[2,8,16,512]{3,2,1,0:T(8,128)(2,1)S(1)}, bf16[2,8,16,512]{3,2,1,0:T(8,128)(2,1)S(1)}, u32[]{:S(2)}, u32[]{:S(2)}) collective-permute-start(bf16[2,8,16,512]{3,2,1,0:T(8,128)(2,1)S(1)} %join.3.refs_0_), channel_id=1, source_target_pairs={{2,0},{3,1},{4,2},{5,3},{6,4},{7,5},{0,6},{1,7},{10,8},{11,9},{12,... | collective-permute-start | bytes 786440 | tf_op jit(solution)/shard_map/ppermute | solution.py:411
  16.4 10.7 %collective-permute-start.2 = (bf16[2,8,16,512]{3,2,1,0:T(8,128)(2,1)S(1)}, bf16[2,8,16,512]{3,2,1,0:T(8,128)(2,1)S(1)}, u32[]{:S(2)}, u32[]{:S(2)}) collective-permute-start(bf16[2,8,16,512]{3,2,1,0:T(8,128)(2,1)S(1)} %join.3.refs_0_), channel_id=1, source_target_pairs={{4,0},{5,1},{6,2},{7,3},{0,4},{1,5},{2,6},{3,7},{12,8},{13,9},{14,... | collective-permute-start | bytes 786440 | tf_op jit(solution)/shard_map/ppermute | solution.py:411
  17.2 13.2 %collective-permute-start.3 = (bf16[2,8,16,512]{3,2,1,0:T(8,128)(2,1)S(1)}, bf16[2,8,16,512]{3,2,1,0:T(8,128)(2,1)S(1)}, u32[]{:S(2)}, u32[]{:S(2)}) collective-permute-start(bf16[2,8,16,512]{3,2,1,0:T(8,128)(2,1)S(1)} %join.3.refs_0_), channel_id=1, source_target_pairs={{6,0},{7,1},{0,2},{1,3},{2,4},{3,5},{4,6},{5,7},{14,8},{15,9},{8,1... | collective-permute-start | bytes 786440 | tf_op jit(solution)/shard_map/ppermute | solution.py:411
  18.1 12.5 %collective-permute-start.4 = (bf16[2,8,16,512]{3,2,1,0:T(8,128)(2,1)S(1)}, bf16[2,8,16,512]{3,2,1,0:T(8,128)(2,1)S(1)}, u32[]{:S(2)}, u32[]{:S(2)}) collective-permute-start(bf16[2,8,16,512]{3,2,1,0:T(8,128)(2,1)S(1)} %join.3.refs_0_), channel_id=1, source_target_pairs={{16,0},{17,1},{18,2},{19,3},{20,4},{21,5},{22,6},{23,7},{24,8},{25... | collective-permute-start | bytes 786440 | tf_op jit(solution)/shard_map/ppermute | solution.py:411
  22.0 15.0 %copy-start.19 = (bf16[256,256]{1,0:T(8,128)(2,1)S(1)}, bf16[256,256]{1,0:T(8,128)(2,1)}, u32[]{:S(2)}) copy-start(bf16[256,256]{1,0:T(8,128)(2,1)} %k_w.3) | copy-start | bytes 393220
  22.0 15.0 %copy-start.20 = (bf16[256,256]{1,0:T(8,128)(2,1)S(1)}, bf16[256,256]{1,0:T(8,128)(2,1)}, u32[]{:S(2)}) copy-start(bf16[256,256]{1,0:T(8,128)(2,1)} %v_w.3) | copy-start | bytes 393220
  22.0 15.0 %copy-start.21 = (bf16[256,256]{1,0:T(8,128)(2,1)S(1)}, bf16[256,256]{1,0:T(8,128)(2,1)}, u32[]{:S(2)}) copy-start(bf16[256,256]{1,0:T(8,128)(2,1)} %g_w.3) | copy-start | bytes 393220
  30.5 20.0 %collective-permute-start.7 = (bf16[2,8,16,512]{3,2,1,0:T(8,128)(2,1)S(1)}, bf16[2,8,16,512]{3,2,1,0:T(8,128)(2,1)S(1)}, u32[]{:S(2)}, u32[]{:S(2)}) collective-permute-start(bf16[2,8,16,512]{3,2,1,0:T(8,128)(2,1)S(1)} %collective-permute-done.4.refs_0_), channel_id=1, source_target_pairs={{2,0},{3,1},{4,2},{5,3},{6,4},{7,5},{0,6},{1,7},{10,8},{11,9},{12,... | collective-permute-start | bytes 786440 | tf_op jit(solution)/shard_map/ppermute | solution.py:411
  31.2 19.3 %collective-permute-start.8 = (bf16[2,8,16,512]{3,2,1,0:T(8,128)(2,1)S(1)}, bf16[2,8,16,512]{3,2,1,0:T(8,128)(2,1)S(1)}, u32[]{:S(2)}, u32[]{:S(2)}) collective-permute-start(bf16[2,8,16,512]{3,2,1,0:T(8,128)(2,1)S(1)} %collective-permute-done.4.refs_0_), channel_id=1, source_target_pairs={{4,0},{5,1},{6,2},{7,3},{0,4},{1,5},{2,6},{3,7},{12,8},{13,9},{14,... | collective-permute-start | bytes 786440 | tf_op jit(solution)/shard_map/ppermute | solution.py:411
  32.0 18.5 %collective-permute-start.9 = (bf16[2,8,16,512]{3,2,1,0:T(8,128)(2,1)S(1)}, bf16[2,8,16,512]{3,2,1,0:T(8,128)(2,1)S(1)}, u32[]{:S(2)}, u32[]{:S(2)}) collective-permute-start(bf16[2,8,16,512]{3,2,1,0:T(8,128)(2,1)S(1)} %collective-permute-done.4.refs_0_), channel_id=1, source_target_pairs={{6,0},{7,1},{0,2},{1,3},{2,4},{3,5},{4,6},{5,7},{14,8},{15,9},{8,1... | collective-permute-start | bytes 786440 | tf_op jit(solution)/shard_map/ppermute | solution.py:411
  32.8 26.8 %collective-permute-start.5 = (bf16[8,8,16,512]{3,2,1,0:T(8,128)(2,1)S(1)}, bf16[8,8,16,512]{3,2,1,0:T(8,128)(2,1)S(1)}, u32[]{:S(2)}, u32[]{:S(2)}) collective-permute-start(bf16[8,8,16,512]{3,2,1,0:T(8,128)(2,1)S(1)} %join.4.refs_8_), channel_id=1, source_target_pairs={{8,0},{9,1},{10,2},{11,3},{12,4},{13,5},{14,6},{15,7},{16,8},{17,9... | collective-permute-start | bytes 3145736 | tf_op jit(solution)/shard_map/ppermute | solution.py:411
  36.9 25.3 %collective-permute-start.6 = (bf16[8,8,16,512]{3,2,1,0:T(8,128)(2,1)S(1)}, bf16[8,8,16,512]{3,2,1,0:T(8,128)(2,1)S(1)}, u32[]{:S(2)}, u32[]{:S(2)}) collective-permute-start(bf16[8,8,16,512]{3,2,1,0:T(8,128)(2,1)S(1)} %join.4.refs_8_), channel_id=1, source_target_pairs={{24,0},{25,1},{26,2},{27,3},{28,4},{29,5},{30,6},{31,7},{0,8},{1,9... | collective-permute-start | bytes 3145736 | tf_op jit(solution)/shard_map/ppermute | solution.py:411
  36.9 4.4 %copy-start.22 = (bf16[256,256]{1,0:T(8,128)(2,1)S(1)}, bf16[256,256]{1,0:T(8,128)(2,1)}, u32[]{:S(2)}) copy-start(bf16[256,256]{1,0:T(8,128)(2,1)} %refs_10_.3) | copy-start | bytes 393220
  37.0 4.4 %copy-start.26 = (f32[256]{0:T(256)S(1)}, f32[256]{0:T(256)}, u32[]{:S(2)}) copy-start(f32[256]{0:T(256)} %param.34) | copy-start | bytes 3076
  41.3 20.8 %copy-start.27 = (f32[8,512,256]{2,1,0:T(8,128)}, f32[8,512,256]{2,1,0:T(8,128)S(1)}, u32[]{:S(2)}) copy-start(f32[8,512,256]{2,1,0:T(8,128)S(1)} %get-tuple-element.20.refs_2_.refs_3_) | copy-start | bytes 12582916
  41.3 20.8 %copy-start.29 = (bf16[8,512,256]{2,1,0:T(8,128)(2,1)}, bf16[8,512,256]{2,1,0:T(8,128)(2,1)S(1)}, u32[]{:S(2)}) copy-start(bf16[8,512,256]{2,1,0:T(8,128)(2,1)S(1)} %get-tuple-element.19.refs_0_.refs_1_) | copy-start | bytes 6291460
  41.3 20.8 %copy-start.31 = (bf16[8,256,512]{2,1,0:T(8,128)(2,1)}, bf16[8,256,512]{2,1,0:T(8,128)(2,1)S(1)}, u32[]{:S(2)}) copy-start(bf16[8,256,512]{2,1,0:T(8,128)(2,1)S(1)} %get-tuple-element.21.refs_6_) | copy-start | bytes 6291460
  41.3 20.8 %copy-start.33 = (bf16[8,512,256]{2,1,0:T(8,128)(2,1)}, bf16[8,512,256]{2,1,0:T(8,128)(2,1)S(1)}, u32[]{:S(2)}) copy-start(bf16[8,512,256]{2,1,0:T(8,128)(2,1)S(1)} %get-tuple-element.22.refs_7_) | copy-start | bytes 6291460
  71.3 1.0 copy-start.14
  72.2 1.0 copy-start.16
  73.3 28.6 %all-to-all-start = ((bf16[32,64,256]{2,1,0:T(8,128)(2,1)}), bf16[32,64,256]{2,1,0:T(8,128)(2,1)S(1)}, u32[]{:S(2)}, u32[]{:S(2)}) async-start(bf16[32,64,256]{2,1,0:T(8,128)(2,1)} %row_attention.6), calls=%async_computation | async-start | bytes 2097152 | tf_op jit(solution)/shard_map/all_to_all | solution.py:442
  81.7 1.6 copy-start.13
  83.3 1.2 copy-start.15
  84.5 1.2 copy-start.17
  85.7 2.2 %copy-start.28 = (f32[8,512,256]{2,1,0:T(8,128)S(1)}, f32[8,512,256]{2,1,0:T(8,128)}, u32[]{:S(2)}) copy-start(f32[8,512,256]{2,1,0:T(8,128)} %copy-done.27) | copy-start | bytes 12582916
  87.9 1.6 copy-start.30
  89.5 1.6 copy-start.32
  91.1 1.6 copy-start.34
  101.8 10.4 %copy-start = (bf16[256,256]{1,0:T(8,128)(2,1)S(1)}, bf16[256,256]{1,0:T(8,128)(2,1)}, u32[]{:S(2)}) copy-start(bf16[256,256]{1,0:T(8,128)(2,1)} %q_w.5) | copy-start | bytes 393220
  101.8 10.4 %copy-start.1 = (bf16[256,256]{1,0:T(8,128)(2,1)S(1)}, bf16[256,256]{1,0:T(8,128)(2,1)}, u32[]{:S(2)}) copy-start(bf16[256,256]{1,0:T(8,128)(2,1)} %k_w.5) | copy-start | bytes 393220
  101.8 10.4 %copy-start.2 = (bf16[256,256]{1,0:T(8,128)(2,1)S(1)}, bf16[256,256]{1,0:T(8,128)(2,1)}, u32[]{:S(2)}) copy-start(bf16[256,256]{1,0:T(8,128)(2,1)} %v_w.5) | copy-start | bytes 393220
  101.8 10.4 %copy-start.8 = (f32[256]{0:T(256)S(1)}, f32[256]{0:T(256)}, u32[]{:S(2)}) copy-start(f32[256]{0:T(256)} %param.35) | copy-start | bytes 3076
  101.8 10.4 %copy-start.9 = (f32[256]{0:T(256)S(1)}, f32[256]{0:T(256)}, u32[]{:S(2)}) copy-start(f32[256]{0:T(256)} %param.36) | copy-start | bytes 3076
  101.8 10.4 %copy-start.10 = (f32[256]{0:T(256)S(1)}, f32[256]{0:T(256)}, u32[]{:S(2)}) copy-start(f32[256]{0:T(256)} %param.41) | copy-start | bytes 3076
  101.8 10.4 %copy-start.11 = (f32[256]{0:T(256)S(1)}, f32[256]{0:T(256)}, u32[]{:S(2)}) copy-start(f32[256]{0:T(256)} %param.43) | copy-start | bytes 3076
  101.9 27.6 %all-to-all-start.1 = ((bf16[32,64,256]{2,1,0:T(8,128)(2,1)}), bf16[32,64,256]{2,1,0:T(8,128)(2,1)}, u32[]{:S(2)}, u32[]{:S(2)}) async-start(bf16[32,64,256]{2,1,0:T(8,128)(2,1)} %row_attention.7), calls=%async_computation.1 | async-start | bytes 2097152 | tf_op jit(solution)/shard_map/all_to_all | solution.py:442
  112.3 0.9 copy-start.3
  113.2 0.9 copy-start.5
  129.5 0.9 copy-start.4
  130.4 0.9 copy-start.6

commit v4 on v3

--- a/solution.py
+++ b/solution.py
@@ -21,8 +21,9 @@
 NT = (((1,), (1,)), ((), ()))
 
 
-def norm(x, gain, bias):
-    center = jnp.mean(x, axis=-1, keepdims=True)
+def norm(x, gain, bias, center=None):
+    if center is None:
+        center = jnp.mean(x, axis=-1, keepdims=True)
     moved = x - center
     spread = jnp.mean(moved * moved, axis=-1, keepdims=True)
     return moved * lax.rsqrt(spread + EPS) * gain + bias
@@ -83,9 +84,11 @@
 
 def pair_kernel(x_ref, gain_ref, w_ref, out_ref, held):
     step = pl.program_id(0)
-    rows = x_ref.shape[0]
+    rows, _, cz = x_ref.shape
+    mean = jnp.full((cz, cz), 1.0 / cz, jnp.bfloat16)
     for i in range(rows):
-        normed = norm(x_ref[i].astype(jnp.float32), gain_ref[...], 0.0).astype(jnp.bfloat16)
+        x = x_ref[i]
+        normed = norm(x.astype(jnp.float32), gain_ref[...], 0.0, dot(x, mean)).astype(jnp.bfloat16)
         bias = lax.dot_general(w_ref[...], normed, NT, preferred_element_type=jnp.float32)
         for part in range(held.shape[0]):
             low = step * rows // HALF_ROWS * (H * HALF_ROWS) + lax.rem(step * rows, HALF_ROWS) + i
@@ -153,7 +156,7 @@
         ],
         in_specs=[block, vector, vector] + [weight] * 4 + [vector],
         out_specs=[block, turned, block, block],
-        compiler_params=pltpu.CompilerParams(vmem_limit_bytes=24 * MIB),
+        compiler_params=pltpu.CompilerParams(vmem_limit_bytes=56 * MIB),
         cost_estimate=pl.CostEstimate(
             flops=2 * seqs * res * width * width * 4,
             bytes_accessed=x.size * 12,
@@ -306,7 +309,7 @@
             ],
         ),
         input_output_aliases={len(args) + 1 - len(held) + n: n for n in range(len(held))},
-        compiler_params=pltpu.CompilerParams(vmem_limit_bytes=24 * MIB),
+        compiler_params=pltpu.CompilerParams(vmem_limit_bytes=56 * MIB),
         cost_estimate=pl.CostEstimate(
             flops=seqs * H * part_rows * len(blocks) * res * 256 * 16,
             bytes_accessed=8 * 1024 * 1024,
@@ -393,7 +396,7 @@
             pltpu.VMEM((2, GROUP * seqs, seqs), jnp.float32),
             pltpu.VMEM((2, GROUP * seqs, seqs), jnp.bfloat16),
         ],
-        compiler_params=pltpu.CompilerParams(vmem_limit_bytes=24 * MIB),
+        compiler_params=pltpu.CompilerParams(vmem_limit_bytes=56 * MIB),
         name="column_attention",
     )(
         x, gain.reshape(1, -1), bias.reshape(1, -1), q_w, k_w, v_w, g_w, g_b.reshape(1, -1),
@@ -433,7 +436,7 @@
         in_specs=[pl.BlockSpec(memory_space=pl.ANY)] * len(parts),
         out_specs=pl.BlockSpec(memory_space=pl.ANY),
         scratch_shapes=[pltpu.SemaphoreType.DMA((len(parts),))],
-        compiler_params=pltpu.CompilerParams(vmem_limit_bytes=8 * MIB),
+        compiler_params=pltpu.CompilerParams(vmem_limit_bytes=4 * MIB),
         name="join",
     )(*parts)
 
@@ -472,14 +475,17 @@
     here = jnp.stack([me // (NX * NY), me // NY % NX, me % NY]).astype(jnp.int32)
     local = pair_bias(pair_state, pair_norm_gain, pair_weight)[None]
     pair = join(local, fetch(local, y=1))
-    own_plane = join(pair, *(fetch(pair, x=step) for step in (1, 2, 3)))
+    near = [fetch(pair, x=step) for step in (1, 2, 3)]
     far_pair = fetch(pair, z=2)
-    own_plane, far_pair, inputs = lax.optimization_barrier((own_plane, far_pair, alignment))
-    ahead, behind = fetch(own_plane, z=1), fetch(own_plane, z=3)
-    far_plane = join(far_pair, *(fetch(far_pair, x=step) for step in (1, 2, 3)))
+    pair, inputs = lax.optimization_barrier((pair, alignment))
     projected = row_project(
         inputs, row_norm_gain, row_norm_bias, row_query, row_key, row_value, row_gate, row_gate_bias
     )
+    near, projected = lax.optimization_barrier((near, projected))
+    own_plane = join(pair, *near)
+    far_pair, own_plane = lax.optimization_barrier((far_pair, own_plane))
+    ahead, behind = fetch(own_plane, z=1), fetch(own_plane, z=3)
+    far_plane = join(far_pair, *(fetch(far_pair, x=step) for step in (1, 2, 3)))
 
     def attend(blocks, biases, *held):
         return row_attention(

time: 175 us -> 169 us (0.966)
  Pallas kernels: 65.6 us -> 80.3 us
  local copies, waits for them, and re-layouts: 19.1 us -> 5.46 us
  starting transfers between devices: 36.8 us -> 31.6 us
  waiting for transfers between devices: 21 us -> 18.1 us
    unnamed x70 -> x14, local copies, waits for them, and re-layouts: 17.6 us -> 3.95 us
    ppermute x10, waiting for transfers between devices: 14.6 us -> 6.03 us  [fetch(): return lax.ppermute(value, 'dap', pairs)]
    pallas_call x4, Pallas kernels: 36.2 us -> 44.8 us  [row_attention(): pl.pallas_call(functools.partial(row_kernel, blocks), out_shape=[jax.Shap...]
    all_to_all x2, waiting for transfers between devices: 6.36 us -> 12.1 us  [exchange(): return lax.all_to_all(value, 'dap', split_axis=0, concat_axis=0, tiled=True)]
    all_to_all x2, starting transfers between devices: 18.7 us -> 13.6 us  [exchange(): return lax.all_to_all(value, 'dap', split_axis=0, concat_axis=0, tiled=True)]
    pallas_call x2, Pallas kernels: 19.3 us -> 22.9 us  [column_attention(): pl.pallas_call(functools.partial(column_kernel, at_once), grid=(items //...]
    pallas_call x1, Pallas kernels: 4.32 us -> 7.4 us  [row_project(): pl.pallas_call(project_kernel, grid=(seqs // count,), out_shape=[shape((s...]
  transfers between devices with their start and end apart: 12 -> 12, of which waited for: 6 -> 5; matrix products, arithmetic and copies ran while one was open for 0% -> 0% of each run, Pallas kernels for 23% -> 31%
where the time goes in v4:
time: 169 us; the launch traced here: 168 us
  Pallas kernels  80.3 us (48%)
  blocking collectives  31.9 us (19%)
  starting transfers between devices  31.6 us (19%)
  waiting for transfers between devices  18.1 us (11%)
  local copies, waits for them, and re-layouts  5.46 us (3%)
    pallas_call x4, Pallas kernels, row_attention(): pl.pallas_call(functools.partial(row_kernel, blocks), out_shape=[jax.Shap...  44.8 us
    all_to_all x1, blocking collectives, exchange(): return lax.all_to_all(value, 'dap', split_axis=0, concat_axis=0, tiled=True)  31.9 us
    pallas_call x2, Pallas kernels, column_attention(): pl.pallas_call(functools.partial(column_kernel, at_once), grid=(items //...  22.9 us
    ppermute x10, starting transfers between devices, fetch(): return lax.ppermute(value, 'dap', pairs)  18.1 us
    all_to_all x2, starting transfers between devices, exchange(): return lax.all_to_all(value, 'dap', split_axis=0, concat_axis=0, tiled=True)  13.6 us
    all_to_all x2, waiting for transfers between devices, exchange(): return lax.all_to_all(value, 'dap', split_axis=0, concat_axis=0, tiled=True)  12.1 us
    pallas_call x1, Pallas kernels, row_project(): pl.pallas_call(project_kernel, grid=(seqs // count,), out_shape=[shape((s...  7.4 us
    ppermute x10, waiting for transfers between devices, fetch(): return lax.ppermute(value, 'dap', pairs)  6.03 us
  transfers between devices with their start and end apart: 12, of which 5 were waited for; matrix products, arithmetic and copies ran while one was open for 0% of the time, Pallas kernels for 31%

profile of v4, /device:TPU:0, one launch (start us, length us, event | category | flops | bytes accessed | tf_op | source)
XLA Modules:
  0.0 168.3 jit_solution(7329961901384371491)
XLA Ops:
  0.0 4.7 %pair_bias.1 = bf16[8,16,512]{2,1,0:T(8,128)(2,1)} custom-call(bf16[16,512,128]{2,1,0:T(8,128)(2,1)} %x_ref.1, f32[1,128]{1,0:T(1,128)} %bitcast.30, bf16[8,128]{1,0:T(8,128)(2,1)} %bitcast.29), custom_call_target="tpu_custom_call" | custom-call | tf_op jit(solution)/shard_map/pair_bias/pallas_call | solution.py:108
  4.7 3.3 %collective-permute-start = (bf16[1,8,16,512]{3,2,1,0:T(8,128)(2,1)}, bf16[1,8,16,512]{3,2,1,0:T(8,128)(2,1)S(1)}, u32[]{:S(2)}, u32[]{:S(2)}) collective-permute-start(bf16[1,8,16,512]{3,2,1,0:T(8,128)(2,1)} %bitcast.18), channel_id=1, source_target_pairs={{1,0},{0,1},{3,2},{2,3},{5,4},{4,5},{7,6},{6,7},{9,8},{8,9},{11,10... | collective-permute-start | bytes 393224 | tf_op jit(solution)/shard_map/ppermute | solution.py:414
  8.0 3.7 %collective-permute-done.refs_1_ = bf16[1,8,16,512]{3,2,1,0:T(8,128)(2,1)S(1)} collective-permute-done((bf16[1,8,16,512]{3,2,1,0:T(8,128)(2,1)}, bf16[1,8,16,512]{3,2,1,0:T(8,128)(2,1)S(1)}, u32[]{:S(2)}, u32[]{:S(2)}) %collective-permute-start) | collective-permute-done | bytes 131104 | tf_op jit(solution)/shard_map/ppermute | solution.py:414
  11.7 0.9 copy-done.2
  12.6 0.3 join.3.refs_0_
  12.9 2.9 %collective-permute-start.1 = (bf16[2,8,16,512]{3,2,1,0:T(8,128)(2,1)S(1)}, bf16[2,8,16,512]{3,2,1,0:T(8,128)(2,1)S(1)}, u32[]{:S(2)}, u32[]{:S(2)}) collective-permute-start(bf16[2,8,16,512]{3,2,1,0:T(8,128)(2,1)S(1)} %join.3.refs_0_), channel_id=1, source_target_pairs={{2,0},{3,1},{4,2},{5,3},{6,4},{7,5},{0,6},{1,7},{10,8},{11,9},{12,... | collective-permute-start | bytes 786440 | tf_op jit(solution)/shard_map/ppermute | solution.py:414
  15.8 0.8 collective-permute-start.2
  16.6 0.9 collective-permute-start.3
  17.5 3.9 %collective-permute-start.4 = (bf16[2,8,16,512]{3,2,1,0:T(8,128)(2,1)S(1)}, bf16[2,8,16,512]{3,2,1,0:T(8,128)(2,1)S(1)}, u32[]{:S(2)}, u32[]{:S(2)}) collective-permute-start(bf16[2,8,16,512]{3,2,1,0:T(8,128)(2,1)S(1)} %join.3.refs_0_), channel_id=1, source_target_pairs={{16,0},{17,1},{18,2},{19,3},{20,4},{21,5},{22,6},{23,7},{24,8},{25... | collective-permute-start | bytes 786440 | tf_op jit(solution)/shard_map/ppermute | solution.py:414
  21.4 0.6 pad_add_fusion.here_ref
  22.0 7.4 %row_project.1 = (bf16[8,512,256]{2,1,0:T(8,128)(2,1)}, bf16[8,256,512]{2,1,0:T(8,128)(2,1)}, bf16[8,512,256]{2,1,0:T(8,128)(2,1)}, f32[8,512,256]{2,1,0:T(8,128)}) custom-call(bf16[8,512,256]{2,1,0:T(8,128)(2,1)} %refs_5_.7, f32[1,256]{1,0:T(1,128)} %bitcast.31, f32[1,256]{1,0:T(1,128)} %bitcast.32, bf16[256,256]{1,0:T(8,128)(2,1)} %q_w.3, ...), custom_call_target="tpu_custom_call" | custom-call | flops 2147483648 | bytes 12582912 | tf_op jit(solution)/shard_map/row_project/pallas_call | solution.py:148
  29.4 0.0 collective-permute-done.1.refs_1_
  29.4 0.0 collective-permute-done.2.refs_2_
  29.4 0.4 collective-permute-done.3.refs_3_
  29.8 0.1 join.4.refs_8_
  29.9 0.0 copy-start
  30.0 0.0 collective-permute-done.4.refs_0_
  30.0 2.1 %collective-permute-start.7 = (bf16[2,8,16,512]{3,2,1,0:T(8,128)(2,1)S(1)}, bf16[2,8,16,512]{3,2,1,0:T(8,128)(2,1)S(1)}, u32[]{:S(2)}, u32[]{:S(2)}) collective-permute-start(bf16[2,8,16,512]{3,2,1,0:T(8,128)(2,1)S(1)} %collective-permute-done.4.refs_0_), channel_id=1, source_target_pairs={{2,0},{3,1},{4,2},{5,3},{6,4},{7,5},{0,6},{1,7},{10,8},{11,9},{12,... | collective-permute-start | bytes 786440 | tf_op jit(solution)/shard_map/ppermute | solution.py:414
  32.0 1.5 collective-permute-start.8
  33.5 0.0 collective-permute-start.9
  33.5 2.8 %collective-permute-start.5 = (bf16[8,8,16,512]{3,2,1,0:T(8,128)(2,1)S(1)}, bf16[8,8,16,512]{3,2,1,0:T(8,128)(2,1)S(1)}, u32[]{:S(2)}, u32[]{:S(2)}) collective-permute-start(bf16[8,8,16,512]{3,2,1,0:T(8,128)(2,1)S(1)} %join.4.refs_8_), channel_id=1, source_target_pairs={{8,0},{9,1},{10,2},{11,3},{12,4},{13,5},{14,6},{15,7},{16,8},{17,9... | collective-permute-start | bytes 3145736 | tf_op jit(solution)/shard_map/ppermute | solution.py:414
  36.3 0.0 collective-permute-start.6
  36.3 0.0 copy-done
  36.3 11.0 %row_attention.4 = (bf16[32,64,256]{2,1,0:T(8,128)(2,1)}, bf16[32,64,256]{2,1,0:T(8,128)(2,1)}) custom-call(s32[3]{0:T(128)} %pad_add_fusion.here_ref, bf16[8,512,256]{2,1,0:T(8,128)(2,1)} %get-tuple-element.31.refs_0_.refs_1_, bf16[8,512,256]{2,1,0:T(8,128)(2,1)} %get-tuple-element.31.refs_0_.refs_1_, f32[8,512,256]{2,1,0:T(8,128)} %get-tuple-element.32.refs_2_.refs_3_, ...), custom_call_target="tpu_custom_call" | custom-call | flops 17179869184 | bytes 8388608 | tf_op jit(solution)/shard_map/row_attention/pallas_call | solution.py:282
  47.3 0.0 collective-permute-done.7.refs_1_
  47.4 0.0 collective-permute-done.8.refs_2_
  47.4 0.0 collective-permute-done.9.refs_3_
  47.4 0.1 join.5.refs_8_
  47.5 0.0 copy-start.1
  47.5 1.0 copy-done.1
  48.6 11.0 %row_attention.5 = (bf16[32,64,256]{2,1,0:T(8,128)(2,1)}, bf16[32,64,256]{2,1,0:T(8,128)(2,1)}) custom-call(s32[3]{0:T(128)} %pad_add_fusion.here_ref, bf16[8,512,256]{2,1,0:T(8,128)(2,1)} %get-tuple-element.31.refs_0_.refs_1_, bf16[8,512,256]{2,1,0:T(8,128)(2,1)} %get-tuple-element.31.refs_0_.refs_1_, ...), custom_call_target="tpu_custom_call", output_to_operand_aliasing={{0}: (12, {}), {1}: (13, {})} | custom-call | flops 17179869184 | bytes 8388608 | tf_op jit(solution)/shard_map/row_attention/pallas_call | solution.py:282
  59.6 0.0 collective-permute-done.5.refs_8_
  59.6 0.0 copy-start.5
  59.6 1.9 %collective-permute-done.6.refs_9_ = bf16[8,8,16,512]{3,2,1,0:T(8,128)(2,1)S(1)} collective-permute-done((bf16[8,8,16,512]{3,2,1,0:T(8,128)(2,1)S(1)}, bf16[8,8,16,512]{3,2,1,0:T(8,128)(2,1)S(1)}, u32[]{:S(2)}, u32[]{:S(2)}) %collective-permute-start.6) | collective-permute-done | bytes 1048608 | tf_op jit(solution)/shard_map/ppermute | solution.py:414
  61.6 0.0 copy-done.5
  61.6 1.0 copy-done.6
  62.6 11.4 %row_attention.6 = bf16[32,64,256]{2,1,0:T(8,128)(2,1)} custom-call(s32[3]{0:T(128)} %pad_add_fusion.here_ref, bf16[8,512,256]{2,1,0:T(8,128)(2,1)} %get-tuple-element.31.refs_0_.refs_1_, bf16[8,512,256]{2,1,0:T(8,128)(2,1)} %get-tuple-element.31.refs_0_.refs_1_, f32[8,512,256]{2,1,0:T(8,128)} %get-tuple-element.32.refs_2_.refs_3_, ...), custom_call_target="tpu_custom_call", output_to_operand_aliasing={{}: (13, {})} | custom-call | flops 17179869184 | bytes 8388608 | tf_op jit(solution)/shard_map/row_attention/pallas_call | solution.py:282
  73.9 9.7 %all-to-all-start = ((bf16[32,64,256]{2,1,0:T(8,128)(2,1)}), bf16[32,64,256]{2,1,0:T(8,128)(2,1)S(1)}, u32[]{:S(2)}, u32[]{:S(2)}) async-start(bf16[32,64,256]{2,1,0:T(8,128)(2,1)} %row_attention.6), calls=%async_computation | async-start | bytes 2097152 | tf_op jit(solution)/shard_map/all_to_all | solution.py:445
  83.6 11.3 %row_attention.7 = bf16[32,64,256]{2,1,0:T(8,128)(2,1)} custom-call(s32[3]{0:T(128)} %pad_add_fusion.here_ref, bf16[8,512,256]{2,1,0:T(8,128)(2,1)} %get-tuple-element.31.refs_0_.refs_1_, bf16[8,512,256]{2,1,0:T(8,128)(2,1)} %get-tuple-element.31.refs_0_.refs_1_, f32[8,512,256]{2,1,0:T(8,128)} %get-tuple-element.32.refs_2_.refs_3_, ...), custom_call_target="tpu_custom_call", output_to_operand_aliasing={{}: (13, {})} | custom-call | flops 17179869184 | bytes 8388608 | tf_op jit(solution)/shard_map/row_attention/pallas_call | solution.py:282
  95.0 6.5 %all-to-all-done.x_ref = bf16[32,64,256]{2,1,0:T(8,128)(2,1)S(1)} async-done(((bf16[32,64,256]{2,1,0:T(8,128)(2,1)}), bf16[32,64,256]{2,1,0:T(8,128)(2,1)S(1)}, u32[]{:S(2)}, u32[]{:S(2)}) %all-to-all-start) | async-done | bytes 1048608 | tf_op jit(solution)/shard_map/all_to_all | solution.py:445
  101.5 3.9 %all-to-all-start.1 = ((bf16[32,64,256]{2,1,0:T(8,128)(2,1)}), bf16[32,64,256]{2,1,0:T(8,128)(2,1)S(1)}, u32[]{:S(2)}, u32[]{:S(2)}) async-start(bf16[32,64,256]{2,1,0:T(8,128)(2,1)} %row_attention.7), calls=%async_computation.1 | async-start | bytes 2097152 | tf_op jit(solution)/shard_map/all_to_all | solution.py:445
  105.4 0.0 copy-done.3
  105.4 11.4 %column_attention.2.refs_0_ = bf16[32,128,256]{2,1,0:T(8,128)(2,1)} custom-call(bf16[32,64,256]{2,1,0:T(8,128)(2,1)} %copy-done.3, f32[1,256]{1,0:T(1,128)} %bitcast.21, f32[1,256]{1,0:T(1,128)} %bitcast.23, bf16[256,256]{1,0:T(8,128)(2,1)} %q_w.5, bf16[256,256]{1,0:T(8,128)(2,1)} %k_w.5, bf16[256,256]{1,0:T(8,128)(2,1)} %v_w.5, bf16[256,256]{1,0:T(8,128)(2,1)} %g_w.5, ...), custom_call_target="tpu_custom_call" | custom-call | tf_op jit(solution)/shard_map/column_attention/pallas_call | solution.py:384
  116.9 5.5 %all-to-all-done.1.x_ref = bf16[32,64,256]{2,1,0:T(8,128)(2,1)S(1)} async-done(((bf16[32,64,256]{2,1,0:T(8,128)(2,1)}), bf16[32,64,256]{2,1,0:T(8,128)(2,1)S(1)}, u32[]{:S(2)}, u32[]{:S(2)}) %all-to-all-start.1) | async-done | bytes 1048608 | tf_op jit(solution)/shard_map/all_to_all | solution.py:445
  122.4 1.0 copy-done.4
  123.4 11.4 %column_attention.3 = bf16[32,128,256]{2,1,0:T(8,128)(2,1)} custom-call(bf16[32,64,256]{2,1,0:T(8,128)(2,1)} %copy-done.4, f32[1,256]{1,0:T(1,128)} %bitcast.22, f32[1,256]{1,0:T(1,128)} %bitcast.24, bf16[256,256]{1,0:T(8,128)(2,1)} %q_w.5, bf16[256,256]{1,0:T(8,128)(2,1)} %k_w.5, bf16[256,256]{1,0:T(8,128)(2,1)} %v_w.5, ...), custom_call_target="tpu_custom_call", output_to_operand_aliasing={{}: (10, {})} | custom-call | tf_op jit(solution)/shard_map/column_attention/pallas_call | solution.py:384
  134.9 31.9 %all_to_all.15 = bf16[32,128,256]{2,1,0:T(8,128)(2,1)S(1)} all-to-all(bf16[32,128,256]{2,1,0:T(8,128)(2,1)} %column_attention.3), channel_id=1, replica_groups=mesh['batch'=4,'dap'=32] {'dap'}, dimensions={0} | all-to-all | bytes 4194304 | tf_op jit(solution)/shard_map/all_to_all | solution.py:445
  166.8 1.5 copy.28
  (4 shorter events, 0.0 us)
Async XLA Ops:
  4.7 7.0 %collective-permute-start = (bf16[1,8,16,512]{3,2,1,0:T(8,128)(2,1)}, bf16[1,8,16,512]{3,2,1,0:T(8,128)(2,1)S(1)}, u32[]{:S(2)}, u32[]{:S(2)}) collective-permute-start(bf16[1,8,16,512]{3,2,1,0:T(8,128)(2,1)} %bitcast.18), channel_id=1, source_target_pairs={{1,0},{0,1},{3,2},{2,3},{5,4},{4,5},{7,6},{6,7},{9,8},{8,9},{11,10... | collective-permute-start | bytes 393224 | tf_op jit(solution)/shard_map/ppermute | solution.py:414
  11.7 0.9 copy-start.2
  12.9 16.5 %collective-permute-start.1 = (bf16[2,8,16,512]{3,2,1,0:T(8,128)(2,1)S(1)}, bf16[2,8,16,512]{3,2,1,0:T(8,128)(2,1)S(1)}, u32[]{:S(2)}, u32[]{:S(2)}) collective-permute-start(bf16[2,8,16,512]{3,2,1,0:T(8,128)(2,1)S(1)} %join.3.refs_0_), channel_id=1, source_target_pairs={{2,0},{3,1},{4,2},{5,3},{6,4},{7,5},{0,6},{1,7},{10,8},{11,9},{12,... | collective-permute-start | bytes 786440 | tf_op jit(solution)/shard_map/ppermute | solution.py:414
  15.8 13.6 %collective-permute-start.2 = (bf16[2,8,16,512]{3,2,1,0:T(8,128)(2,1)S(1)}, bf16[2,8,16,512]{3,2,1,0:T(8,128)(2,1)S(1)}, u32[]{:S(2)}, u32[]{:S(2)}) collective-permute-start(bf16[2,8,16,512]{3,2,1,0:T(8,128)(2,1)S(1)} %join.3.refs_0_), channel_id=1, source_target_pairs={{4,0},{5,1},{6,2},{7,3},{0,4},{1,5},{2,6},{3,7},{12,8},{13,9},{14,... | collective-permute-start | bytes 786440 | tf_op jit(solution)/shard_map/ppermute | solution.py:414
  16.6 13.2 %collective-permute-start.3 = (bf16[2,8,16,512]{3,2,1,0:T(8,128)(2,1)S(1)}, bf16[2,8,16,512]{3,2,1,0:T(8,128)(2,1)S(1)}, u32[]{:S(2)}, u32[]{:S(2)}) collective-permute-start(bf16[2,8,16,512]{3,2,1,0:T(8,128)(2,1)S(1)} %join.3.refs_0_), channel_id=1, source_target_pairs={{6,0},{7,1},{0,2},{1,3},{2,4},{3,5},{4,6},{5,7},{14,8},{15,9},{8,1... | collective-permute-start | bytes 786440 | tf_op jit(solution)/shard_map/ppermute | solution.py:414
  17.5 12.5 %collective-permute-start.4 = (bf16[2,8,16,512]{3,2,1,0:T(8,128)(2,1)S(1)}, bf16[2,8,16,512]{3,2,1,0:T(8,128)(2,1)S(1)}, u32[]{:S(2)}, u32[]{:S(2)}) collective-permute-start(bf16[2,8,16,512]{3,2,1,0:T(8,128)(2,1)S(1)} %join.3.refs_0_), channel_id=1, source_target_pairs={{16,0},{17,1},{18,2},{19,3},{20,4},{21,5},{22,6},{23,7},{24,8},{25... | collective-permute-start | bytes 786440 | tf_op jit(solution)/shard_map/ppermute | solution.py:414
  29.9 6.4 %copy-start = (bf16[8,8,16,512]{3,2,1,0:T(8,128)(2,1)}, bf16[8,8,16,512]{3,2,1,0:T(8,128)(2,1)S(1)}, u32[]{:S(2)}) copy-start(bf16[8,8,16,512]{3,2,1,0:T(8,128)(2,1)S(1)} %join.4.refs_8_) | copy-start | bytes 3145732
  30.0 17.4 %collective-permute-start.7 = (bf16[2,8,16,512]{3,2,1,0:T(8,128)(2,1)S(1)}, bf16[2,8,16,512]{3,2,1,0:T(8,128)(2,1)S(1)}, u32[]{:S(2)}, u32[]{:S(2)}) collective-permute-start(bf16[2,8,16,512]{3,2,1,0:T(8,128)(2,1)S(1)} %collective-permute-done.4.refs_0_), channel_id=1, source_target_pairs={{2,0},{3,1},{4,2},{5,3},{6,4},{7,5},{0,6},{1,7},{10,8},{11,9},{12,... | collective-permute-start | bytes 786440 | tf_op jit(solution)/shard_map/ppermute | solution.py:414
  32.0 15.3 %collective-permute-start.8 = (bf16[2,8,16,512]{3,2,1,0:T(8,128)(2,1)S(1)}, bf16[2,8,16,512]{3,2,1,0:T(8,128)(2,1)S(1)}, u32[]{:S(2)}, u32[]{:S(2)}) collective-permute-start(bf16[2,8,16,512]{3,2,1,0:T(8,128)(2,1)S(1)} %collective-permute-done.4.refs_0_), channel_id=1, source_target_pairs={{4,0},{5,1},{6,2},{7,3},{0,4},{1,5},{2,6},{3,7},{12,8},{13,9},{14,... | collective-permute-start | bytes 786440 | tf_op jit(solution)/shard_map/ppermute | solution.py:414
  33.5 13.8 %collective-permute-start.9 = (bf16[2,8,16,512]{3,2,1,0:T(8,128)(2,1)S(1)}, bf16[2,8,16,512]{3,2,1,0:T(8,128)(2,1)S(1)}, u32[]{:S(2)}, u32[]{:S(2)}) collective-permute-start(bf16[2,8,16,512]{3,2,1,0:T(8,128)(2,1)S(1)} %collective-permute-done.4.refs_0_), channel_id=1, source_target_pairs={{6,0},{7,1},{0,2},{1,3},{2,4},{3,5},{4,6},{5,7},{14,8},{15,9},{8,1... | collective-permute-start | bytes 786440 | tf_op jit(solution)/shard_map/ppermute | solution.py:414
  33.5 26.1 %collective-permute-start.5 = (bf16[8,8,16,512]{3,2,1,0:T(8,128)(2,1)S(1)}, bf16[8,8,16,512]{3,2,1,0:T(8,128)(2,1)S(1)}, u32[]{:S(2)}, u32[]{:S(2)}) collective-permute-start(bf16[8,8,16,512]{3,2,1,0:T(8,128)(2,1)S(1)} %join.4.refs_8_), channel_id=1, source_target_pairs={{8,0},{9,1},{10,2},{11,3},{12,4},{13,5},{14,6},{15,7},{16,8},{17,9... | collective-permute-start | bytes 3145736 | tf_op jit(solution)/shard_map/ppermute | solution.py:414
  36.3 25.3 %collective-permute-start.6 = (bf16[8,8,16,512]{3,2,1,0:T(8,128)(2,1)S(1)}, bf16[8,8,16,512]{3,2,1,0:T(8,128)(2,1)S(1)}, u32[]{:S(2)}, u32[]{:S(2)}) collective-permute-start(bf16[8,8,16,512]{3,2,1,0:T(8,128)(2,1)S(1)} %join.4.refs_8_), channel_id=1, source_target_pairs={{24,0},{25,1},{26,2},{27,3},{28,4},{29,5},{30,6},{31,7},{0,8},{1,9... | collective-permute-start | bytes 3145736 | tf_op jit(solution)/shard_map/ppermute | solution.py:414
  47.5 1.1 copy-start.1
  59.6 1.9 %copy-start.5 = (bf16[8,8,16,512]{3,2,1,0:T(8,128)(2,1)}, bf16[8,8,16,512]{3,2,1,0:T(8,128)(2,1)S(1)}, u32[]{:S(2)}) copy-start(bf16[8,8,16,512]{3,2,1,0:T(8,128)(2,1)S(1)} %collective-permute-done.5.refs_8_) | copy-start | bytes 3145732
  61.6 1.0 copy-start.6
  73.9 27.6 %all-to-all-start = ((bf16[32,64,256]{2,1,0:T(8,128)(2,1)}), bf16[32,64,256]{2,1,0:T(8,128)(2,1)S(1)}, u32[]{:S(2)}, u32[]{:S(2)}) async-start(bf16[32,64,256]{2,1,0:T(8,128)(2,1)} %row_attention.6), calls=%async_computation | async-start | bytes 2097152 | tf_op jit(solution)/shard_map/all_to_all | solution.py:445
  101.5 3.9 %copy-start.3 = (bf16[32,64,256]{2,1,0:T(8,128)(2,1)}, bf16[32,64,256]{2,1,0:T(8,128)(2,1)S(1)}, u32[]{:S(2)}) copy-start(bf16[32,64,256]{2,1,0:T(8,128)(2,1)S(1)} %all-to-all-done.x_ref) | copy-start | bytes 3145732
  101.5 20.9 %all-to-all-start.1 = ((bf16[32,64,256]{2,1,0:T(8,128)(2,1)}), bf16[32,64,256]{2,1,0:T(8,128)(2,1)S(1)}, u32[]{:S(2)}, u32[]{:S(2)}) async-start(bf16[32,64,256]{2,1,0:T(8,128)(2,1)} %row_attention.7), calls=%async_computation.1 | async-start | bytes 2097152 | tf_op jit(solution)/shard_map/all_to_all | solution.py:445
  122.4 1.0 copy-start.4

commit v5 on v4

--- a/solution.py
+++ b/solution.py
@@ -41,7 +41,8 @@
     top = jnp.max(scores, axis=-1, keepdims=True)
     e = jnp.exp(scores - top)
     total = jnp.sum(e, axis=-1, keepdims=True)
-    return (e * (1.0 / total)).astype(jnp.bfloat16)
+    guess = pl.reciprocal(total, approx=True)
+    return (e * (guess * (2.0 - total * guess))).astype(jnp.bfloat16)
 
 
 def head_of_lane():
@@ -78,7 +79,7 @@
     q = (dot(at_queries, q_w[...]) * HEAD ** (-0.5)).astype(jnp.bfloat16)
     k_t = dot(normed, k_w[...]).T.astype(jnp.bfloat16)
     v = dot(normed, v_w[...]).astype(jnp.bfloat16)
-    g = jax.nn.sigmoid(dot(at_queries, g_w[...]) + g_b[...])
+    g = 0.5 * jnp.tanh(0.5 * (dot(at_queries, g_w[...]) + g_b[...])) + 0.5
     return q, k_t, v, g
 
 

time: 169 us -> 170 us (level)
  transfers between devices with their start and end apart: 12 -> 12, of which waited for: 5 -> 5; matrix products, arithmetic and copies ran while one was open for 0% -> 0% of each run, Pallas kernels for 31% -> 32%
where the time goes in v5:
time: 170 us
  Pallas kernels  81.9 us (48%)
  starting transfers between devices  32.2 us (19%)
  blocking collectives  32.1 us (19%)
  waiting for transfers between devices  17.1 us (10%)
  local copies, waits for them, and re-layouts  5.46 us (3%)
    pallas_call x4, Pallas kernels, row_attention(): pl.pallas_call(functools.partial(row_kernel, blocks), out_shape=[jax.Shap...  45.9 us
    all_to_all x1, blocking collectives, exchange(): return lax.all_to_all(value, 'dap', split_axis=0, concat_axis=0, tiled=True)  32.1 us
    pallas_call x2, Pallas kernels, column_attention(): pl.pallas_call(functools.partial(column_kernel, at_once), grid=(items //...  23.2 us
    ppermute x10, starting transfers between devices, fetch(): return lax.ppermute(value, 'dap', pairs)  18.1 us
    all_to_all x2, starting transfers between devices, exchange(): return lax.all_to_all(value, 'dap', split_axis=0, concat_axis=0, tiled=True)  14.2 us
    all_to_all x2, waiting for transfers between devices, exchange(): return lax.all_to_all(value, 'dap', split_axis=0, concat_axis=0, tiled=True)  11.6 us
    pallas_call x1, Pallas kernels, row_project(): pl.pallas_call(project_kernel, grid=(seqs // count,), out_shape=[shape((s...  7.41 us
    ppermute x10, waiting for transfers between devices, fetch(): return lax.ppermute(value, 'dap', pairs)  5.44 us
  transfers between devices with their start and end apart: 12, of which 5 were waited for; matrix products, arithmetic and copies ran while one was open for 0% of the time, Pallas kernels for 32%

profile of v5, /device:TPU:0, one launch (start us, length us, event | category | flops | bytes accessed | tf_op | source)
XLA Modules:
  0.0 169.5 jit_solution(17666891078623411463)
XLA Ops:
  0.0 4.7 %pair_bias.1 = bf16[8,16,512]{2,1,0:T(8,128)(2,1)} custom-call(bf16[16,512,128]{2,1,0:T(8,128)(2,1)} %x_ref.1, f32[1,128]{1,0:T(1,128)} %bitcast.30, bf16[8,128]{1,0:T(8,128)(2,1)} %bitcast.29), custom_call_target="tpu_custom_call" | custom-call | tf_op jit(solution)/shard_map/pair_bias/pallas_call | solution.py:109
  4.7 3.3 %collective-permute-start = (bf16[1,8,16,512]{3,2,1,0:T(8,128)(2,1)}, bf16[1,8,16,512]{3,2,1,0:T(8,128)(2,1)S(1)}, u32[]{:S(2)}, u32[]{:S(2)}) collective-permute-start(bf16[1,8,16,512]{3,2,1,0:T(8,128)(2,1)} %bitcast.18), channel_id=1, source_target_pairs={{1,0},{0,1},{3,2},{2,3},{5,4},{4,5},{7,6},{6,7},{9,8},{8,9},{11,10... | collective-permute-start | bytes 393224 | tf_op jit(solution)/shard_map/ppermute | solution.py:415
  8.0 3.7 %collective-permute-done.refs_1_ = bf16[1,8,16,512]{3,2,1,0:T(8,128)(2,1)S(1)} collective-permute-done((bf16[1,8,16,512]{3,2,1,0:T(8,128)(2,1)}, bf16[1,8,16,512]{3,2,1,0:T(8,128)(2,1)S(1)}, u32[]{:S(2)}, u32[]{:S(2)}) %collective-permute-start) | collective-permute-done | bytes 131104 | tf_op jit(solution)/shard_map/ppermute | solution.py:415
  11.7 0.9 copy-done.2
  12.6 0.3 join.3.refs_0_
  12.9 2.9 %collective-permute-start.1 = (bf16[2,8,16,512]{3,2,1,0:T(8,128)(2,1)S(1)}, bf16[2,8,16,512]{3,2,1,0:T(8,128)(2,1)S(1)}, u32[]{:S(2)}, u32[]{:S(2)}) collective-permute-start(bf16[2,8,16,512]{3,2,1,0:T(8,128)(2,1)S(1)} %join.3.refs_0_), channel_id=1, source_target_pairs={{2,0},{3,1},{4,2},{5,3},{6,4},{7,5},{0,6},{1,7},{10,8},{11,9},{12,... | collective-permute-start | bytes 786440 | tf_op jit(solution)/shard_map/ppermute | solution.py:415
  15.8 0.8 collective-permute-start.2
  16.6 0.9 collective-permute-start.3
  17.5 3.9 %collective-permute-start.4 = (bf16[2,8,16,512]{3,2,1,0:T(8,128)(2,1)S(1)}, bf16[2,8,16,512]{3,2,1,0:T(8,128)(2,1)S(1)}, u32[]{:S(2)}, u32[]{:S(2)}) collective-permute-start(bf16[2,8,16,512]{3,2,1,0:T(8,128)(2,1)S(1)} %join.3.refs_0_), channel_id=1, source_target_pairs={{16,0},{17,1},{18,2},{19,3},{20,4},{21,5},{22,6},{23,7},{24,8},{25... | collective-permute-start | bytes 786440 | tf_op jit(solution)/shard_map/ppermute | solution.py:415
  21.4 0.6 pad_add_fusion.here_ref
  22.0 7.4 %row_project.1 = (bf16[8,512,256]{2,1,0:T(8,128)(2,1)}, bf16[8,256,512]{2,1,0:T(8,128)(2,1)}, bf16[8,512,256]{2,1,0:T(8,128)(2,1)}, f32[8,512,256]{2,1,0:T(8,128)}) custom-call(bf16[8,512,256]{2,1,0:T(8,128)(2,1)} %refs_5_.7, f32[1,256]{1,0:T(1,128)} %bitcast.31, f32[1,256]{1,0:T(1,128)} %bitcast.32, bf16[256,256]{1,0:T(8,128)(2,1)} %q_w.3, ...), custom_call_target="tpu_custom_call" | custom-call | flops 2147483648 | bytes 12582912 | tf_op jit(solution)/shard_map/row_project/pallas_call | solution.py:149
  29.4 0.0 collective-permute-done.1.refs_1_
  29.4 0.0 collective-permute-done.2.refs_2_
  29.4 0.4 collective-permute-done.3.refs_3_
  29.8 0.1 join.4.refs_8_
  29.9 0.0 copy-start
  30.0 0.0 collective-permute-done.4.refs_0_
  30.0 2.1 %collective-permute-start.7 = (bf16[2,8,16,512]{3,2,1,0:T(8,128)(2,1)S(1)}, bf16[2,8,16,512]{3,2,1,0:T(8,128)(2,1)S(1)}, u32[]{:S(2)}, u32[]{:S(2)}) collective-permute-start(bf16[2,8,16,512]{3,2,1,0:T(8,128)(2,1)S(1)} %collective-permute-done.4.refs_0_), channel_id=1, source_target_pairs={{2,0},{3,1},{4,2},{5,3},{6,4},{7,5},{0,6},{1,7},{10,8},{11,9},{12,... | collective-permute-start | bytes 786440 | tf_op jit(solution)/shard_map/ppermute | solution.py:415
  32.0 1.5 collective-permute-start.8
  33.5 0.0 collective-permute-start.9
  33.5 2.8 %collective-permute-start.5 = (bf16[8,8,16,512]{3,2,1,0:T(8,128)(2,1)S(1)}, bf16[8,8,16,512]{3,2,1,0:T(8,128)(2,1)S(1)}, u32[]{:S(2)}, u32[]{:S(2)}) collective-permute-start(bf16[8,8,16,512]{3,2,1,0:T(8,128)(2,1)S(1)} %join.4.refs_8_), channel_id=1, source_target_pairs={{8,0},{9,1},{10,2},{11,3},{12,4},{13,5},{14,6},{15,7},{16,8},{17,9... | collective-permute-start | bytes 3145736 | tf_op jit(solution)/shard_map/ppermute | solution.py:415
  36.3 0.0 collective-permute-start.6
  36.3 0.0 copy-done
  36.3 11.3 %row_attention.4 = (bf16[32,64,256]{2,1,0:T(8,128)(2,1)}, bf16[32,64,256]{2,1,0:T(8,128)(2,1)}) custom-call(s32[3]{0:T(128)} %pad_add_fusion.here_ref, bf16[8,512,256]{2,1,0:T(8,128)(2,1)} %get-tuple-element.31.refs_0_.refs_1_, bf16[8,512,256]{2,1,0:T(8,128)(2,1)} %get-tuple-element.31.refs_0_.refs_1_, f32[8,512,256]{2,1,0:T(8,128)} %get-tuple-element.32.refs_2_.refs_3_, ...), custom_call_target="tpu_custom_call" | custom-call | flops 17179869184 | bytes 8388608 | tf_op jit(solution)/shard_map/row_attention/pallas_call | solution.py:283
  47.6 0.0 collective-permute-done.7.refs_1_
  47.6 0.0 collective-permute-done.8.refs_2_
  47.7 0.0 collective-permute-done.9.refs_3_
  47.7 0.1 join.5.refs_8_
  47.8 0.0 copy-start.1
  47.8 1.0 copy-done.1
  48.8 11.3 %row_attention.5 = (bf16[32,64,256]{2,1,0:T(8,128)(2,1)}, bf16[32,64,256]{2,1,0:T(8,128)(2,1)}) custom-call(s32[3]{0:T(128)} %pad_add_fusion.here_ref, bf16[8,512,256]{2,1,0:T(8,128)(2,1)} %get-tuple-element.31.refs_0_.refs_1_, bf16[8,512,256]{2,1,0:T(8,128)(2,1)} %get-tuple-element.31.refs_0_.refs_1_, ...), custom_call_target="tpu_custom_call", output_to_operand_aliasing={{0}: (12, {}), {1}: (13, {})} | custom-call | flops 17179869184 | bytes 8388608 | tf_op jit(solution)/shard_map/row_attention/pallas_call | solution.py:283
  60.2 0.0 collective-permute-done.5.refs_8_
  60.2 0.0 copy-start.5
  60.2 1.4 collective-permute-done.6.refs_9_
  61.6 0.0 copy-done.5
  61.6 1.0 copy-done.6
  62.6 11.7 %row_attention.6 = bf16[32,64,256]{2,1,0:T(8,128)(2,1)} custom-call(s32[3]{0:T(128)} %pad_add_fusion.here_ref, bf16[8,512,256]{2,1,0:T(8,128)(2,1)} %get-tuple-element.31.refs_0_.refs_1_, bf16[8,512,256]{2,1,0:T(8,128)(2,1)} %get-tuple-element.31.refs_0_.refs_1_, f32[8,512,256]{2,1,0:T(8,128)} %get-tuple-element.32.refs_2_.refs_3_, ...), custom_call_target="tpu_custom_call", output_to_operand_aliasing={{}: (13, {})} | custom-call | flops 17179869184 | bytes 8388608 | tf_op jit(solution)/shard_map/row_attention/pallas_call | solution.py:283
  74.2 10.2 %all-to-all-start = ((bf16[32,64,256]{2,1,0:T(8,128)(2,1)}), bf16[32,64,256]{2,1,0:T(8,128)(2,1)S(1)}, u32[]{:S(2)}, u32[]{:S(2)}) async-start(bf16[32,64,256]{2,1,0:T(8,128)(2,1)} %row_attention.6), calls=%async_computation | async-start | bytes 2097152 | tf_op jit(solution)/shard_map/all_to_all | solution.py:446
  84.5 11.6 %row_attention.7 = bf16[32,64,256]{2,1,0:T(8,128)(2,1)} custom-call(s32[3]{0:T(128)} %pad_add_fusion.here_ref, bf16[8,512,256]{2,1,0:T(8,128)(2,1)} %get-tuple-element.31.refs_0_.refs_1_, bf16[8,512,256]{2,1,0:T(8,128)(2,1)} %get-tuple-element.31.refs_0_.refs_1_, f32[8,512,256]{2,1,0:T(8,128)} %get-tuple-element.32.refs_2_.refs_3_, ...), custom_call_target="tpu_custom_call", output_to_operand_aliasing={{}: (13, {})} | custom-call | flops 17179869184 | bytes 8388608 | tf_op jit(solution)/shard_map/row_attention/pallas_call | solution.py:283
  96.1 6.3 %all-to-all-done.x_ref = bf16[32,64,256]{2,1,0:T(8,128)(2,1)S(1)} async-done(((bf16[32,64,256]{2,1,0:T(8,128)(2,1)}), bf16[32,64,256]{2,1,0:T(8,128)(2,1)S(1)}, u32[]{:S(2)}, u32[]{:S(2)}) %all-to-all-start) | async-done | bytes 1048608 | tf_op jit(solution)/shard_map/all_to_all | solution.py:446
  102.4 3.9 %all-to-all-start.1 = ((bf16[32,64,256]{2,1,0:T(8,128)(2,1)}), bf16[32,64,256]{2,1,0:T(8,128)(2,1)S(1)}, u32[]{:S(2)}, u32[]{:S(2)}) async-start(bf16[32,64,256]{2,1,0:T(8,128)(2,1)} %row_attention.7), calls=%async_computation.1 | async-start | bytes 2097152 | tf_op jit(solution)/shard_map/all_to_all | solution.py:446
  106.3 0.0 copy-done.3
  106.3 11.6 %column_attention.2.refs_0_ = bf16[32,128,256]{2,1,0:T(8,128)(2,1)} custom-call(bf16[32,64,256]{2,1,0:T(8,128)(2,1)} %copy-done.3, f32[1,256]{1,0:T(1,128)} %bitcast.21, f32[1,256]{1,0:T(1,128)} %bitcast.23, bf16[256,256]{1,0:T(8,128)(2,1)} %q_w.5, bf16[256,256]{1,0:T(8,128)(2,1)} %k_w.5, bf16[256,256]{1,0:T(8,128)(2,1)} %v_w.5, bf16[256,256]{1,0:T(8,128)(2,1)} %g_w.5, ...), custom_call_target="tpu_custom_call" | custom-call | tf_op jit(solution)/shard_map/column_attention/pallas_call | solution.py:385
  117.9 5.4 %all-to-all-done.1.x_ref = bf16[32,64,256]{2,1,0:T(8,128)(2,1)S(1)} async-done(((bf16[32,64,256]{2,1,0:T(8,128)(2,1)}), bf16[32,64,256]{2,1,0:T(8,128)(2,1)S(1)}, u32[]{:S(2)}, u32[]{:S(2)}) %all-to-all-start.1) | async-done | bytes 1048608 | tf_op jit(solution)/shard_map/all_to_all | solution.py:446
  123.3 1.0 copy-done.4
  124.3 11.6 %column_attention.3 = bf16[32,128,256]{2,1,0:T(8,128)(2,1)} custom-call(bf16[32,64,256]{2,1,0:T(8,128)(2,1)} %copy-done.4, f32[1,256]{1,0:T(1,128)} %bitcast.22, f32[1,256]{1,0:T(1,128)} %bitcast.24, bf16[256,256]{1,0:T(8,128)(2,1)} %q_w.5, bf16[256,256]{1,0:T(8,128)(2,1)} %k_w.5, bf16[256,256]{1,0:T(8,128)(2,1)} %v_w.5, ...), custom_call_target="tpu_custom_call", output_to_operand_aliasing={{}: (10, {})} | custom-call | tf_op jit(solution)/shard_map/column_attention/pallas_call | solution.py:385
  135.9 32.1 %all_to_all.15 = bf16[32,128,256]{2,1,0:T(8,128)(2,1)S(1)} all-to-all(bf16[32,128,256]{2,1,0:T(8,128)(2,1)} %column_attention.3), channel_id=1, replica_groups=mesh['batch'=4,'dap'=32] {'dap'}, dimensions={0} | all-to-all | bytes 4194304 | tf_op jit(solution)/shard_map/all_to_all | solution.py:446
  168.0 1.5 copy.28
  (4 shorter events, 0.0 us)
Async XLA Ops:
  4.7 7.0 %collective-permute-start = (bf16[1,8,16,512]{3,2,1,0:T(8,128)(2,1)}, bf16[1,8,16,512]{3,2,1,0:T(8,128)(2,1)S(1)}, u32[]{:S(2)}, u32[]{:S(2)}) collective-permute-start(bf16[1,8,16,512]{3,2,1,0:T(8,128)(2,1)} %bitcast.18), channel_id=1, source_target_pairs={{1,0},{0,1},{3,2},{2,3},{5,4},{4,5},{7,6},{6,7},{9,8},{8,9},{11,10... | collective-permute-start | bytes 393224 | tf_op jit(solution)/shard_map/ppermute | solution.py:415
  11.7 0.9 copy-start.2
  12.9 16.5 %collective-permute-start.1 = (bf16[2,8,16,512]{3,2,1,0:T(8,128)(2,1)S(1)}, bf16[2,8,16,512]{3,2,1,0:T(8,128)(2,1)S(1)}, u32[]{:S(2)}, u32[]{:S(2)}) collective-permute-start(bf16[2,8,16,512]{3,2,1,0:T(8,128)(2,1)S(1)} %join.3.refs_0_), channel_id=1, source_target_pairs={{2,0},{3,1},{4,2},{5,3},{6,4},{7,5},{0,6},{1,7},{10,8},{11,9},{12,... | collective-permute-start | bytes 786440 | tf_op jit(solution)/shard_map/ppermute | solution.py:415
  15.8 13.6 %collective-permute-start.2 = (bf16[2,8,16,512]{3,2,1,0:T(8,128)(2,1)S(1)}, bf16[2,8,16,512]{3,2,1,0:T(8,128)(2,1)S(1)}, u32[]{:S(2)}, u32[]{:S(2)}) collective-permute-start(bf16[2,8,16,512]{3,2,1,0:T(8,128)(2,1)S(1)} %join.3.refs_0_), channel_id=1, source_target_pairs={{4,0},{5,1},{6,2},{7,3},{0,4},{1,5},{2,6},{3,7},{12,8},{13,9},{14,... | collective-permute-start | bytes 786440 | tf_op jit(solution)/shard_map/ppermute | solution.py:415
  16.6 13.2 %collective-permute-start.3 = (bf16[2,8,16,512]{3,2,1,0:T(8,128)(2,1)S(1)}, bf16[2,8,16,512]{3,2,1,0:T(8,128)(2,1)S(1)}, u32[]{:S(2)}, u32[]{:S(2)}) collective-permute-start(bf16[2,8,16,512]{3,2,1,0:T(8,128)(2,1)S(1)} %join.3.refs_0_), channel_id=1, source_target_pairs={{6,0},{7,1},{0,2},{1,3},{2,4},{3,5},{4,6},{5,7},{14,8},{15,9},{8,1... | collective-permute-start | bytes 786440 | tf_op jit(solution)/shard_map/ppermute | solution.py:415
  17.5 12.5 %collective-permute-start.4 = (bf16[2,8,16,512]{3,2,1,0:T(8,128)(2,1)S(1)}, bf16[2,8,16,512]{3,2,1,0:T(8,128)(2,1)S(1)}, u32[]{:S(2)}, u32[]{:S(2)}) collective-permute-start(bf16[2,8,16,512]{3,2,1,0:T(8,128)(2,1)S(1)} %join.3.refs_0_), channel_id=1, source_target_pairs={{16,0},{17,1},{18,2},{19,3},{20,4},{21,5},{22,6},{23,7},{24,8},{25... | collective-permute-start | bytes 786440 | tf_op jit(solution)/shard_map/ppermute | solution.py:415
  29.9 6.4 %copy-start = (bf16[8,8,16,512]{3,2,1,0:T(8,128)(2,1)}, bf16[8,8,16,512]{3,2,1,0:T(8,128)(2,1)S(1)}, u32[]{:S(2)}) copy-start(bf16[8,8,16,512]{3,2,1,0:T(8,128)(2,1)S(1)} %join.4.refs_8_) | copy-start | bytes 3145732
  30.0 17.7 %collective-permute-start.7 = (bf16[2,8,16,512]{3,2,1,0:T(8,128)(2,1)S(1)}, bf16[2,8,16,512]{3,2,1,0:T(8,128)(2,1)S(1)}, u32[]{:S(2)}, u32[]{:S(2)}) collective-permute-start(bf16[2,8,16,512]{3,2,1,0:T(8,128)(2,1)S(1)} %collective-permute-done.4.refs_0_), channel_id=1, source_target_pairs={{2,0},{3,1},{4,2},{5,3},{6,4},{7,5},{0,6},{1,7},{10,8},{11,9},{12,... | collective-permute-start | bytes 786440 | tf_op jit(solution)/shard_map/ppermute | solution.py:415
  32.0 15.6 %collective-permute-start.8 = (bf16[2,8,16,512]{3,2,1,0:T(8,128)(2,1)S(1)}, bf16[2,8,16,512]{3,2,1,0:T(8,128)(2,1)S(1)}, u32[]{:S(2)}, u32[]{:S(2)}) collective-permute-start(bf16[2,8,16,512]{3,2,1,0:T(8,128)(2,1)S(1)} %collective-permute-done.4.refs_0_), channel_id=1, source_target_pairs={{4,0},{5,1},{6,2},{7,3},{0,4},{1,5},{2,6},{3,7},{12,8},{13,9},{14,... | collective-permute-start | bytes 786440 | tf_op jit(solution)/shard_map/ppermute | solution.py:415
  33.5 14.1 %collective-permute-start.9 = (bf16[2,8,16,512]{3,2,1,0:T(8,128)(2,1)S(1)}, bf16[2,8,16,512]{3,2,1,0:T(8,128)(2,1)S(1)}, u32[]{:S(2)}, u32[]{:S(2)}) collective-permute-start(bf16[2,8,16,512]{3,2,1,0:T(8,128)(2,1)S(1)} %collective-permute-done.4.refs_0_), channel_id=1, source_target_pairs={{6,0},{7,1},{0,2},{1,3},{2,4},{3,5},{4,6},{5,7},{14,8},{15,9},{8,1... | collective-permute-start | bytes 786440 | tf_op jit(solution)/shard_map/ppermute | solution.py:415
  33.5 26.6 %collective-permute-start.5 = (bf16[8,8,16,512]{3,2,1,0:T(8,128)(2,1)S(1)}, bf16[8,8,16,512]{3,2,1,0:T(8,128)(2,1)S(1)}, u32[]{:S(2)}, u32[]{:S(2)}) collective-permute-start(bf16[8,8,16,512]{3,2,1,0:T(8,128)(2,1)S(1)} %join.4.refs_8_), channel_id=1, source_target_pairs={{8,0},{9,1},{10,2},{11,3},{12,4},{13,5},{14,6},{15,7},{16,8},{17,9... | collective-permute-start | bytes 3145736 | tf_op jit(solution)/shard_map/ppermute | solution.py:415
  36.3 25.3 %collective-permute-start.6 = (bf16[8,8,16,512]{3,2,1,0:T(8,128)(2,1)S(1)}, bf16[8,8,16,512]{3,2,1,0:T(8,128)(2,1)S(1)}, u32[]{:S(2)}, u32[]{:S(2)}) collective-permute-start(bf16[8,8,16,512]{3,2,1,0:T(8,128)(2,1)S(1)} %join.4.refs_8_), channel_id=1, source_target_pairs={{24,0},{25,1},{26,2},{27,3},{28,4},{29,5},{30,6},{31,7},{0,8},{1,9... | collective-permute-start | bytes 3145736 | tf_op jit(solution)/shard_map/ppermute | solution.py:415
  47.8 1.1 copy-start.1
  60.2 1.4 copy-start.5
  61.6 1.0 copy-start.6
  74.2 28.1 %all-to-all-start = ((bf16[32,64,256]{2,1,0:T(8,128)(2,1)}), bf16[32,64,256]{2,1,0:T(8,128)(2,1)S(1)}, u32[]{:S(2)}, u32[]{:S(2)}) async-start(bf16[32,64,256]{2,1,0:T(8,128)(2,1)} %row_attention.6), calls=%async_computation | async-start | bytes 2097152 | tf_op jit(solution)/shard_map/all_to_all | solution.py:446
  102.4 3.9 %copy-start.3 = (bf16[32,64,256]{2,1,0:T(8,128)(2,1)}, bf16[32,64,256]{2,1,0:T(8,128)(2,1)S(1)}, u32[]{:S(2)}) copy-start(bf16[32,64,256]{2,1,0:T(8,128)(2,1)S(1)} %all-to-all-done.x_ref) | copy-start | bytes 3145732
  102.4 20.9 %all-to-all-start.1 = ((bf16[32,64,256]{2,1,0:T(8,128)(2,1)}), bf16[32,64,256]{2,1,0:T(8,128)(2,1)S(1)}, u32[]{:S(2)}, u32[]{:S(2)}) async-start(bf16[32,64,256]{2,1,0:T(8,128)(2,1)} %row_attention.7), calls=%async_computation.1 | async-start | bytes 2097152 | tf_op jit(solution)/shard_map/all_to_all | solution.py:446
  123.3 1.0 copy-start.4

commit v6 on v4

--- a/solution.py
+++ b/solution.py
@@ -17,7 +17,8 @@
 HALVES = 2
 HALF_ROWS = 8
 NZ, NX, NY = 4, 4, 2
-DAP = NZ * NX * NY
+PLANE = NX * NY
+DAP = NZ * PLANE
 NT = (((1,), (1,)), ((), ()))
 
 
@@ -82,7 +83,7 @@
     return q, k_t, v, g
 
 
-def pair_kernel(x_ref, gain_ref, w_ref, out_ref, held):
+def pair_kernel(x_ref, gain_ref, w_ref, out_ref, copies_ref, held):
     step = pl.program_id(0)
     rows, _, cz = x_ref.shape
     mean = jnp.full((cz, cz), 1.0 / cz, jnp.bfloat16)
@@ -97,9 +98,10 @@
     @pl.when(step == pl.num_programs(0) - 1)
     def _():
         for part in range(held.shape[0]):
-            out_ref[:, :, lanes_of(part)] = (
-                held[part].astype(jnp.bfloat16).reshape(out_ref.shape[:2] + (LANES,))
-            )
+            value = held[part].astype(jnp.bfloat16).reshape(out_ref.shape[:2] + (LANES,))
+            out_ref[:, :, lanes_of(part)] = value
+            for n in range(PLANE):
+                copies_ref[n, :, :, lanes_of(part)] = value
 
 
 def pair_bias(pair_state, gain, weight):
@@ -108,13 +110,19 @@
     return pl.pallas_call(
         pair_kernel,
         grid=(count // rows,),
-        out_shape=jax.ShapeDtypeStruct((H, count, res), jnp.bfloat16),
+        out_shape=[
+            jax.ShapeDtypeStruct((H, count, res), jnp.bfloat16),
+            jax.ShapeDtypeStruct((PLANE, H, count, res), jnp.bfloat16),
+        ],
         in_specs=[
             pl.BlockSpec((rows, res, cz), lambda i: (i, 0, 0)),
             pl.BlockSpec((1, cz), lambda i: (0, 0)),
             pl.BlockSpec((H, cz), lambda i: (0, 0)),
         ],
-        out_specs=pl.BlockSpec((H, count, res), lambda i: (0, 0, 0)),
+        out_specs=[
+            pl.BlockSpec((H, count, res), lambda i: (0, 0, 0)),
+            pl.BlockSpec((PLANE, H, count, res), lambda i: (0, 0, 0, 0)),
+        ],
         scratch_shapes=[pltpu.VMEM((res // LANES, H * count, LANES), jnp.float32)],
         compiler_params=pltpu.CompilerParams(vmem_limit_bytes=56 * MIB),
         name="pair_bias",
@@ -191,10 +199,6 @@
         q = both(lambda b: q_refs[b][seq, :, lanes])
         held[n % 2] = dot(stacked(q), k_ref[seq, lanes, :])
 
-    def slot(x, y):
-        return lax.rem(x - here_ref[1] + NX, NX) * NY + lax.rem(y - here_ref[2] + NY, NY)
-
-    slots = [slot(x, y) for x in range(NX) for y in range(NY)]
     taken = 4
 
     def soften(n, _):
@@ -204,7 +208,7 @@
                 for first in range(0, owners, taken):
                     piece = (half * H + group * GROUP + two) // 2
                     bias = [
-                        bias_refs[which][slots[o], piece].astype(jnp.float32)
+                        bias_refs[which][o, piece].astype(jnp.float32)
                         for o in range(first, first + taken)
                     ]
                     for i in range(2):
@@ -404,41 +408,16 @@
     )
 
 
-def fetch(value, z=0, x=0, y=0):
-    pairs = []
-    for dz in range(NZ):
-        for dx in range(NX):
-            for dy in range(NY):
-                src = ((dz + z) % NZ * NX + (dx + x) % NX) * NY + (dy + y) % NY
-                pairs.append((src, (dz * NX + dx) * NY + dy))
+def fetch(value, z):
+    pairs = [((n + z * PLANE) % DAP, n) for n in range(DAP)]
     return lax.ppermute(value, "dap", pairs)
 
 
-def join_kernel(*refs):
-    count = len(refs) - 2
-    parts, out_ref, sems = refs[:count], refs[count], refs[count + 1]
-    place, copies = 0, []
-    for n, part in enumerate(parts):
-        size = part.shape[0]
-        copies.append(pltpu.make_async_copy(part, out_ref.at[pl.ds(place, size)], sems.at[n]))
-        place += size
-    for copy in copies:
-        copy.start()
-    for copy in copies:
-        copy.wait()
-
-
-def join(*parts):
-    total = sum(part.shape[0] for part in parts)
-    return pl.pallas_call(
-        join_kernel,
-        out_shape=jax.ShapeDtypeStruct((total,) + parts[0].shape[1:], parts[0].dtype),
-        in_specs=[pl.BlockSpec(memory_space=pl.ANY)] * len(parts),
-        out_specs=pl.BlockSpec(memory_space=pl.ANY),
-        scratch_shapes=[pltpu.SemaphoreType.DMA((len(parts),))],
-        compiler_params=pltpu.CompilerParams(vmem_limit_bytes=4 * MIB),
-        name="join",
-    )(*parts)
+def gather_plane(copies):
+    groups = [[z * PLANE + n for n in range(PLANE)] for z in range(NZ)]
+    return lax.all_to_all(
+        copies, "dap", split_axis=0, concat_axis=0, axis_index_groups=groups, tiled=True
+    )
 
 
 def exchange(value):
@@ -472,20 +451,16 @@
     seqs, res, width = alignment.shape
     own = res // DAP
     me = lax.axis_index("dap")
-    here = jnp.stack([me // (NX * NY), me // NY % NX, me % NY]).astype(jnp.int32)
-    local = pair_bias(pair_state, pair_norm_gain, pair_weight)[None]
-    pair = join(local, fetch(local, y=1))
-    near = [fetch(pair, x=step) for step in (1, 2, 3)]
-    far_pair = fetch(pair, z=2)
-    pair, inputs = lax.optimization_barrier((pair, alignment))
+    here = (me // PLANE).astype(jnp.int32).reshape(1)
+    local, copies = pair_bias(pair_state, pair_norm_gain, pair_weight)
+    far_rows = fetch(local, 2)
+    own_plane = gather_plane(copies)
     projected = row_project(
-        inputs, row_norm_gain, row_norm_bias, row_query, row_key, row_value, row_gate, row_gate_bias
+        alignment, row_norm_gain, row_norm_bias, row_query, row_key, row_value, row_gate, row_gate_bias
     )
-    near, projected = lax.optimization_barrier((near, projected))
-    own_plane = join(pair, *near)
-    far_pair, own_plane = lax.optimization_barrier((far_pair, own_plane))
-    ahead, behind = fetch(own_plane, z=1), fetch(own_plane, z=3)
-    far_plane = join(far_pair, *(fetch(far_pair, x=step) for step in (1, 2, 3)))
+    own_plane, far_rows, projected = lax.optimization_barrier((own_plane, far_rows, projected))
+    ahead, behind = fetch(own_plane, 1), fetch(own_plane, 3)
+    far_plane = gather_plane(jnp.broadcast_to(far_rows, (PLANE,) + far_rows.shape))
 
     def attend(blocks, biases, *held):
         return row_attention(

time: 169 us -> 170 us (level)
  waiting for transfers between devices: 18.1 us -> 23.6 us
  Pallas kernels: 80.3 us -> 77.8 us
    all_to_all x0 -> x2, starting transfers between devices: none -> 11.3 us  [gather_plane(): lax.all_to_all(copies, 'dap', split_axis=0, concat_axis=0, axis_index_gro...]
    ppermute x10 -> x3, starting transfers between devices: 18.1 us -> 8 us  [fetch(): return lax.ppermute(value, 'dap', pairs)]
    all_to_all x0 -> x2, waiting for transfers between devices: none -> 9.15 us  [gather_plane(): lax.all_to_all(copies, 'dap', split_axis=0, concat_axis=0, axis_index_gro...]
    ppermute x10 -> x3, waiting for transfers between devices: 6.03 us -> 0.01 us  [fetch(): return lax.ppermute(value, 'dap', pairs)]
    pallas_call x4, Pallas kernels: 44.8 us -> 42.1 us  [row_attention(): pl.pallas_call(functools.partial(row_kernel, blocks), out_shape=[jax.Shap...]
    all_to_all x2, starting transfers between devices: 13.6 us -> 11.1 us  [exchange(): return lax.all_to_all(value, 'dap', split_axis=0, concat_axis=0, tiled=True)]
    all_to_all x2, waiting for transfers between devices: 12.1 us -> 14.4 us  [exchange(): return lax.all_to_all(value, 'dap', split_axis=0, concat_axis=0, tiled=True)]
    unnamed x14 -> x12, local copies, waits for them, and re-layouts: 3.95 us -> 2.98 us
  transfers between devices with their start and end apart: 12 -> 7, of which waited for: 5 -> 4; matrix products, arithmetic and copies ran while one was open for 0% -> 1% of each run, Pallas kernels for 31% -> 30%
where the time goes in v6:
time: 170 us
  Pallas kernels  77.8 us (46%)
  blocking collectives  32.1 us (19%)
  starting transfers between devices  30.4 us (18%)
  waiting for transfers between devices  23.6 us (14%)
  local copies, waits for them, and re-layouts  5.63 us (3%)
    pallas_call x4, Pallas kernels, row_attention(): pl.pallas_call(functools.partial(row_kernel, blocks), out_shape=[jax.Shap...  42.1 us
    all_to_all x1, blocking collectives, exchange(): return lax.all_to_all(value, 'dap', split_axis=0, concat_axis=0, tiled=True)  32.1 us
    pallas_call x2, Pallas kernels, column_attention(): pl.pallas_call(functools.partial(column_kernel, at_once), grid=(items //...  22.9 us
    all_to_all x2, waiting for transfers between devices, exchange(): return lax.all_to_all(value, 'dap', split_axis=0, concat_axis=0, tiled=True)  14.4 us
    all_to_all x2, starting transfers between devices, gather_plane(): lax.all_to_all(copies, 'dap', split_axis=0, concat_axis=0, axis_index_gro...  11.3 us
    all_to_all x2, starting transfers between devices, exchange(): return lax.all_to_all(value, 'dap', split_axis=0, concat_axis=0, tiled=True)  11.1 us
    all_to_all x2, waiting for transfers between devices, gather_plane(): lax.all_to_all(copies, 'dap', split_axis=0, concat_axis=0, axis_index_gro...  9.15 us
    ppermute x3, starting transfers between devices, fetch(): return lax.ppermute(value, 'dap', pairs)  8 us
  transfers between devices with their start and end apart: 7, of which 4 were waited for; matrix products, arithmetic and copies ran while one was open for 1% of the time, Pallas kernels for 30%

profile of v6, /device:TPU:0, one launch (start us, length us, event | category | flops | bytes accessed | tf_op | source)
XLA Modules:
  0.0 169.6 jit_solution(637605332121582804)
XLA Ops:
  0.0 5.4 %pair_bias.1 = (bf16[8,16,512]{2,1,0:T(8,128)(2,1)}, bf16[8,8,16,512]{3,2,1,0:T(8,128)(2,1)}) custom-call(bf16[16,512,128]{2,1,0:T(8,128)(2,1)} %x_ref.2, f32[1,128]{1,0:T(1,128)} %bitcast.25, bf16[8,128]{1,0:T(8,128)(2,1)} %bitcast.24), custom_call_target="tpu_custom_call" | custom-call | tf_op jit(solution)/shard_map/pair_bias/pallas_call | solution.py:110
  5.4 0.0 copy-start.5
  5.4 7.1 %all-to-all-start = ((bf16[8,8,16,512]{3,2,1,0:T(8,128)(2,1)}), bf16[8,8,16,512]{3,2,1,0:T(8,128)(2,1)S(1)}, u32[]{:S(2)}, u32[]{:S(2)}) async-start(bf16[8,8,16,512]{3,2,1,0:T(8,128)(2,1)} %get-tuple-element.23), calls=%async_computation | async-start | bytes 2097152 | tf_op jit(solution)/shard_map/all_to_all | solution.py:418
  12.5 0.0 copy-done.5
  12.5 4.0 %collective-permute-start = (bf16[8,16,512]{2,1,0:T(8,128)(2,1)S(1)}, bf16[8,16,512]{2,1,0:T(8,128)(2,1)S(1)}, u32[]{:S(2)}, u32[]{:S(2)}) collective-permute-start(bf16[8,16,512]{2,1,0:T(8,128)(2,1)S(1)} %copy-done.5), channel_id=1, source_target_pairs={{16,0},{17,1},{18,2},{19,3},{20,4},{21,5},{22,6},{23,7},{24,8},{25... | collective-permute-start | bytes 393224 | tf_op jit(solution)/shard_map/ppermute | solution.py:413
  16.5 7.4 %row_project.1 = (bf16[8,512,256]{2,1,0:T(8,128)(2,1)}, bf16[8,256,512]{2,1,0:T(8,128)(2,1)}, bf16[8,512,256]{2,1,0:T(8,128)(2,1)}, f32[8,512,256]{2,1,0:T(8,128)}) custom-call(bf16[8,512,256]{2,1,0:T(8,128)(2,1)} %refs_5_.7, f32[1,256]{1,0:T(1,128)} %bitcast.26, f32[1,256]{1,0:T(1,128)} %bitcast.27, bf16[256,256]{1,0:T(8,128)(2,1)} %q_w.3, ...), custom_call_target="tpu_custom_call" | custom-call | flops 2147483648 | bytes 12582912 | tf_op jit(solution)/shard_map/row_project/pallas_call | solution.py:156
  23.9 0.0 collective-permute-done
  23.9 4.4 %all-to-all-done.refs_8_ = bf16[8,8,16,512]{3,2,1,0:T(8,128)(2,1)S(1)} async-done(((bf16[8,8,16,512]{3,2,1,0:T(8,128)(2,1)}), bf16[8,8,16,512]{3,2,1,0:T(8,128)(2,1)S(1)}, u32[]{:S(2)}, u32[]{:S(2)}) %all-to-all-start) | async-done | bytes 1048608 | tf_op jit(solution)/shard_map/all_to_all | solution.py:418
  28.4 0.0 copy-start.2
  28.4 4.0 %collective-permute-start.1 = (bf16[8,8,16,512]{3,2,1,0:T(8,128)(2,1)S(1)}, bf16[8,8,16,512]{3,2,1,0:T(8,128)(2,1)S(1)}, u32[]{:S(2)}, u32[]{:S(2)}) collective-permute-start(bf16[8,8,16,512]{3,2,1,0:T(8,128)(2,1)S(1)} %all-to-all-done.refs_8_), channel_id=1, source_target_pairs={{8,0},{9,1},{10,2},{11,3},{12,4},{13,5},{14,6},{15,7},{16,8},{17,9... | collective-permute-start | bytes 3145736 | tf_op jit(solution)/shard_map/ppermute | solution.py:413
  32.4 0.0 collective-permute-start.2
  32.4 1.1 broadcast_in_dim.3
  33.5 4.1 %all-to-all-start.1 = ((bf16[8,8,16,512]{3,2,1,0:T(8,128)(2,1)}), bf16[8,8,16,512]{3,2,1,0:T(8,128)(2,1)S(1)}, u32[]{:S(2)}, u32[]{:S(2)}) async-start(bf16[8,8,16,512]{3,2,1,0:T(8,128)(2,1)} %broadcast_in_dim.3), calls=%async_computation.1 | async-start | bytes 2097152 | tf_op jit(solution)/shard_map/all_to_all | solution.py:418
  37.7 0.0 copy-done.2
  37.7 10.4 %row_attention.4 = (bf16[32,64,256]{2,1,0:T(8,128)(2,1)}, bf16[32,64,256]{2,1,0:T(8,128)(2,1)}) custom-call(s32[1]{0:T(128)} %bitcast.here_ref, bf16[8,512,256]{2,1,0:T(8,128)(2,1)} %get-tuple-element.29.refs_0_.refs_1_, bf16[8,512,256]{2,1,0:T(8,128)(2,1)} %get-tuple-element.29.refs_0_.refs_1_, f32[8,512,256]{2,1,0:T(8,128)} %get-tuple-element.30.refs_2_.refs_3_, ...), custom_call_target="tpu_custom_call" | custom-call | flops 17179869184 | bytes 8388608 | tf_op jit(solution)/shard_map/row_attention/pallas_call | solution.py:286
  48.1 4.7 %all-to-all-done.1.refs_8_ = bf16[8,8,16,512]{3,2,1,0:T(8,128)(2,1)S(1)} async-done(((bf16[8,8,16,512]{3,2,1,0:T(8,128)(2,1)}), bf16[8,8,16,512]{3,2,1,0:T(8,128)(2,1)S(1)}, u32[]{:S(2)}, u32[]{:S(2)}) %all-to-all-start.1) | async-done | bytes 1048608 | tf_op jit(solution)/shard_map/all_to_all | solution.py:418
  52.8 0.0 copy-start.3
  52.8 1.0 copy-done.3
  53.8 10.3 %row_attention.5 = (bf16[32,64,256]{2,1,0:T(8,128)(2,1)}, bf16[32,64,256]{2,1,0:T(8,128)(2,1)}) custom-call(s32[1]{0:T(128)} %bitcast.here_ref, bf16[8,512,256]{2,1,0:T(8,128)(2,1)} %get-tuple-element.29.refs_0_.refs_1_, bf16[8,512,256]{2,1,0:T(8,128)(2,1)} %get-tuple-element.29.refs_0_.refs_1_, ...), custom_call_target="tpu_custom_call", output_to_operand_aliasing={{0}: (12, {}), {1}: (13, {})} | custom-call | flops 17179869184 | bytes 8388608 | tf_op jit(solution)/shard_map/row_attention/pallas_call | solution.py:286
  64.1 0.0 collective-permute-done.1.refs_8_
  64.1 0.0 copy-start.4
  64.1 0.0 collective-permute-done.2.refs_9_
  64.1 1.0 copy-done.4
  65.1 10.7 %row_attention.6 = bf16[32,64,256]{2,1,0:T(8,128)(2,1)} custom-call(s32[1]{0:T(128)} %bitcast.here_ref, bf16[8,512,256]{2,1,0:T(8,128)(2,1)} %get-tuple-element.29.refs_0_.refs_1_, bf16[8,512,256]{2,1,0:T(8,128)(2,1)} %get-tuple-element.29.refs_0_.refs_1_, f32[8,512,256]{2,1,0:T(8,128)} %get-tuple-element.30.refs_2_.refs_3_, ...), custom_call_target="tpu_custom_call", output_to_operand_aliasing={{}: (13, {})} | custom-call | flops 17179869184 | bytes 8388608 | tf_op jit(solution)/shard_map/row_attention/pallas_call | solution.py:286
  75.8 7.2 %all-to-all-start.2 = ((bf16[32,64,256]{2,1,0:T(8,128)(2,1)}), bf16[32,64,256]{2,1,0:T(8,128)(2,1)S(1)}, u32[]{:S(2)}, u32[]{:S(2)}) async-start(bf16[32,64,256]{2,1,0:T(8,128)(2,1)} %row_attention.6), calls=%async_computation.2 | async-start | bytes 2097152 | tf_op jit(solution)/shard_map/all_to_all | solution.py:424
  83.0 10.7 %row_attention.7 = bf16[32,64,256]{2,1,0:T(8,128)(2,1)} custom-call(s32[1]{0:T(128)} %bitcast.here_ref, bf16[8,512,256]{2,1,0:T(8,128)(2,1)} %get-tuple-element.29.refs_0_.refs_1_, bf16[8,512,256]{2,1,0:T(8,128)(2,1)} %get-tuple-element.29.refs_0_.refs_1_, f32[8,512,256]{2,1,0:T(8,128)} %get-tuple-element.30.refs_2_.refs_3_, ...), custom_call_target="tpu_custom_call", output_to_operand_aliasing={{}: (13, {})} | custom-call | flops 17179869184 | bytes 8388608 | tf_op jit(solution)/shard_map/row_attention/pallas_call | solution.py:286
  93.7 7.9 %all-to-all-done.2.x_ref = bf16[32,64,256]{2,1,0:T(8,128)(2,1)S(1)} async-done(((bf16[32,64,256]{2,1,0:T(8,128)(2,1)}), bf16[32,64,256]{2,1,0:T(8,128)(2,1)S(1)}, u32[]{:S(2)}, u32[]{:S(2)}) %all-to-all-start.2) | async-done | bytes 1048608 | tf_op jit(solution)/shard_map/all_to_all | solution.py:424
  101.6 0.0 copy-start
  101.6 3.9 %all-to-all-start.3 = ((bf16[32,64,256]{2,1,0:T(8,128)(2,1)}), bf16[32,64,256]{2,1,0:T(8,128)(2,1)S(1)}, u32[]{:S(2)}, u32[]{:S(2)}) async-start(bf16[32,64,256]{2,1,0:T(8,128)(2,1)} %row_attention.7), calls=%async_computation.3 | async-start | bytes 2097152 | tf_op jit(solution)/shard_map/all_to_all | solution.py:424
  105.5 0.0 copy-done
  105.6 11.5 %column_attention.2.refs_0_ = bf16[32,128,256]{2,1,0:T(8,128)(2,1)} custom-call(bf16[32,64,256]{2,1,0:T(8,128)(2,1)} %copy-done, f32[1,256]{1,0:T(1,128)} %bitcast.16, f32[1,256]{1,0:T(1,128)} %bitcast.18, bf16[256,256]{1,0:T(8,128)(2,1)} %q_w.5, bf16[256,256]{1,0:T(8,128)(2,1)} %k_w.5, bf16[256,256]{1,0:T(8,128)(2,1)} %v_w.5, bf16[256,256]{1,0:T(8,128)(2,1)} %g_w.5, ...), custom_call_target="tpu_custom_call" | custom-call | tf_op jit(solution)/shard_map/column_attention/pallas_call | solution.py:388
  117.0 6.5 %all-to-all-done.3.x_ref = bf16[32,64,256]{2,1,0:T(8,128)(2,1)S(1)} async-done(((bf16[32,64,256]{2,1,0:T(8,128)(2,1)}), bf16[32,64,256]{2,1,0:T(8,128)(2,1)S(1)}, u32[]{:S(2)}, u32[]{:S(2)}) %all-to-all-start.3) | async-done | bytes 1048608 | tf_op jit(solution)/shard_map/all_to_all | solution.py:424
  123.5 0.0 copy-start.1
  123.5 1.0 copy-done.1
  124.5 11.4 %column_attention.3 = bf16[32,128,256]{2,1,0:T(8,128)(2,1)} custom-call(bf16[32,64,256]{2,1,0:T(8,128)(2,1)} %copy-done.1, f32[1,256]{1,0:T(1,128)} %bitcast.17, f32[1,256]{1,0:T(1,128)} %bitcast.19, bf16[256,256]{1,0:T(8,128)(2,1)} %q_w.5, bf16[256,256]{1,0:T(8,128)(2,1)} %k_w.5, bf16[256,256]{1,0:T(8,128)(2,1)} %v_w.5, ...), custom_call_target="tpu_custom_call", output_to_operand_aliasing={{}: (10, {})} | custom-call | tf_op jit(solution)/shard_map/column_attention/pallas_call | solution.py:388
  136.0 32.1 %all_to_all.25 = bf16[32,128,256]{2,1,0:T(8,128)(2,1)S(1)} all-to-all(bf16[32,128,256]{2,1,0:T(8,128)(2,1)} %column_attention.3), channel_id=1, replica_groups=mesh['batch'=4,'dap'=32] {'dap'}, dimensions={0} | all-to-all | bytes 4194304 | tf_op jit(solution)/shard_map/all_to_all | solution.py:424
  168.1 1.5 copy.28
Async XLA Ops:
  5.4 7.2 %copy-start.5 = (bf16[8,16,512]{2,1,0:T(8,128)(2,1)S(1)}, bf16[8,16,512]{2,1,0:T(8,128)(2,1)}, u32[]{:S(2)}) copy-start(bf16[8,16,512]{2,1,0:T(8,128)(2,1)} %get-tuple-element.24) | copy-start | bytes 393220
  5.4 23.0 %all-to-all-start = ((bf16[8,8,16,512]{3,2,1,0:T(8,128)(2,1)}), bf16[8,8,16,512]{3,2,1,0:T(8,128)(2,1)S(1)}, u32[]{:S(2)}, u32[]{:S(2)}) async-start(bf16[8,8,16,512]{3,2,1,0:T(8,128)(2,1)} %get-tuple-element.23), calls=%async_computation | async-start | bytes 2097152 | tf_op jit(solution)/shard_map/all_to_all | solution.py:418
  12.5 11.4 %collective-permute-start = (bf16[8,16,512]{2,1,0:T(8,128)(2,1)S(1)}, bf16[8,16,512]{2,1,0:T(8,128)(2,1)S(1)}, u32[]{:S(2)}, u32[]{:S(2)}) collective-permute-start(bf16[8,16,512]{2,1,0:T(8,128)(2,1)S(1)} %copy-done.5), channel_id=1, source_target_pairs={{16,0},{17,1},{18,2},{19,3},{20,4},{21,5},{22,6},{23,7},{24,8},{25... | collective-permute-start | bytes 393224 | tf_op jit(solution)/shard_map/ppermute | solution.py:413
  28.4 9.3 %copy-start.2 = (bf16[8,8,16,512]{3,2,1,0:T(8,128)(2,1)}, bf16[8,8,16,512]{3,2,1,0:T(8,128)(2,1)S(1)}, u32[]{:S(2)}) copy-start(bf16[8,8,16,512]{3,2,1,0:T(8,128)(2,1)S(1)} %all-to-all-done.refs_8_) | copy-start | bytes 3145732
  28.4 35.8 %collective-permute-start.1 = (bf16[8,8,16,512]{3,2,1,0:T(8,128)(2,1)S(1)}, bf16[8,8,16,512]{3,2,1,0:T(8,128)(2,1)S(1)}, u32[]{:S(2)}, u32[]{:S(2)}) collective-permute-start(bf16[8,8,16,512]{3,2,1,0:T(8,128)(2,1)S(1)} %all-to-all-done.refs_8_), channel_id=1, source_target_pairs={{8,0},{9,1},{10,2},{11,3},{12,4},{13,5},{14,6},{15,7},{16,8},{17,9... | collective-permute-start | bytes 3145736 | tf_op jit(solution)/shard_map/ppermute | solution.py:413
  32.4 31.7 %collective-permute-start.2 = (bf16[8,8,16,512]{3,2,1,0:T(8,128)(2,1)S(1)}, bf16[8,8,16,512]{3,2,1,0:T(8,128)(2,1)}, u32[]{:S(2)}, u32[]{:S(2)}) collective-permute-start(bf16[8,8,16,512]{3,2,1,0:T(8,128)(2,1)S(1)} %all-to-all-done.refs_8_), channel_id=1, source_target_pairs={{24,0},{25,1},{26,2},{27,3},{28,4},{29,5},{30,6},{31,7},{0,8},{1,9... | collective-permute-start | bytes 3145736 | tf_op jit(solution)/shard_map/ppermute | solution.py:413
  33.5 19.2 %all-to-all-start.1 = ((bf16[8,8,16,512]{3,2,1,0:T(8,128)(2,1)}), bf16[8,8,16,512]{3,2,1,0:T(8,128)(2,1)S(1)}, u32[]{:S(2)}, u32[]{:S(2)}) async-start(bf16[8,8,16,512]{3,2,1,0:T(8,128)(2,1)} %broadcast_in_dim.3), calls=%async_computation.1 | async-start | bytes 2097152 | tf_op jit(solution)/shard_map/all_to_all | solution.py:418
  52.8 1.0 copy-start.3
  64.1 1.0 copy-start.4
  75.8 25.8 %all-to-all-start.2 = ((bf16[32,64,256]{2,1,0:T(8,128)(2,1)}), bf16[32,64,256]{2,1,0:T(8,128)(2,1)S(1)}, u32[]{:S(2)}, u32[]{:S(2)}) async-start(bf16[32,64,256]{2,1,0:T(8,128)(2,1)} %row_attention.6), calls=%async_computation.2 | async-start | bytes 2097152 | tf_op jit(solution)/shard_map/all_to_all | solution.py:424
  101.6 3.9 %copy-start = (bf16[32,64,256]{2,1,0:T(8,128)(2,1)}, bf16[32,64,256]{2,1,0:T(8,128)(2,1)S(1)}, u32[]{:S(2)}) copy-start(bf16[32,64,256]{2,1,0:T(8,128)(2,1)S(1)} %all-to-all-done.2.x_ref) | copy-start | bytes 3145732
  101.6 21.9 %all-to-all-start.3 = ((bf16[32,64,256]{2,1,0:T(8,128)(2,1)}), bf16[32,64,256]{2,1,0:T(8,128)(2,1)S(1)}, u32[]{:S(2)}, u32[]{:S(2)}) async-start(bf16[32,64,256]{2,1,0:T(8,128)(2,1)} %row_attention.7), calls=%async_computation.3 | async-start | bytes 2097152 | tf_op jit(solution)/shard_map/all_to_all | solution.py:424
  123.5 1.0 copy-start.1

commit v7 on v4

--- a/solution.py
+++ b/solution.py
@@ -121,7 +121,14 @@
     )(pair_state, gain.reshape(1, cz), weight.T)
 
 
-def project_kernel(x_ref, gain, bias, q_w, k_w, v_w, g_w, g_b, q_ref, k_ref, v_ref, g_ref):
+def project_kernel(x_ref, gain, bias, q_w, k_w, v_w, g_w, g_b, *refs):
+    later, (q_ref, k_ref, v_ref, g_ref, stack_ref) = refs[:-5], refs[-5:]
+
+    @pl.when(pl.program_id(0) == 0)
+    def _():
+        for n, w_ref in enumerate(later):
+            stack_ref[n] = w_ref[...]
+
     count, res, width = x_ref.shape
     x = x_ref[...].reshape(count * res, width).astype(jnp.float32)
     normed = norm(x, gain[...], bias[...])
@@ -137,7 +144,7 @@
         k_ref[n] = k_t[:, n * res : (n + 1) * res]
 
 
-def row_project(x, gain, bias, q_w, k_w, v_w, g_w, g_b):
+def row_project(x, gain, bias, q_w, k_w, v_w, g_w, g_b, later):
     seqs, res, width = x.shape
     count = 2
     block = pl.BlockSpec((count, res, width), lambda s: (s, 0, 0))
@@ -153,9 +160,12 @@
             shape((seqs, width, res), jnp.bfloat16),
             shape((seqs, res, width), jnp.bfloat16),
             shape((seqs, res, width), jnp.float32),
+            shape((len(later), width, width), jnp.bfloat16),
         ],
-        in_specs=[block, vector, vector] + [weight] * 4 + [vector],
-        out_specs=[block, turned, block, block],
+        in_specs=[block, vector, vector] + [weight] * 4 + [vector] + [weight] * len(later),
+        out_specs=[
+            block, turned, block, block, pl.BlockSpec((len(later), width, width), lambda s: (0, 0, 0))
+        ],
         compiler_params=pltpu.CompilerParams(vmem_limit_bytes=56 * MIB),
         cost_estimate=pl.CostEstimate(
             flops=2 * seqs * res * width * width * 4,
@@ -163,7 +173,7 @@
             transcendentals=x.size * 2,
         ),
         name="row_project",
-    )(x, gain.reshape(1, -1), bias.reshape(1, -1), q_w, k_w, v_w, g_w, g_b.reshape(1, -1))
+    )(x, gain.reshape(1, -1), bias.reshape(1, -1), q_w, k_w, v_w, g_w, g_b.reshape(1, -1), *later)
 
 
 def row_kernel(blocks, here_ref, *refs):
@@ -191,10 +201,6 @@
         q = both(lambda b: q_refs[b][seq, :, lanes])
         held[n % 2] = dot(stacked(q), k_ref[seq, lanes, :])
 
-    def slot(x, y):
-        return lax.rem(x - here_ref[1] + NX, NX) * NY + lax.rem(y - here_ref[2] + NY, NY)
-
-    slots = [slot(x, y) for x in range(NX) for y in range(NY)]
     taken = 4
 
     def soften(n, _):
@@ -204,7 +210,7 @@
                 for first in range(0, owners, taken):
                     piece = (half * H + group * GROUP + two) // 2
                     bias = [
-                        bias_refs[which][slots[o], piece].astype(jnp.float32)
+                        bias_refs[which][o, piece].astype(jnp.float32)
                         for o in range(first, first + taken)
                     ]
                     for i in range(2):
@@ -319,7 +325,8 @@
     )(here, *args)
 
 
-def column_kernel(at_once, x_ref, gain, bias, q_w, k_w, v_w, g_w, g_b, o_w, o_b, *refs):
+def column_kernel(at_once, x_ref, gain, bias, w_ref, g_b, o_b, *refs):
+    q_w, k_w, v_w, g_w, o_w = (w_ref.at[n] for n in range(5))
     out_ref, held, scores, weights = refs[-4:]
     step = pl.program_id(0)
     owners, per, width = x_ref.shape
@@ -374,33 +381,30 @@
             )
 
 
-def column_attention(items, half, before, x, gain, bias, q_w, k_w, v_w, g_w, g_b, o_w, o_b):
+def column_attention(items, half, before, x, gain, bias, weights, g_b, o_b):
     width = x.shape[2]
     seqs = x.size // (items * width)
     at_once = 4
     whole = pl.BlockSpec(x.shape, lambda r: (0, 0, 0))
     vector = pl.BlockSpec((1, width), lambda r: (0, 0))
-    weight = pl.BlockSpec((width, width), lambda r: (0, 0))
+    weight = pl.BlockSpec((5, width, width), lambda r: (0, 0, 0))
     return pl.pallas_call(
         functools.partial(column_kernel, at_once),
         grid=(items // at_once,),
         out_shape=[jax.ShapeDtypeStruct((DAP, HALVES * x.shape[1], width), jnp.bfloat16)],
-        in_specs=[whole, vector, vector]
-        + [weight] * 4
-        + [vector, weight, vector]
+        in_specs=[whole, vector, vector, weight, vector, vector]
         + [pl.BlockSpec(memory_space=pl.ANY)] * len(before),
         out_specs=[pl.BlockSpec(x.shape, lambda r: (0, half, 0))],
-        input_output_aliases={10: 0} if before else {},
+        input_output_aliases={6: 0} if before else {},
         scratch_shapes=[
             pltpu.VMEM((width // LANES, seqs * items, LANES), jnp.float32),
             pltpu.VMEM((2, GROUP * seqs, seqs), jnp.float32),
             pltpu.VMEM((2, GROUP * seqs, seqs), jnp.bfloat16),
         ],
-        compiler_params=pltpu.CompilerParams(vmem_limit_bytes=56 * MIB),
+        compiler_params=pltpu.CompilerParams(vmem_limit_bytes=44 * MIB),
         name="column_attention",
     )(
-        x, gain.reshape(1, -1), bias.reshape(1, -1), q_w, k_w, v_w, g_w, g_b.reshape(1, -1),
-        o_w, o_b.reshape(1, -1), *before,
+        x, gain.reshape(1, -1), bias.reshape(1, -1), weights, g_b.reshape(1, -1), o_b.reshape(1, -1), *before
     )
 
 
@@ -414,31 +418,31 @@
     return lax.ppermute(value, "dap", pairs)
 
 
-def join_kernel(*refs):
-    count = len(refs) - 2
-    parts, out_ref, sems = refs[:count], refs[count], refs[count + 1]
-    place, copies = 0, []
+def join_kernel(axis, here_ref, *refs):
+    parts, (out_ref, sems) = refs[:-2], refs[-2:]
+    size = parts[0].shape[0]
+    copies = []
     for n, part in enumerate(parts):
-        size = part.shape[0]
+        place = lax.rem(here_ref[axis] + n, len(parts)) * size
         copies.append(pltpu.make_async_copy(part, out_ref.at[pl.ds(place, size)], sems.at[n]))
-        place += size
     for copy in copies:
         copy.start()
     for copy in copies:
         copy.wait()
 
 
-def join(*parts):
-    total = sum(part.shape[0] for part in parts)
+def join(here, axis, *parts):
+    anywhere = pl.BlockSpec(memory_space=pl.ANY)
+    shape = (len(parts) * parts[0].shape[0],) + parts[0].shape[1:]
     return pl.pallas_call(
-        join_kernel,
-        out_shape=jax.ShapeDtypeStruct((total,) + parts[0].shape[1:], parts[0].dtype),
-        in_specs=[pl.BlockSpec(memory_space=pl.ANY)] * len(parts),
-        out_specs=pl.BlockSpec(memory_space=pl.ANY),
+        functools.partial(join_kernel, axis),
+        out_shape=jax.ShapeDtypeStruct(shape, parts[0].dtype),
+        in_specs=[pl.BlockSpec(memory_space=pltpu.SMEM)] + [anywhere] * len(parts),
+        out_specs=anywhere,
         scratch_shapes=[pltpu.SemaphoreType.DMA((len(parts),))],
         compiler_params=pltpu.CompilerParams(vmem_limit_bytes=4 * MIB),
         name="join",
-    )(*parts)
+    )(here, *parts)
 
 
 def exchange(value):
@@ -474,18 +478,19 @@
     me = lax.axis_index("dap")
     here = jnp.stack([me // (NX * NY), me // NY % NX, me % NY]).astype(jnp.int32)
     local = pair_bias(pair_state, pair_norm_gain, pair_weight)[None]
-    pair = join(local, fetch(local, y=1))
+    pair = join(here, 2, local, fetch(local, y=1))
     near = [fetch(pair, x=step) for step in (1, 2, 3)]
     far_pair = fetch(pair, z=2)
     pair, inputs = lax.optimization_barrier((pair, alignment))
     projected = row_project(
-        inputs, row_norm_gain, row_norm_bias, row_query, row_key, row_value, row_gate, row_gate_bias
+        inputs, row_norm_gain, row_norm_bias, row_query, row_key, row_value, row_gate, row_gate_bias,
+        (column_query, column_key, column_value, column_gate, column_output),
     )
-    near, projected = lax.optimization_barrier((near, projected))
-    own_plane = join(pair, *near)
+    near, (*projected, weights) = lax.optimization_barrier((near, projected))
+    own_plane = join(here, 1, pair, *near)
     far_pair, own_plane = lax.optimization_barrier((far_pair, own_plane))
     ahead, behind = fetch(own_plane, z=1), fetch(own_plane, z=3)
-    far_plane = join(far_pair, *(fetch(far_pair, x=step) for step in (1, 2, 3)))
+    far_plane = join(here, 1, far_pair, *(fetch(far_pair, x=step) for step in (1, 2, 3)))
 
     def attend(blocks, biases, *held):
         return row_attention(
@@ -507,12 +512,8 @@
             part,
             column_norm_gain,
             column_norm_bias,
-            column_query,
-            column_key,
-            column_value,
-            column_gate,
+            weights,
             column_gate_bias,
-            column_output,
             column_output_bias,
         )
     back = exchange(columns[0]).reshape(DAP, HALVES, seqs, items, width)

time: 169 us -> 169 us (level)
    pallas_call x2, Pallas kernels: 22.9 us -> 19.2 us  [column_attention(): pl.pallas_call(functools.partial(column_kernel, at_once), grid=(items //...]
    unnamed x14 -> x26, local copies, waits for them, and re-layouts: 3.95 us -> 5.15 us
where the time goes in v7:
time: 169 us
  Pallas kernels  78.7 us (47%)
  starting transfers between devices  33.1 us (20%)
  blocking collectives  31 us (18%)
  waiting for transfers between devices  19 us (11%)
  local copies, waits for them, and re-layouts  6.66 us (4%)
    pallas_call x4, Pallas kernels, row_attention(): pl.pallas_call(functools.partial(row_kernel, blocks), out_shape=[jax.Shap...  44.9 us
    all_to_all x1, blocking collectives, exchange(): return lax.all_to_all(value, 'dap', split_axis=0, concat_axis=0, tiled=True)  31 us
    pallas_call x2, Pallas kernels, column_attention(): pl.pallas_call(functools.partial(column_kernel, at_once), grid=(items //...  19.2 us
    ppermute x10, starting transfers between devices, fetch(): return lax.ppermute(value, 'dap', pairs)  18.1 us
    all_to_all x2, starting transfers between devices, exchange(): return lax.all_to_all(value, 'dap', split_axis=0, concat_axis=0, tiled=True)  15 us
    all_to_all x2, waiting for transfers between devices, exchange(): return lax.all_to_all(value, 'dap', split_axis=0, concat_axis=0, tiled=True)  13.3 us
    pallas_call x1, Pallas kernels, row_project(): pl.pallas_call(project_kernel, grid=(seqs // count,), out_shape=[shape((s...  7.66 us
    ppermute x10, waiting for transfers between devices, fetch(): return lax.ppermute(value, 'dap', pairs)  5.65 us
  transfers between devices with their start and end apart: 12, of which 5 were waited for; matrix products, arithmetic and copies ran while one was open for 0% of the time, Pallas kernels for 31%

profile of v7, /device:TPU:0, one launch (start us, length us, event | category | flops | bytes accessed | tf_op | source)
XLA Modules:
  0.0 168.8 jit_solution(8221002753797515003)
XLA Ops:
  0.0 4.7 %pair_bias.1 = bf16[8,16,512]{2,1,0:T(8,128)(2,1)} custom-call(bf16[16,512,128]{2,1,0:T(8,128)(2,1)} %x_ref.1, f32[1,128]{1,0:T(1,128)} %bitcast.30, bf16[8,128]{1,0:T(8,128)(2,1)} %bitcast.29), custom_call_target="tpu_custom_call" | custom-call | tf_op jit(solution)/shard_map/pair_bias/pallas_call | solution.py:108
  4.7 3.3 %collective-permute-start = (bf16[1,8,16,512]{3,2,1,0:T(8,128)(2,1)}, bf16[1,8,16,512]{3,2,1,0:T(8,128)(2,1)S(1)}, u32[]{:S(2)}, u32[]{:S(2)}) collective-permute-start(bf16[1,8,16,512]{3,2,1,0:T(8,128)(2,1)} %bitcast.18), channel_id=1, source_target_pairs={{1,0},{0,1},{3,2},{2,3},{5,4},{4,5},{7,6},{6,7},{9,8},{8,9},{11,10... | collective-permute-start | bytes 393224 | tf_op jit(solution)/shard_map/ppermute | solution.py:418
  8.0 0.1 pad_add_fusion.here_ref
  8.1 3.6 %collective-permute-done.refs_1_ = bf16[1,8,16,512]{3,2,1,0:T(8,128)(2,1)S(1)} collective-permute-done((bf16[1,8,16,512]{3,2,1,0:T(8,128)(2,1)}, bf16[1,8,16,512]{3,2,1,0:T(8,128)(2,1)S(1)}, u32[]{:S(2)}, u32[]{:S(2)}) %collective-permute-start) | collective-permute-done | bytes 131104 | tf_op jit(solution)/shard_map/ppermute | solution.py:418
  11.7 0.9 copy-done.4
  12.6 0.9 join.3.refs_0_
  13.5 2.9 %collective-permute-start.1 = (bf16[2,8,16,512]{3,2,1,0:T(8,128)(2,1)S(1)}, bf16[2,8,16,512]{3,2,1,0:T(8,128)(2,1)S(1)}, u32[]{:S(2)}, u32[]{:S(2)}) collective-permute-start(bf16[2,8,16,512]{3,2,1,0:T(8,128)(2,1)S(1)} %join.3.refs_0_), channel_id=1, source_target_pairs={{2,0},{3,1},{4,2},{5,3},{6,4},{7,5},{0,6},{1,7},{10,8},{11,9},{12,... | collective-permute-start | bytes 786440 | tf_op jit(solution)/shard_map/ppermute | solution.py:418
  16.4 0.8 collective-permute-start.2
  17.2 0.9 collective-permute-start.3
  18.1 3.9 %collective-permute-start.4 = (bf16[2,8,16,512]{3,2,1,0:T(8,128)(2,1)S(1)}, bf16[2,8,16,512]{3,2,1,0:T(8,128)(2,1)S(1)}, u32[]{:S(2)}, u32[]{:S(2)}) collective-permute-start(bf16[2,8,16,512]{3,2,1,0:T(8,128)(2,1)S(1)} %join.3.refs_0_), channel_id=1, source_target_pairs={{16,0},{17,1},{18,2},{19,3},{20,4},{21,5},{22,6},{23,7},{24,8},{25... | collective-permute-start | bytes 786440 | tf_op jit(solution)/shard_map/ppermute | solution.py:418
  22.0 7.7 %row_project.1 = (bf16[8,512,256]{2,1,0:T(8,128)(2,1)}, bf16[8,256,512]{2,1,0:T(8,128)(2,1)}, bf16[8,512,256]{2,1,0:T(8,128)(2,1)}, f32[8,512,256]{2,1,0:T(8,128)}, bf16[5,256,256]{2,1,0:T(8,128)(2,1)}) custom-call(bf16[8,512,256]{2,1,0:T(8,128)(2,1)} %refs_5_.7, f32[1,256]{1,0:T(1,128)} %bitcast.31, f32[1,256]{1,0:T(1,128)} %bitcast.32, ...), custom_call_target="tpu_custom_call" | custom-call | flops 2147483648 | bytes 12582912 | tf_op jit(solution)/shard_map/row_project/pallas_call | solution.py:155
  29.6 0.0 collective-permute-done.1.refs_1_
  29.6 0.0 collective-permute-done.2.refs_2_
  29.6 0.8 collective-permute-done.3.refs_3_
  30.4 0.7 join.4.refs_8_
  31.1 0.0 collective-permute-done.4.refs_0_
  31.1 1.7 collective-permute-start.7
  32.8 1.5 collective-permute-start.8
  34.3 0.0 collective-permute-start.9
  34.3 3.1 %collective-permute-start.5 = (bf16[8,8,16,512]{3,2,1,0:T(8,128)(2,1)S(1)}, bf16[8,8,16,512]{3,2,1,0:T(8,128)(2,1)S(1)}, u32[]{:S(2)}, u32[]{:S(2)}) collective-permute-start(bf16[8,8,16,512]{3,2,1,0:T(8,128)(2,1)S(1)} %join.4.refs_8_), channel_id=1, source_target_pairs={{8,0},{9,1},{10,2},{11,3},{12,4},{13,5},{14,6},{15,7},{16,8},{17,9... | collective-permute-start | bytes 3145736 | tf_op jit(solution)/shard_map/ppermute | solution.py:418
  37.4 0.0 collective-permute-start.6
  37.4 0.0 copy-done.2
  37.4 11.1 %row_attention.4 = (bf16[32,64,256]{2,1,0:T(8,128)(2,1)}, bf16[32,64,256]{2,1,0:T(8,128)(2,1)}) custom-call(s32[3]{0:T(128)} %copy-done.5, bf16[8,512,256]{2,1,0:T(8,128)(2,1)} %get-tuple-element.34.refs_0_.refs_1_, bf16[8,512,256]{2,1,0:T(8,128)(2,1)} %get-tuple-element.34.refs_0_.refs_1_, f32[8,512,256]{2,1,0:T(8,128)} %get-tuple-element.35.refs_2_.refs_3_, ...), custom_call_target="tpu_custom_call" | custom-call | flops 17179869184 | bytes 8388608 | tf_op jit(solution)/shard_map/row_attention/pallas_call | solution.py:288
  48.6 0.0 collective-permute-done.7.refs_1_
  48.6 0.0 collective-permute-done.8.refs_2_
  48.6 0.0 collective-permute-done.9.refs_3_
  48.6 0.7 join.5.refs_8_
  49.3 1.0 copy-done.3
  50.4 11.1 %row_attention.5 = (bf16[32,64,256]{2,1,0:T(8,128)(2,1)}, bf16[32,64,256]{2,1,0:T(8,128)(2,1)}) custom-call(s32[3]{0:T(128)} %copy-done.5, bf16[8,512,256]{2,1,0:T(8,128)(2,1)} %get-tuple-element.34.refs_0_.refs_1_, bf16[8,512,256]{2,1,0:T(8,128)(2,1)} %get-tuple-element.34.refs_0_.refs_1_, ...), custom_call_target="tpu_custom_call", output_to_operand_aliasing={{0}: (12, {}), {1}: (13, {})} | custom-call | flops 17179869184 | bytes 8388608 | tf_op jit(solution)/shard_map/row_attention/pallas_call | solution.py:288
  61.4 0.0 collective-permute-done.5.refs_8_
  61.5 1.2 collective-permute-done.6.refs_9_
  62.7 1.0 copy-done.12
  63.7 11.3 %row_attention.6 = bf16[32,64,256]{2,1,0:T(8,128)(2,1)} custom-call(s32[3]{0:T(128)} %copy-done.5, bf16[8,512,256]{2,1,0:T(8,128)(2,1)} %get-tuple-element.34.refs_0_.refs_1_, bf16[8,512,256]{2,1,0:T(8,128)(2,1)} %get-tuple-element.34.refs_0_.refs_1_, f32[8,512,256]{2,1,0:T(8,128)} %get-tuple-element.35.refs_2_.refs_3_, ...), custom_call_target="tpu_custom_call", output_to_operand_aliasing={{}: (13, {})} | custom-call | flops 17179869184 | bytes 8388608 | tf_op jit(solution)/shard_map/row_attention/pallas_call | solution.py:288
  75.0 10.4 %all-to-all-start = ((bf16[32,64,256]{2,1,0:T(8,128)(2,1)}), bf16[32,64,256]{2,1,0:T(8,128)(2,1)S(1)}, u32[]{:S(2)}, u32[]{:S(2)}) async-start(bf16[32,64,256]{2,1,0:T(8,128)(2,1)} %row_attention.6), calls=%async_computation | async-start | bytes 2097152 | tf_op jit(solution)/shard_map/all_to_all | solution.py:449
  85.4 11.4 %row_attention.7 = bf16[32,64,256]{2,1,0:T(8,128)(2,1)} custom-call(s32[3]{0:T(128)} %copy-done.5, bf16[8,512,256]{2,1,0:T(8,128)(2,1)} %get-tuple-element.34.refs_0_.refs_1_, bf16[8,512,256]{2,1,0:T(8,128)(2,1)} %get-tuple-element.34.refs_0_.refs_1_, f32[8,512,256]{2,1,0:T(8,128)} %get-tuple-element.35.refs_2_.refs_3_, ...), custom_call_target="tpu_custom_call", output_to_operand_aliasing={{}: (13, {})} | custom-call | flops 17179869184 | bytes 8388608 | tf_op jit(solution)/shard_map/row_attention/pallas_call | solution.py:288
  96.8 0.0 copy-start.7
  96.8 0.0 copy-start.8
  96.8 0.0 copy-start.9
  96.8 0.0 copy-start.10
  96.8 6.5 %all-to-all-done.x_ref = bf16[32,64,256]{2,1,0:T(8,128)(2,1)S(1)} async-done(((bf16[32,64,256]{2,1,0:T(8,128)(2,1)}), bf16[32,64,256]{2,1,0:T(8,128)(2,1)S(1)}, u32[]{:S(2)}, u32[]{:S(2)}) %all-to-all-start) | async-done | bytes 1048608 | tf_op jit(solution)/shard_map/all_to_all | solution.py:449
  103.3 4.7 %all-to-all-start.1 = ((bf16[32,64,256]{2,1,0:T(8,128)(2,1)}), bf16[32,64,256]{2,1,0:T(8,128)(2,1)}, u32[]{:S(2)}, u32[]{:S(2)}) async-start(bf16[32,64,256]{2,1,0:T(8,128)(2,1)} %row_attention.7), calls=%async_computation.1 | async-start | bytes 2097152 | tf_op jit(solution)/shard_map/all_to_all | solution.py:449
  108.0 1.1 copy-done
  109.1 9.0 %column_attention.2.refs_0_ = bf16[32,128,256]{2,1,0:T(8,128)(2,1)S(1)} custom-call(bf16[32,64,256]{2,1,0:T(8,128)(2,1)S(1)} %all-to-all-done.x_ref, f32[1,256]{1,0:T(1,128)S(1)} %bitcast.20, f32[1,256]{1,0:T(1,128)S(1)} %bitcast.22, bf16[5,256,256]{2,1,0:T(8,128)(2,1)S(1)} %copy-done, f32[1,256]{1,0:T(1,128)S(1)} %bitcast.24, f32[1,256]{1,0:T(1,128)S(1)} %bitcast.26), custom_call_target="tpu_custom_call" | custom-call | tf_op jit(solution)/shard_map/column_attention/pallas_call | solution.py:391
  118.1 6.8 %all-to-all-done.1.x_ref = bf16[32,64,256]{2,1,0:T(8,128)(2,1)} async-done(((bf16[32,64,256]{2,1,0:T(8,128)(2,1)}), bf16[32,64,256]{2,1,0:T(8,128)(2,1)}, u32[]{:S(2)}, u32[]{:S(2)}) %all-to-all-start.1) | async-done | bytes 1048608 | tf_op jit(solution)/shard_map/all_to_all | solution.py:449
  124.9 1.1 copy-done.1
  126.0 10.2 %column_attention.3 = bf16[32,128,256]{2,1,0:T(8,128)(2,1)S(1)} custom-call(bf16[32,64,256]{2,1,0:T(8,128)(2,1)} %all-to-all-done.1.x_ref, f32[1,256]{1,0:T(1,128)S(1)} %bitcast.21, f32[1,256]{1,0:T(1,128)S(1)} %bitcast.23, bf16[5,256,256]{2,1,0:T(8,128)(2,1)S(1)} %copy-done.1, f32[1,256]{1,0:T(1,128)S(1)} %bitcast.25, ...), custom_call_target="tpu_custom_call", output_to_operand_aliasing={{}: (6, {})} | custom-call | tf_op jit(solution)/shard_map/column_attention/pallas_call | solution.py:391
  136.3 31.0 %all_to_all.15 = bf16[32,128,256]{2,1,0:T(8,128)(2,1)S(1)} all-to-all(bf16[32,128,256]{2,1,0:T(8,128)(2,1)S(1)} %column_attention.3), channel_id=1, replica_groups=mesh['batch'=4,'dap'=32] {'dap'}, dimensions={0} | all-to-all | bytes 4194304 | tf_op jit(solution)/shard_map/all_to_all | solution.py:449
  167.3 1.5 copy.28
  (16 shorter events, 0.0 us)
Async XLA Ops:
  4.7 7.0 %collective-permute-start = (bf16[1,8,16,512]{3,2,1,0:T(8,128)(2,1)}, bf16[1,8,16,512]{3,2,1,0:T(8,128)(2,1)S(1)}, u32[]{:S(2)}, u32[]{:S(2)}) collective-permute-start(bf16[1,8,16,512]{3,2,1,0:T(8,128)(2,1)} %bitcast.18), channel_id=1, source_target_pairs={{1,0},{0,1},{3,2},{2,3},{5,4},{4,5},{7,6},{6,7},{9,8},{8,9},{11,10... | collective-permute-start | bytes 393224 | tf_op jit(solution)/shard_map/ppermute | solution.py:418
  8.1 22.3 %copy-start.5 = (s32[3]{0:T(128)}, s32[3]{0:T(128)S(1)}, u32[]{:S(2)}) copy-start(s32[3]{0:T(128)S(1)} %pad_add_fusion.here_ref) | copy-start | bytes 40
  11.7 0.9 copy-start.4
  13.5 16.1 %collective-permute-start.1 = (bf16[2,8,16,512]{3,2,1,0:T(8,128)(2,1)S(1)}, bf16[2,8,16,512]{3,2,1,0:T(8,128)(2,1)S(1)}, u32[]{:S(2)}, u32[]{:S(2)}) collective-permute-start(bf16[2,8,16,512]{3,2,1,0:T(8,128)(2,1)S(1)} %join.3.refs_0_), channel_id=1, source_target_pairs={{2,0},{3,1},{4,2},{5,3},{6,4},{7,5},{0,6},{1,7},{10,8},{11,9},{12,... | collective-permute-start | bytes 786440 | tf_op jit(solution)/shard_map/ppermute | solution.py:418
  16.4 13.2 %collective-permute-start.2 = (bf16[2,8,16,512]{3,2,1,0:T(8,128)(2,1)S(1)}, bf16[2,8,16,512]{3,2,1,0:T(8,128)(2,1)S(1)}, u32[]{:S(2)}, u32[]{:S(2)}) collective-permute-start(bf16[2,8,16,512]{3,2,1,0:T(8,128)(2,1)S(1)} %join.3.refs_0_), channel_id=1, source_target_pairs={{4,0},{5,1},{6,2},{7,3},{0,4},{1,5},{2,6},{3,7},{12,8},{13,9},{14,... | collective-permute-start | bytes 786440 | tf_op jit(solution)/shard_map/ppermute | solution.py:418
  17.2 13.2 %collective-permute-start.3 = (bf16[2,8,16,512]{3,2,1,0:T(8,128)(2,1)S(1)}, bf16[2,8,16,512]{3,2,1,0:T(8,128)(2,1)S(1)}, u32[]{:S(2)}, u32[]{:S(2)}) collective-permute-start(bf16[2,8,16,512]{3,2,1,0:T(8,128)(2,1)S(1)} %join.3.refs_0_), channel_id=1, source_target_pairs={{6,0},{7,1},{0,2},{1,3},{2,4},{3,5},{4,6},{5,7},{14,8},{15,9},{8,1... | collective-permute-start | bytes 786440 | tf_op jit(solution)/shard_map/ppermute | solution.py:418
  18.1 13.0 %collective-permute-start.4 = (bf16[2,8,16,512]{3,2,1,0:T(8,128)(2,1)S(1)}, bf16[2,8,16,512]{3,2,1,0:T(8,128)(2,1)S(1)}, u32[]{:S(2)}, u32[]{:S(2)}) collective-permute-start(bf16[2,8,16,512]{3,2,1,0:T(8,128)(2,1)S(1)} %join.3.refs_0_), channel_id=1, source_target_pairs={{16,0},{17,1},{18,2},{19,3},{20,4},{21,5},{22,6},{23,7},{24,8},{25... | collective-permute-start | bytes 786440 | tf_op jit(solution)/shard_map/ppermute | solution.py:418
  31.1 6.4 %copy-start.2 = (bf16[8,8,16,512]{3,2,1,0:T(8,128)(2,1)}, bf16[8,8,16,512]{3,2,1,0:T(8,128)(2,1)S(1)}, u32[]{:S(2)}) copy-start(bf16[8,8,16,512]{3,2,1,0:T(8,128)(2,1)S(1)} %join.4.refs_8_) | copy-start | bytes 3145732
  31.1 17.5 %collective-permute-start.7 = (bf16[2,8,16,512]{3,2,1,0:T(8,128)(2,1)S(1)}, bf16[2,8,16,512]{3,2,1,0:T(8,128)(2,1)S(1)}, u32[]{:S(2)}, u32[]{:S(2)}) collective-permute-start(bf16[2,8,16,512]{3,2,1,0:T(8,128)(2,1)S(1)} %collective-permute-done.4.refs_0_), channel_id=1, source_target_pairs={{2,0},{3,1},{4,2},{5,3},{6,4},{7,5},{0,6},{1,7},{10,8},{11,9},{12,... | collective-permute-start | bytes 786440 | tf_op jit(solution)/shard_map/ppermute | solution.py:418
  32.8 15.8 %collective-permute-start.8 = (bf16[2,8,16,512]{3,2,1,0:T(8,128)(2,1)S(1)}, bf16[2,8,16,512]{3,2,1,0:T(8,128)(2,1)S(1)}, u32[]{:S(2)}, u32[]{:S(2)}) collective-permute-start(bf16[2,8,16,512]{3,2,1,0:T(8,128)(2,1)S(1)} %collective-permute-done.4.refs_0_), channel_id=1, source_target_pairs={{4,0},{5,1},{6,2},{7,3},{0,4},{1,5},{2,6},{3,7},{12,8},{13,9},{14,... | collective-permute-start | bytes 786440 | tf_op jit(solution)/shard_map/ppermute | solution.py:418
  34.3 14.3 %collective-permute-start.9 = (bf16[2,8,16,512]{3,2,1,0:T(8,128)(2,1)S(1)}, bf16[2,8,16,512]{3,2,1,0:T(8,128)(2,1)S(1)}, u32[]{:S(2)}, u32[]{:S(2)}) collective-permute-start(bf16[2,8,16,512]{3,2,1,0:T(8,128)(2,1)S(1)} %collective-permute-done.4.refs_0_), channel_id=1, source_target_pairs={{6,0},{7,1},{0,2},{1,3},{2,4},{3,5},{4,6},{5,7},{14,8},{15,9},{8,1... | collective-permute-start | bytes 786440 | tf_op jit(solution)/shard_map/ppermute | solution.py:418
  34.3 27.1 %collective-permute-start.5 = (bf16[8,8,16,512]{3,2,1,0:T(8,128)(2,1)S(1)}, bf16[8,8,16,512]{3,2,1,0:T(8,128)(2,1)S(1)}, u32[]{:S(2)}, u32[]{:S(2)}) collective-permute-start(bf16[8,8,16,512]{3,2,1,0:T(8,128)(2,1)S(1)} %join.4.refs_8_), channel_id=1, source_target_pairs={{8,0},{9,1},{10,2},{11,3},{12,4},{13,5},{14,6},{15,7},{16,8},{17,9... | collective-permute-start | bytes 3145736 | tf_op jit(solution)/shard_map/ppermute | solution.py:418
  37.4 25.3 %collective-permute-start.6 = (bf16[8,8,16,512]{3,2,1,0:T(8,128)(2,1)S(1)}, bf16[8,8,16,512]{3,2,1,0:T(8,128)(2,1)S(1)}, u32[]{:S(2)}, u32[]{:S(2)}) collective-permute-start(bf16[8,8,16,512]{3,2,1,0:T(8,128)(2,1)S(1)} %join.4.refs_8_), channel_id=1, source_target_pairs={{24,0},{25,1},{26,2},{27,3},{28,4},{29,5},{30,6},{31,7},{0,8},{1,9... | collective-permute-start | bytes 3145736 | tf_op jit(solution)/shard_map/ppermute | solution.py:418
  37.4 11.2 %copy-start.6 = (s32[3]{0:T(128)S(1)}, s32[3]{0:T(128)}, u32[]{:S(2)}) copy-start(s32[3]{0:T(128)} %copy-done.5) | copy-start | bytes 40
  49.3 1.1 copy-start.3
  61.4 1.3 copy-start.11
  62.7 1.0 copy-start.12
  75.0 28.3 %all-to-all-start = ((bf16[32,64,256]{2,1,0:T(8,128)(2,1)}), bf16[32,64,256]{2,1,0:T(8,128)(2,1)S(1)}, u32[]{:S(2)}, u32[]{:S(2)}) async-start(bf16[32,64,256]{2,1,0:T(8,128)(2,1)} %row_attention.6), calls=%async_computation | async-start | bytes 2097152 | tf_op jit(solution)/shard_map/all_to_all | solution.py:449
  96.8 11.2 %copy-start.7 = (f32[256]{0:T(256)S(1)}, f32[256]{0:T(256)}, u32[]{:S(2)}) copy-start(f32[256]{0:T(256)} %param.35) | copy-start | bytes 3076
  96.8 11.2 %copy-start.8 = (f32[256]{0:T(256)S(1)}, f32[256]{0:T(256)}, u32[]{:S(2)}) copy-start(f32[256]{0:T(256)} %param.36) | copy-start | bytes 3076
  96.8 11.2 %copy-start.9 = (f32[256]{0:T(256)S(1)}, f32[256]{0:T(256)}, u32[]{:S(2)}) copy-start(f32[256]{0:T(256)} %param.41) | copy-start | bytes 3076
  96.8 11.2 %copy-start.10 = (f32[256]{0:T(256)S(1)}, f32[256]{0:T(256)}, u32[]{:S(2)}) copy-start(f32[256]{0:T(256)} %param.43) | copy-start | bytes 3076
  103.3 21.7 %all-to-all-start.1 = ((bf16[32,64,256]{2,1,0:T(8,128)(2,1)}), bf16[32,64,256]{2,1,0:T(8,128)(2,1)}, u32[]{:S(2)}, u32[]{:S(2)}) async-start(bf16[32,64,256]{2,1,0:T(8,128)(2,1)} %row_attention.7), calls=%async_computation.1 | async-start | bytes 2097152 | tf_op jit(solution)/shard_map/all_to_all | solution.py:449
  108.0 1.1 copy-start
  124.9 1.1 copy-start.1

commit v8 on v4

--- a/solution.py
+++ b/solution.py
@@ -156,7 +156,7 @@
         ],
         in_specs=[block, vector, vector] + [weight] * 4 + [vector],
         out_specs=[block, turned, block, block],
-        compiler_params=pltpu.CompilerParams(vmem_limit_bytes=56 * MIB),
+        compiler_params=pltpu.CompilerParams(vmem_limit_bytes=24 * MIB),
         cost_estimate=pl.CostEstimate(
             flops=2 * seqs * res * width * width * 4,
             bytes_accessed=x.size * 12,
@@ -164,6 +164,20 @@
         ),
         name="row_project",
     )(x, gain.reshape(1, -1), bias.reshape(1, -1), q_w, k_w, v_w, g_w, g_b.reshape(1, -1))
+
+
+def stack_kernel(*refs):
+    for n, ref in enumerate(refs[:-1]):
+        refs[-1][n] = ref[...]
+
+
+def stack(*weights):
+    return pl.pallas_call(
+        stack_kernel,
+        out_shape=jax.ShapeDtypeStruct((len(weights),) + weights[0].shape, weights[0].dtype),
+        compiler_params=pltpu.CompilerParams(vmem_limit_bytes=56 * MIB),
+        name="stack",
+    )(*weights)
 
 
 def row_kernel(blocks, here_ref, *refs):
@@ -195,7 +209,7 @@
         return lax.rem(x - here_ref[1] + NX, NX) * NY + lax.rem(y - here_ref[2] + NY, NY)
 
     slots = [slot(x, y) for x in range(NX) for y in range(NY)]
-    taken = 4
+    taken = 2
 
     def soften(n, _):
         _, group, _ = place(n)
@@ -257,7 +271,7 @@
                 copy.wait()
 
 
-def row_attention(blocks, here, q, k, v, g, x, biases, o_w, o_b, held):
+def row_attention(grant, blocks, here, q, k, v, g, x, biases, o_w, o_b, held):
     seqs, res, width = x.shape
     own = res // DAP
     part_rows = DAP // NZ * HALF_ROWS
@@ -309,7 +323,7 @@
             ],
         ),
         input_output_aliases={len(args) + 1 - len(held) + n: n for n in range(len(held))},
-        compiler_params=pltpu.CompilerParams(vmem_limit_bytes=56 * MIB),
+        compiler_params=pltpu.CompilerParams(vmem_limit_bytes=grant * MIB),
         cost_estimate=pl.CostEstimate(
             flops=seqs * H * part_rows * len(blocks) * res * 256 * 16,
             bytes_accessed=8 * 1024 * 1024,
@@ -319,7 +333,8 @@
     )(here, *args)
 
 
-def column_kernel(at_once, x_ref, gain, bias, q_w, k_w, v_w, g_w, g_b, o_w, o_b, *refs):
+def column_kernel(at_once, x_ref, gain, bias, w_ref, g_b, o_b, *refs):
+    q_w, k_w, v_w, g_w, o_w = (w_ref.at[n] for n in range(5))
     out_ref, held, scores, weights = refs[-4:]
     step = pl.program_id(0)
     owners, per, width = x_ref.shape
@@ -348,8 +363,8 @@
         scores[n % 2] = dot(stacked(q[rows, lanes]), k_t[lanes, rows])
 
     def soften(n, _):
-        for low in range(0, GROUP * seqs, 64):
-            weights[n % 2, low : low + 64] = softmax_rounded(scores[n % 2, low : low + 64])
+        for low in range(0, GROUP * seqs, 32):
+            weights[n % 2, low : low + 32] = softmax_rounded(scores[n % 2, low : low + 32])
 
     def average(n, _):
         rows, lanes = place(n)
@@ -374,33 +389,30 @@
             )
 
 
-def column_attention(items, half, before, x, gain, bias, q_w, k_w, v_w, g_w, g_b, o_w, o_b):
+def column_attention(items, half, before, x, gain, bias, weights, g_b, o_b):
     width = x.shape[2]
     seqs = x.size // (items * width)
     at_once = 4
     whole = pl.BlockSpec(x.shape, lambda r: (0, 0, 0))
     vector = pl.BlockSpec((1, width), lambda r: (0, 0))
-    weight = pl.BlockSpec((width, width), lambda r: (0, 0))
+    weight = pl.BlockSpec((5, width, width), lambda r: (0, 0, 0))
     return pl.pallas_call(
         functools.partial(column_kernel, at_once),
         grid=(items // at_once,),
         out_shape=[jax.ShapeDtypeStruct((DAP, HALVES * x.shape[1], width), jnp.bfloat16)],
-        in_specs=[whole, vector, vector]
-        + [weight] * 4
-        + [vector, weight, vector]
+        in_specs=[whole, vector, vector, weight, vector, vector]
         + [pl.BlockSpec(memory_space=pl.ANY)] * len(before),
         out_specs=[pl.BlockSpec(x.shape, lambda r: (0, half, 0))],
-        input_output_aliases={10: 0} if before else {},
+        input_output_aliases={6: 0} if before else {},
         scratch_shapes=[
             pltpu.VMEM((width // LANES, seqs * items, LANES), jnp.float32),
             pltpu.VMEM((2, GROUP * seqs, seqs), jnp.float32),
             pltpu.VMEM((2, GROUP * seqs, seqs), jnp.bfloat16),
         ],
-        compiler_params=pltpu.CompilerParams(vmem_limit_bytes=56 * MIB),
+        compiler_params=pltpu.CompilerParams(vmem_limit_bytes=44 * MIB),
         name="column_attention",
     )(
-        x, gain.reshape(1, -1), bias.reshape(1, -1), q_w, k_w, v_w, g_w, g_b.reshape(1, -1),
-        o_w, o_b.reshape(1, -1), *before,
+        x, gain.reshape(1, -1), bias.reshape(1, -1), weights, g_b.reshape(1, -1), o_b.reshape(1, -1), *before
     )
 
 
@@ -477,25 +489,25 @@
     pair = join(local, fetch(local, y=1))
     near = [fetch(pair, x=step) for step in (1, 2, 3)]
     far_pair = fetch(pair, z=2)
-    pair, inputs = lax.optimization_barrier((pair, alignment))
+    weights = stack(column_query, column_key, column_value, column_gate, column_output)
+    near, weights = lax.optimization_barrier((near, weights))
+    own_plane = join(pair, *near)
+    own_plane, far_pair, inputs = lax.optimization_barrier((own_plane, far_pair, alignment))
+    ahead, behind = fetch(own_plane, z=1), fetch(own_plane, z=3)
+    far_plane = join(far_pair, *(fetch(far_pair, x=step) for step in (1, 2, 3)))
     projected = row_project(
         inputs, row_norm_gain, row_norm_bias, row_query, row_key, row_value, row_gate, row_gate_bias
     )
-    near, projected = lax.optimization_barrier((near, projected))
-    own_plane = join(pair, *near)
-    far_pair, own_plane = lax.optimization_barrier((far_pair, own_plane))
-    ahead, behind = fetch(own_plane, z=1), fetch(own_plane, z=3)
-    far_plane = join(far_pair, *(fetch(far_pair, x=step) for step in (1, 2, 3)))
-
-    def attend(blocks, biases, *held):
+
+    def attend(blocks, biases, *held, grant=24):
         return row_attention(
-            blocks, here, *projected, alignment, biases, row_output, row_output_bias, held
+            grant, blocks, here, *projected, alignment, biases, row_output, row_output_bias, held
         )
 
     after = attend(((0, 0, 0), (0, 1, 0)), [own_plane])
     after = attend(((2, 0, 0), (2, 1, 0)), [far_plane], *after)
     first = attend(((1, 0, 0), (3, 0, 1)), [ahead, behind], after[0])[0]
-    second = attend(((1, 1, 0), (3, 1, 1)), [ahead, behind], after[1])[0]
+    second = attend(((1, 1, 0), (3, 1, 1)), [ahead, behind], after[1], grant=56)[0]
     first, second = lax.optimization_barrier((exchange(first), second))
     items = own // HALVES
     columns = ()
@@ -507,12 +519,8 @@
             part,
             column_norm_gain,
             column_norm_bias,
-            column_query,
-            column_key,
-            column_value,
-            column_gate,
+            weights,
             column_gate_bias,
-            column_output,
             column_output_bias,
         )
     back = exchange(columns[0]).reshape(DAP, HALVES, seqs, items, width)

time: 169 us -> 165 us (0.976)
  Pallas kernels: 80.3 us -> 69.3 us
  waiting for transfers between devices: 18.1 us -> 24.4 us
    pallas_call x4, Pallas kernels: 44.8 us -> 38.4 us  [row_attention(): pl.pallas_call(functools.partial(row_kernel, blocks), out_shape=[jax.Shap...]
    ppermute x10, waiting for transfers between devices: 6.03 us -> 11.3 us  [fetch(): return lax.ppermute(value, 'dap', pairs)]
    pallas_call x2, Pallas kernels: 22.9 us -> 19.2 us  [column_attention(): pl.pallas_call(functools.partial(column_kernel, at_once), grid=(items //...]
    pallas_call x1, Pallas kernels: 7.4 us -> 4.25 us  [row_project(): pl.pallas_call(project_kernel, grid=(seqs // count,), out_shape=[shape((s...]
    pallas_call x0 -> x1, Pallas kernels: none -> 2.06 us  [stack(): pl.pallas_call(stack_kernel, out_shape=jax.ShapeDtypeStruct((len(weights)...]
    unnamed x14 -> x52, local copies, waits for them, and re-layouts: 3.95 us -> 4.77 us
  transfers between devices with their start and end apart: 12 -> 12, of which waited for: 5 -> 7; matrix products, arithmetic and copies ran while one was open for 0% -> 0% of each run, Pallas kernels for 31% -> 27%
where the time goes in v8:
time: 165 us; the launch traced here: 164 us
  Pallas kernels  69.3 us (42%)
  starting transfers between devices  32.7 us (20%)
  blocking collectives  31 us (19%)
  waiting for transfers between devices  24.4 us (15%)
  local copies, waits for them, and re-layouts  6.28 us (4%)
    pallas_call x4, Pallas kernels, row_attention(): pl.pallas_call(functools.partial(row_kernel, blocks), out_shape=[jax.Shap...  38.4 us
    all_to_all x1, blocking collectives, exchange(): return lax.all_to_all(value, 'dap', split_axis=0, concat_axis=0, tiled=True)  31 us
    pallas_call x2, Pallas kernels, column_attention(): pl.pallas_call(functools.partial(column_kernel, at_once), grid=(items //...  19.2 us
    ppermute x10, starting transfers between devices, fetch(): return lax.ppermute(value, 'dap', pairs)  18.1 us
    all_to_all x2, starting transfers between devices, exchange(): return lax.all_to_all(value, 'dap', split_axis=0, concat_axis=0, tiled=True)  14.6 us
    all_to_all x2, waiting for transfers between devices, exchange(): return lax.all_to_all(value, 'dap', split_axis=0, concat_axis=0, tiled=True)  13.1 us
    ppermute x10, waiting for transfers between devices, fetch(): return lax.ppermute(value, 'dap', pairs)  11.3 us
    pallas_call x1, Pallas kernels, pair_bias(): pl.pallas_call(pair_kernel, grid=(count // rows,), out_shape=jax.ShapeDty...  4.77 us
  transfers between devices with their start and end apart: 12, of which 7 were waited for; matrix products, arithmetic and copies ran while one was open for 0% of the time, Pallas kernels for 27%

profile of v8, /device:TPU:0, one launch (start us, length us, event | category | flops | bytes accessed | tf_op | source)
XLA Modules:
  0.0 164.2 jit_solution(2105608822864247154)
XLA Ops:
  0.0 4.8 %pair_bias.1 = bf16[8,16,512]{2,1,0:T(8,128)(2,1)} custom-call(bf16[16,512,128]{2,1,0:T(8,128)(2,1)} %x_ref.1, f32[1,128]{1,0:T(1,128)} %bitcast.37, bf16[8,128]{1,0:T(8,128)(2,1)} %bitcast.36), custom_call_target="tpu_custom_call" | custom-call | tf_op jit(solution)/shard_map/pair_bias/pallas_call | solution.py:108
  4.8 3.3 %collective-permute-start = (bf16[1,8,16,512]{3,2,1,0:T(8,128)(2,1)}, bf16[1,8,16,512]{3,2,1,0:T(8,128)(2,1)S(1)}, u32[]{:S(2)}, u32[]{:S(2)}) collective-permute-start(bf16[1,8,16,512]{3,2,1,0:T(8,128)(2,1)} %bitcast.18), channel_id=1, source_target_pairs={{1,0},{0,1},{3,2},{2,3},{5,4},{4,5},{7,6},{6,7},{9,8},{8,9},{11,10... | collective-permute-start | bytes 393224 | tf_op jit(solution)/shard_map/ppermute | solution.py:426
  8.1 3.7 %collective-permute-done.refs_1_ = bf16[1,8,16,512]{3,2,1,0:T(8,128)(2,1)S(1)} collective-permute-done((bf16[1,8,16,512]{3,2,1,0:T(8,128)(2,1)}, bf16[1,8,16,512]{3,2,1,0:T(8,128)(2,1)S(1)}, u32[]{:S(2)}, u32[]{:S(2)}) %collective-permute-start) | collective-permute-done | bytes 131104 | tf_op jit(solution)/shard_map/ppermute | solution.py:426
  11.8 0.9 copy-done.4
  12.7 0.3 join.3.refs_0_
  13.1 2.9 %collective-permute-start.1 = (bf16[2,8,16,512]{3,2,1,0:T(8,128)(2,1)S(1)}, bf16[2,8,16,512]{3,2,1,0:T(8,128)(2,1)S(1)}, u32[]{:S(2)}, u32[]{:S(2)}) collective-permute-start(bf16[2,8,16,512]{3,2,1,0:T(8,128)(2,1)S(1)} %join.3.refs_0_), channel_id=1, source_target_pairs={{2,0},{3,1},{4,2},{5,3},{6,4},{7,5},{0,6},{1,7},{10,8},{11,9},{12,... | collective-permute-start | bytes 786440 | tf_op jit(solution)/shard_map/ppermute | solution.py:426
  15.9 0.8 collective-permute-start.2
  16.7 0.9 collective-permute-start.3
  17.6 3.9 %collective-permute-start.4 = (bf16[2,8,16,512]{3,2,1,0:T(8,128)(2,1)S(1)}, bf16[2,8,16,512]{3,2,1,0:T(8,128)(2,1)S(1)}, u32[]{:S(2)}, u32[]{:S(2)}) collective-permute-start(bf16[2,8,16,512]{3,2,1,0:T(8,128)(2,1)S(1)} %join.3.refs_0_), channel_id=1, source_target_pairs={{16,0},{17,1},{18,2},{19,3},{20,4},{21,5},{22,6},{23,7},{24,8},{25... | collective-permute-start | bytes 786440 | tf_op jit(solution)/shard_map/ppermute | solution.py:426
  21.5 2.1 %stack.17.w_ref = bf16[5,256,256]{2,1,0:T(8,128)(2,1)} custom-call(bf16[256,256]{1,0:T(8,128)(2,1)} %refs_0_.1, bf16[256,256]{1,0:T(8,128)(2,1)} %refs_1_.1, bf16[256,256]{1,0:T(8,128)(2,1)} %refs_2_.1, bf16[256,256]{1,0:T(8,128)(2,1)} %refs_3_.1, bf16[256,256]{1,0:T(8,128)(2,1)} %refs_4_.5), custom_call_target="tpu_custom_call" | custom-call | tf_op jit(solution)/shard_map/stack/pallas_call | solution.py:175
  23.6 0.1 pad_add_fusion.here_ref
  23.6 2.6 %collective-permute-done.1.refs_1_ = bf16[2,8,16,512]{3,2,1,0:T(8,128)(2,1)S(1)} collective-permute-done((bf16[2,8,16,512]{3,2,1,0:T(8,128)(2,1)S(1)}, bf16[2,8,16,512]{3,2,1,0:T(8,128)(2,1)S(1)}, u32[]{:S(2)}, u32[]{:S(2)}) %collective-permute-start.1) | collective-permute-done | bytes 262176 | tf_op jit(solution)/shard_map/ppermute | solution.py:426
  26.3 0.4 collective-permute-done.2.refs_2_
  26.7 3.3 %collective-permute-done.3.refs_3_ = bf16[2,8,16,512]{3,2,1,0:T(8,128)(2,1)S(1)} collective-permute-done((bf16[2,8,16,512]{3,2,1,0:T(8,128)(2,1)S(1)}, bf16[2,8,16,512]{3,2,1,0:T(8,128)(2,1)S(1)}, u32[]{:S(2)}, u32[]{:S(2)}) %collective-permute-start.3) | collective-permute-done | bytes 262176 | tf_op jit(solution)/shard_map/ppermute | solution.py:426
  30.0 0.1 join.4.refs_8_
  30.1 0.0 collective-permute-done.4.refs_0_
  30.1 0.7 collective-permute-start.7
  30.8 0.8 collective-permute-start.8
  31.6 0.8 collective-permute-start.9
  32.4 4.0 %collective-permute-start.5 = (bf16[8,8,16,512]{3,2,1,0:T(8,128)(2,1)S(1)}, bf16[8,8,16,512]{3,2,1,0:T(8,128)(2,1)S(1)}, u32[]{:S(2)}, u32[]{:S(2)}) collective-permute-start(bf16[8,8,16,512]{3,2,1,0:T(8,128)(2,1)S(1)} %join.4.refs_8_), channel_id=1, source_target_pairs={{8,0},{9,1},{10,2},{11,3},{12,4},{13,5},{14,6},{15,7},{16,8},{17,9... | collective-permute-start | bytes 3145736 | tf_op jit(solution)/shard_map/ppermute | solution.py:426
  36.4 0.0 collective-permute-start.6
  36.5 0.0 copy-start.10
  36.5 1.6 copy-done.10
  38.1 4.2 %row_project.1 = (bf16[8,512,256]{2,1,0:T(8,128)(2,1)S(1)}, bf16[8,256,512]{2,1,0:T(8,128)(2,1)S(1)}, bf16[8,512,256]{2,1,0:T(8,128)(2,1)S(1)}, f32[8,512,256]{2,1,0:T(8,128)S(1)}) custom-call(bf16[8,512,256]{2,1,0:T(8,128)(2,1)S(1)} %copy-done.10, f32[1,256]{1,0:T(1,128)S(1)} %bitcast.28, f32[1,256]{1,0:T(1,128)S(1)} %bitcast.29, ...), custom_call_target="tpu_custom_call" | custom-call | flops 2147483648 | bytes 12582912 | tf_op jit(solution)/shard_map/row_project/pallas_call | solution.py:148
  42.3 0.0 copy-start.23
  42.4 9.1 %row_attention.4 = (bf16[32,64,256]{2,1,0:T(8,128)(2,1)}, bf16[32,64,256]{2,1,0:T(8,128)(2,1)S(1)}) custom-call(s32[3]{0:T(128)S(1)} %pad_add_fusion.here_ref, bf16[8,512,256]{2,1,0:T(8,128)(2,1)S(1)} %get-tuple-element.26.refs_0_.refs_1_, bf16[8,512,256]{2,1,0:T(8,128)(2,1)S(1)} %get-tuple-element.26.refs_0_.refs_1_, ...), custom_call_target="tpu_custom_call" | custom-call | flops 17179869184 | bytes 8388608 | tf_op jit(solution)/shard_map/row_attention/pallas_call | solution.py:296
  51.5 0.0 collective-permute-done.7.refs_1_
  51.5 0.0 collective-permute-done.8.refs_2_
  51.5 0.1 join.5.refs_8_
  51.6 8.7 %row_attention.5 = (bf16[32,64,256]{2,1,0:T(8,128)(2,1)}, bf16[32,64,256]{2,1,0:T(8,128)(2,1)S(1)}) custom-call(s32[3]{0:T(128)S(1)} %pad_add_fusion.here_ref, bf16[8,512,256]{2,1,0:T(8,128)(2,1)S(1)} %get-tuple-element.26.refs_0_.refs_1_, ...), custom_call_target="tpu_custom_call", output_to_operand_aliasing={{0}: (12, {}), {1}: (13, {})} | custom-call | flops 17179869184 | bytes 8388608 | tf_op jit(solution)/shard_map/row_attention/pallas_call | solution.py:296
  60.4 1.3 collective-permute-done.6.refs_9_
  61.7 9.3 %row_attention.6 = bf16[32,64,256]{2,1,0:T(8,128)(2,1)} custom-call(s32[3]{0:T(128)S(1)} %pad_add_fusion.here_ref, bf16[8,512,256]{2,1,0:T(8,128)(2,1)S(1)} %get-tuple-element.26.refs_0_.refs_1_, bf16[8,512,256]{2,1,0:T(8,128)(2,1)S(1)} %get-tuple-element.26.refs_0_.refs_1_, ...), custom_call_target="tpu_custom_call", output_to_operand_aliasing={{}: (13, {})} | custom-call | flops 17179869184 | bytes 8388608 | tf_op jit(solution)/shard_map/row_attention/pallas_call | solution.py:296
  71.0 1.0 copy-done.12
  72.0 9.7 %all-to-all-start = ((bf16[32,64,256]{2,1,0:T(8,128)(2,1)}), bf16[32,64,256]{2,1,0:T(8,128)(2,1)S(1)}, u32[]{:S(2)}, u32[]{:S(2)}) async-start(bf16[32,64,256]{2,1,0:T(8,128)(2,1)} %row_attention.6), calls=%async_computation | async-start | bytes 2097152 | tf_op jit(solution)/shard_map/all_to_all | solution.py:457
  81.7 11.3 %row_attention.7 = bf16[32,64,256]{2,1,0:T(8,128)(2,1)} custom-call(s32[3]{0:T(128)} %copy-done.9, bf16[8,512,256]{2,1,0:T(8,128)(2,1)} %copy-done.23, bf16[8,512,256]{2,1,0:T(8,128)(2,1)} %copy-done.23, f32[8,512,256]{2,1,0:T(8,128)} %copy-done.22, f32[8,512,256]{2,1,0:T(8,128)} %copy-done.22, ...), custom_call_target="tpu_custom_call", output_to_operand_aliasing={{}: (13, {})} | custom-call | flops 17179869184 | bytes 8388608 | tf_op jit(solution)/shard_map/row_attention/pallas_call | solution.py:296
  93.0 0.0 copy-start.5
  93.0 0.0 copy-start.6
  93.0 0.0 copy-start.7
  93.0 0.0 copy-start.8
  93.1 6.7 %all-to-all-done.x_ref = bf16[32,64,256]{2,1,0:T(8,128)(2,1)S(1)} async-done(((bf16[32,64,256]{2,1,0:T(8,128)(2,1)}), bf16[32,64,256]{2,1,0:T(8,128)(2,1)S(1)}, u32[]{:S(2)}, u32[]{:S(2)}) %all-to-all-start) | async-done | bytes 1048608 | tf_op jit(solution)/shard_map/all_to_all | solution.py:457
  99.8 4.9 %all-to-all-start.1 = ((bf16[32,64,256]{2,1,0:T(8,128)(2,1)}), bf16[32,64,256]{2,1,0:T(8,128)(2,1)}, u32[]{:S(2)}, u32[]{:S(2)}) async-start(bf16[32,64,256]{2,1,0:T(8,128)(2,1)} %row_attention.7), calls=%async_computation.1 | async-start | bytes 2097152 | tf_op jit(solution)/shard_map/all_to_all | solution.py:457
  104.8 0.0 copy-start.2
  104.8 1.2 copy-done.2
  106.0 9.0 %column_attention.2.refs_0_ = bf16[32,128,256]{2,1,0:T(8,128)(2,1)S(1)} custom-call(bf16[32,64,256]{2,1,0:T(8,128)(2,1)S(1)} %copy-done.2, f32[1,256]{1,0:T(1,128)S(1)} %bitcast.20, f32[1,256]{1,0:T(1,128)S(1)} %bitcast.22, bf16[5,256,256]{2,1,0:T(8,128)(2,1)S(1)} %copy-done, f32[1,256]{1,0:T(1,128)S(1)} %bitcast.24, f32[1,256]{1,0:T(1,128)S(1)} %bitcast.26), custom_call_target="tpu_custom_call" | custom-call | tf_op jit(solution)/shard_map/column_attention/pallas_call | solution.py:399
  115.0 6.4 %all-to-all-done.1.x_ref = bf16[32,64,256]{2,1,0:T(8,128)(2,1)} async-done(((bf16[32,64,256]{2,1,0:T(8,128)(2,1)}), bf16[32,64,256]{2,1,0:T(8,128)(2,1)}, u32[]{:S(2)}, u32[]{:S(2)}) %all-to-all-start.1) | async-done | bytes 1048608 | tf_op jit(solution)/shard_map/all_to_all | solution.py:457
  121.4 10.2 %column_attention.3 = bf16[32,128,256]{2,1,0:T(8,128)(2,1)S(1)} custom-call(bf16[32,64,256]{2,1,0:T(8,128)(2,1)} %all-to-all-done.1.x_ref, f32[1,256]{1,0:T(1,128)S(1)} %bitcast.21, f32[1,256]{1,0:T(1,128)S(1)} %bitcast.23, bf16[5,256,256]{2,1,0:T(8,128)(2,1)S(1)} %copy-done, f32[1,256]{1,0:T(1,128)S(1)} %bitcast.25, ...), custom_call_target="tpu_custom_call", output_to_operand_aliasing={{}: (6, {})} | custom-call | tf_op jit(solution)/shard_map/column_attention/pallas_call | solution.py:399
  131.7 31.0 %all_to_all.15 = bf16[32,128,256]{2,1,0:T(8,128)(2,1)S(1)} all-to-all(bf16[32,128,256]{2,1,0:T(8,128)(2,1)S(1)} %column_attention.3), channel_id=1, replica_groups=mesh['batch'=4,'dap'=32] {'dap'}, dimensions={0} | all-to-all | bytes 4194304 | tf_op jit(solution)/shard_map/all_to_all | solution.py:457
  162.7 1.5 copy.28
  (43 shorter events, 0.1 us)
Async XLA Ops:
  0.0 36.4 %copy-start.13 = (bf16[256,256]{1,0:T(8,128)(2,1)S(1)}, bf16[256,256]{1,0:T(8,128)(2,1)}, u32[]{:S(2)}) copy-start(bf16[256,256]{1,0:T(8,128)(2,1)} %q_w.1) | copy-start | bytes 393220
  0.0 36.4 %copy-start.14 = (bf16[256,256]{1,0:T(8,128)(2,1)S(1)}, bf16[256,256]{1,0:T(8,128)(2,1)}, u32[]{:S(2)}) copy-start(bf16[256,256]{1,0:T(8,128)(2,1)} %k_w.1) | copy-start | bytes 393220
  0.0 36.4 %copy-start.15 = (bf16[256,256]{1,0:T(8,128)(2,1)S(1)}, bf16[256,256]{1,0:T(8,128)(2,1)}, u32[]{:S(2)}) copy-start(bf16[256,256]{1,0:T(8,128)(2,1)} %v_w.1) | copy-start | bytes 393220
  0.0 36.4 %copy-start.16 = (bf16[256,256]{1,0:T(8,128)(2,1)S(1)}, bf16[256,256]{1,0:T(8,128)(2,1)}, u32[]{:S(2)}) copy-start(bf16[256,256]{1,0:T(8,128)(2,1)} %g_w.1) | copy-start | bytes 393220
  0.0 36.4 %copy-start.19 = (f32[256]{0:T(256)S(1)}, f32[256]{0:T(256)}, u32[]{:S(2)}) copy-start(f32[256]{0:T(256)} %param.25) | copy-start | bytes 3076
  0.0 36.4 %copy-start.20 = (f32[256]{0:T(256)S(1)}, f32[256]{0:T(256)}, u32[]{:S(2)}) copy-start(f32[256]{0:T(256)} %param.32) | copy-start | bytes 3076
  4.8 31.7 %copy-start.18 = (f32[256]{0:T(256)S(1)}, f32[256]{0:T(256)}, u32[]{:S(2)}) copy-start(f32[256]{0:T(256)} %param.24) | copy-start | bytes 3076
  4.8 7.0 %collective-permute-start = (bf16[1,8,16,512]{3,2,1,0:T(8,128)(2,1)}, bf16[1,8,16,512]{3,2,1,0:T(8,128)(2,1)S(1)}, u32[]{:S(2)}, u32[]{:S(2)}) collective-permute-start(bf16[1,8,16,512]{3,2,1,0:T(8,128)(2,1)} %bitcast.18), channel_id=1, source_target_pairs={{1,0},{0,1},{3,2},{2,3},{5,4},{4,5},{7,6},{6,7},{9,8},{8,9},{11,10... | collective-permute-start | bytes 393224 | tf_op jit(solution)/shard_map/ppermute | solution.py:426
  11.8 0.9 copy-start.4
  13.1 13.2 %collective-permute-start.1 = (bf16[2,8,16,512]{3,2,1,0:T(8,128)(2,1)S(1)}, bf16[2,8,16,512]{3,2,1,0:T(8,128)(2,1)S(1)}, u32[]{:S(2)}, u32[]{:S(2)}) collective-permute-start(bf16[2,8,16,512]{3,2,1,0:T(8,128)(2,1)S(1)} %join.3.refs_0_), channel_id=1, source_target_pairs={{2,0},{3,1},{4,2},{5,3},{6,4},{7,5},{0,6},{1,7},{10,8},{11,9},{12,... | collective-permute-start | bytes 786440 | tf_op jit(solution)/shard_map/ppermute | solution.py:426
  15.9 10.7 %collective-permute-start.2 = (bf16[2,8,16,512]{3,2,1,0:T(8,128)(2,1)S(1)}, bf16[2,8,16,512]{3,2,1,0:T(8,128)(2,1)S(1)}, u32[]{:S(2)}, u32[]{:S(2)}) collective-permute-start(bf16[2,8,16,512]{3,2,1,0:T(8,128)(2,1)S(1)} %join.3.refs_0_), channel_id=1, source_target_pairs={{4,0},{5,1},{6,2},{7,3},{0,4},{1,5},{2,6},{3,7},{12,8},{13,9},{14,... | collective-permute-start | bytes 786440 | tf_op jit(solution)/shard_map/ppermute | solution.py:426
  16.7 13.2 %collective-permute-start.3 = (bf16[2,8,16,512]{3,2,1,0:T(8,128)(2,1)S(1)}, bf16[2,8,16,512]{3,2,1,0:T(8,128)(2,1)S(1)}, u32[]{:S(2)}, u32[]{:S(2)}) collective-permute-start(bf16[2,8,16,512]{3,2,1,0:T(8,128)(2,1)S(1)} %join.3.refs_0_), channel_id=1, source_target_pairs={{6,0},{7,1},{0,2},{1,3},{2,4},{3,5},{4,6},{5,7},{14,8},{15,9},{8,1... | collective-permute-start | bytes 786440 | tf_op jit(solution)/shard_map/ppermute | solution.py:426
  17.6 12.5 %collective-permute-start.4 = (bf16[2,8,16,512]{3,2,1,0:T(8,128)(2,1)S(1)}, bf16[2,8,16,512]{3,2,1,0:T(8,128)(2,1)S(1)}, u32[]{:S(2)}, u32[]{:S(2)}) collective-permute-start(bf16[2,8,16,512]{3,2,1,0:T(8,128)(2,1)S(1)} %join.3.refs_0_), channel_id=1, source_target_pairs={{16,0},{17,1},{18,2},{19,3},{20,4},{21,5},{22,6},{23,7},{24,8},{25... | collective-permute-start | bytes 786440 | tf_op jit(solution)/shard_map/ppermute | solution.py:426
  23.6 38.0 %copy-start.9 = (s32[3]{0:T(128)}, s32[3]{0:T(128)S(1)}, u32[]{:S(2)}) copy-start(s32[3]{0:T(128)S(1)} %pad_add_fusion.here_ref) | copy-start | bytes 40
  30.1 21.4 %collective-permute-start.7 = (bf16[2,8,16,512]{3,2,1,0:T(8,128)(2,1)S(1)}, bf16[2,8,16,512]{3,2,1,0:T(8,128)(2,1)S(1)}, u32[]{:S(2)}, u32[]{:S(2)}) collective-permute-start(bf16[2,8,16,512]{3,2,1,0:T(8,128)(2,1)S(1)} %collective-permute-done.4.refs_0_), channel_id=1, source_target_pairs={{2,0},{3,1},{4,2},{5,3},{6,4},{7,5},{0,6},{1,7},{10,8},{11,9},{12,... | collective-permute-start | bytes 786440 | tf_op jit(solution)/shard_map/ppermute | solution.py:426
  30.8 20.7 %collective-permute-start.8 = (bf16[2,8,16,512]{3,2,1,0:T(8,128)(2,1)S(1)}, bf16[2,8,16,512]{3,2,1,0:T(8,128)(2,1)S(1)}, u32[]{:S(2)}, u32[]{:S(2)}) collective-permute-start(bf16[2,8,16,512]{3,2,1,0:T(8,128)(2,1)S(1)} %collective-permute-done.4.refs_0_), channel_id=1, source_target_pairs={{4,0},{5,1},{6,2},{7,3},{0,4},{1,5},{2,6},{3,7},{12,8},{13,9},{14,... | collective-permute-start | bytes 786440 | tf_op jit(solution)/shard_map/ppermute | solution.py:426
  31.6 19.9 %collective-permute-start.9 = (bf16[2,8,16,512]{3,2,1,0:T(8,128)(2,1)S(1)}, bf16[2,8,16,512]{3,2,1,0:T(8,128)(2,1)S(1)}, u32[]{:S(2)}, u32[]{:S(2)}) collective-permute-start(bf16[2,8,16,512]{3,2,1,0:T(8,128)(2,1)S(1)} %collective-permute-done.4.refs_0_), channel_id=1, source_target_pairs={{6,0},{7,1},{0,2},{1,3},{2,4},{3,5},{4,6},{5,7},{14,8},{15,9},{8,1... | collective-permute-start | bytes 786440 | tf_op jit(solution)/shard_map/ppermute | solution.py:426
  32.4 28.0 %collective-permute-start.5 = (bf16[8,8,16,512]{3,2,1,0:T(8,128)(2,1)S(1)}, bf16[8,8,16,512]{3,2,1,0:T(8,128)(2,1)S(1)}, u32[]{:S(2)}, u32[]{:S(2)}) collective-permute-start(bf16[8,8,16,512]{3,2,1,0:T(8,128)(2,1)S(1)} %join.4.refs_8_), channel_id=1, source_target_pairs={{8,0},{9,1},{10,2},{11,3},{12,4},{13,5},{14,6},{15,7},{16,8},{17,9... | collective-permute-start | bytes 3145736 | tf_op jit(solution)/shard_map/ppermute | solution.py:426
  36.4 25.3 %collective-permute-start.6 = (bf16[8,8,16,512]{3,2,1,0:T(8,128)(2,1)S(1)}, bf16[8,8,16,512]{3,2,1,0:T(8,128)(2,1)S(1)}, u32[]{:S(2)}, u32[]{:S(2)}) collective-permute-start(bf16[8,8,16,512]{3,2,1,0:T(8,128)(2,1)S(1)} %join.4.refs_8_), channel_id=1, source_target_pairs={{24,0},{25,1},{26,2},{27,3},{28,4},{29,5},{30,6},{31,7},{0,8},{1,9... | collective-permute-start | bytes 3145736 | tf_op jit(solution)/shard_map/ppermute | solution.py:426
  36.5 1.6 copy-start.10
  38.1 4.3 %copy-start.17 = (bf16[256,256]{1,0:T(8,128)(2,1)S(1)}, bf16[256,256]{1,0:T(8,128)(2,1)}, u32[]{:S(2)}) copy-start(bf16[256,256]{1,0:T(8,128)(2,1)} %refs_10_.3) | copy-start | bytes 393220
  38.1 4.3 %copy-start.21 = (f32[256]{0:T(256)S(1)}, f32[256]{0:T(256)}, u32[]{:S(2)}) copy-start(f32[256]{0:T(256)} %param.34) | copy-start | bytes 3076
  42.3 19.3 %copy-start.22 = (f32[8,512,256]{2,1,0:T(8,128)}, f32[8,512,256]{2,1,0:T(8,128)S(1)}, u32[]{:S(2)}) copy-start(f32[8,512,256]{2,1,0:T(8,128)S(1)} %get-tuple-element.27.refs_2_.refs_3_) | copy-start | bytes 12582916
  42.3 19.3 %copy-start.23 = (bf16[8,512,256]{2,1,0:T(8,128)(2,1)}, bf16[8,512,256]{2,1,0:T(8,128)(2,1)S(1)}, u32[]{:S(2)}) copy-start(bf16[8,512,256]{2,1,0:T(8,128)(2,1)S(1)} %get-tuple-element.26.refs_0_.refs_1_) | copy-start | bytes 6291460
  42.4 19.3 %copy-start.24 = (bf16[8,256,512]{2,1,0:T(8,128)(2,1)}, bf16[8,256,512]{2,1,0:T(8,128)(2,1)S(1)}, u32[]{:S(2)}) copy-start(bf16[8,256,512]{2,1,0:T(8,128)(2,1)S(1)} %get-tuple-element.28.refs_6_) | copy-start | bytes 6291460
  42.4 19.3 %copy-start.25 = (bf16[8,512,256]{2,1,0:T(8,128)(2,1)}, bf16[8,512,256]{2,1,0:T(8,128)(2,1)S(1)}, u32[]{:S(2)}) copy-start(bf16[8,512,256]{2,1,0:T(8,128)(2,1)S(1)} %get-tuple-element.29.refs_7_) | copy-start | bytes 6291460
  60.4 10.6 %copy-start.3 = (bf16[32,64,256]{2,1,0:T(8,128)(2,1)}, bf16[32,64,256]{2,1,0:T(8,128)(2,1)S(1)}, u32[]{:S(2)}) copy-start(bf16[32,64,256]{2,1,0:T(8,128)(2,1)S(1)} %get-tuple-element.35.refs_12_) | copy-start | bytes 3145732
  60.4 10.6 %copy-start.11 = (bf16[8,8,16,512]{3,2,1,0:T(8,128)(2,1)}, bf16[8,8,16,512]{3,2,1,0:T(8,128)(2,1)S(1)}, u32[]{:S(2)}) copy-start(bf16[8,8,16,512]{3,2,1,0:T(8,128)(2,1)S(1)} %collective-permute-done.5.refs_8_) | copy-start | bytes 3145732
  71.0 1.0 copy-start.12
  72.0 27.8 %all-to-all-start = ((bf16[32,64,256]{2,1,0:T(8,128)(2,1)}), bf16[32,64,256]{2,1,0:T(8,128)(2,1)S(1)}, u32[]{:S(2)}, u32[]{:S(2)}) async-start(bf16[32,64,256]{2,1,0:T(8,128)(2,1)} %row_attention.6), calls=%async_computation | async-start | bytes 2097152 | tf_op jit(solution)/shard_map/all_to_all | solution.py:457
  93.0 11.7 %copy-start = (bf16[5,256,256]{2,1,0:T(8,128)(2,1)S(1)}, bf16[5,256,256]{2,1,0:T(8,128)(2,1)}, u32[]{:S(2)}) copy-start(bf16[5,256,256]{2,1,0:T(8,128)(2,1)} %stack.17.w_ref) | copy-start | bytes 1966084
  93.0 11.7 %copy-start.5 = (f32[256]{0:T(256)S(1)}, f32[256]{0:T(256)}, u32[]{:S(2)}) copy-start(f32[256]{0:T(256)} %param.35) | copy-start | bytes 3076
  93.0 11.7 %copy-start.6 = (f32[256]{0:T(256)S(1)}, f32[256]{0:T(256)}, u32[]{:S(2)}) copy-start(f32[256]{0:T(256)} %param.36) | copy-start | bytes 3076
  93.0 11.7 %copy-start.7 = (f32[256]{0:T(256)S(1)}, f32[256]{0:T(256)}, u32[]{:S(2)}) copy-start(f32[256]{0:T(256)} %param.41) | copy-start | bytes 3076
  93.0 11.7 %copy-start.8 = (f32[256]{0:T(256)S(1)}, f32[256]{0:T(256)}, u32[]{:S(2)}) copy-start(f32[256]{0:T(256)} %param.43) | copy-start | bytes 3076
  99.8 4.9 %copy-start.1 = (bf16[32,64,256]{2,1,0:T(8,128)(2,1)}, bf16[32,64,256]{2,1,0:T(8,128)(2,1)S(1)}, u32[]{:S(2)}) copy-start(bf16[32,64,256]{2,1,0:T(8,128)(2,1)S(1)} %all-to-all-done.x_ref) | copy-start | bytes 3145732
  99.8 21.7 %all-to-all-start.1 = ((bf16[32,64,256]{2,1,0:T(8,128)(2,1)}), bf16[32,64,256]{2,1,0:T(8,128)(2,1)}, u32[]{:S(2)}, u32[]{:S(2)}) async-start(bf16[32,64,256]{2,1,0:T(8,128)(2,1)} %row_attention.7), calls=%async_computation.1 | async-start | bytes 2097152 | tf_op jit(solution)/shard_map/all_to_all | solution.py:457
  104.8 1.2 copy-start.2
